TPU v7x, 1024 devices: a whole 4x8x16 slice. The times are simulated.
1024 devices in a mesh: grp: 32 (over z, core), node: 32 (over y, x).
Axes of the slice: x: 4, y: 8, z: 16, core: 2. Of those that a mesh axis runs over, the one named last changes fastest.
Arguments:
- out_grad: bfloat16 [2048, 7168], P(('grp', 'node')), may hold values from -6 to 6
- expert_ids: int32 [2048, 8], P(('grp', 'node')), may hold values from 0 to 31, as said below
- slot_ids: int32 [2048, 8], P(('grp', 'node')), may hold values from -1 to 511, as said below
- gate_q: int32 [2048, 8], P(('grp', 'node')), may hold values from 1 to 255
- saved_x: bfloat16 [32, 512, 7168], P('grp'), may hold values from -6 to 6
- w_gate: bfloat16 [32, 7168, 2048], P('grp', None, 'node'), may hold values from -0.0625 to 0.0625
- w_up: bfloat16 [32, 7168, 2048], P('grp', None, 'node'), may hold values from -0.0625 to 0.0625
- w_down: bfloat16 [32, 2048, 7168], P('grp', 'node'), may hold values from -0.125 to 0.125
Outputs:
- in_grad: bfloat16 [2048, 7168], P(('grp', 'node'))
Inputs may be any that keep to these rules, and one draw needn't show every extreme that they name: `expert_ids`: each token names 8 different experts, all within at most 4 groups of 4 consecutive experts. `slot_ids`: -1 marks a dropped choice. Kept choices of one expert hold different slots, and a token held by a device at node index n has its slots in n * 16 to (n + 1) * 16 - 1. In every draw some expert has all 16 slots of every node index filled.
All inputs are finite; a program needn't handle non-finite values.
Results may differ from a plain program's by a relative error of at most 0.023.
Values may be sent and summed in bfloat16 or wider, within the bound.
No kernel may reach another device: no remote copies, remote signals or barrier semaphores. Data moves between devices by JAX's collectives and lax.ppermute only.
A program may use at most 128 MiB of HBM per device.

v0:
```python
import jax
import jax.numpy as jnp
from jax import lax
from jax.sharding import PartitionSpec as P


def local(out_grad, expert_ids, slot_ids, gate_q, saved_x, w_gate, w_up, w_down):
    row_count = lax.axis_size("grp")
    node_count = lax.axis_size("node")
    my_node = lax.axis_index("node")
    tok_count = out_grad.shape[0]
    model_width = out_grad.shape[1]
    slot_count = saved_x.shape[1]
    per_node = slot_count // node_count
    usable = slot_ids >= 0
    targets = jnp.arange(row_count, dtype=jnp.int32)
    matched = usable[None, :, :] & (expert_ids[None, :, :] == targets[:, None, None])
    chosen = jnp.any(matched, axis=2)
    outgoing = jnp.where(chosen[:, :, None], out_grad[None, :, :], jnp.zeros((), jnp.bfloat16))
    slot_sent = jnp.sum(jnp.where(matched, slot_ids[None, :, :] + 1, 0), axis=2) - 1
    gate_sent = jnp.sum(jnp.where(matched, gate_q[None, :, :], 0), axis=2)
    meta_data = jnp.stack([slot_sent, gate_sent], axis=2)
    arrived, meta_all = (
        lax.all_to_all(outgoing, "grp", split_axis=0, concat_axis=0, tiled=True),
        lax.all_to_all(meta_data, "grp", split_axis=0, concat_axis=0, tiled=True),
    )
    arrived = arrived.reshape(row_count * tok_count, model_width)
    slot_here = meta_all[:, :, 0].reshape(row_count * tok_count)
    gate_here = meta_all[:, :, 1].reshape(row_count * tok_count)
    local_slot = slot_here - my_node * per_node
    placing = local_slot[None, :] == jnp.arange(per_node, dtype=jnp.int32)[:, None]
    place_bf = placing.astype(jnp.bfloat16)
    rows_block = jnp.dot(place_bf, arrived, preferred_element_type=jnp.float32).astype(jnp.bfloat16)
    gate_block = jnp.dot(placing.astype(jnp.float32), gate_here.astype(jnp.float32)) / 256.0
    fanned, gate_all = (
        lax.all_gather(rows_block, "node", axis=0, tiled=True),
        lax.all_gather(gate_block.astype(jnp.bfloat16), "node", axis=0, tiled=True),
    )
    input_rows = saved_x[0]
    gate_proj = w_gate[0]
    up_proj = w_up[0]
    down_proj = w_down[0]
    pre_gate = jnp.dot(input_rows, gate_proj, preferred_element_type=jnp.float32)
    pre_up = jnp.dot(input_rows, up_proj, preferred_element_type=jnp.float32)
    contract_last = (((1,), (1,)), ((), ()))
    grad_hidden = lax.dot_general(
        fanned, down_proj, contract_last, preferred_element_type=jnp.float32
    )
    grad_hidden = grad_hidden * gate_all.astype(jnp.float32)[:, None]
    squash = jax.nn.sigmoid(pre_gate)
    grad_gate = (grad_hidden * pre_up * squash * (1.0 + pre_gate * (1.0 - squash))).astype(
        jnp.bfloat16
    )
    grad_up = (grad_hidden * pre_gate * squash).astype(jnp.bfloat16)
    term = lax.dot_general(grad_gate, gate_proj, contract_last, preferred_element_type=jnp.float32)
    own_block = lax.psum_scatter(
        (
            term
            + lax.dot_general(grad_up, up_proj, contract_last, preferred_element_type=jnp.float32)
        ).astype(jnp.bfloat16),
        "node",
        scatter_dimension=0,
        tiled=True,
    )
    back_rows = lax.dot_general(
        place_bf, own_block, (((0,), (0,)), ((), ())), preferred_element_type=jnp.float32
    )
    back_rows = back_rows.astype(jnp.bfloat16)
    returned = lax.all_to_all(
        back_rows.reshape(row_count, tok_count, model_width),
        "grp",
        split_axis=0,
        concat_axis=0,
        tiled=True,
    )
    return jnp.sum(returned.astype(jnp.float32), axis=0).astype(jnp.bfloat16)


def solution(mesh):
    in_specs = (
        P(("grp", "node"), None),
        P(("grp", "node"), None),
        P(("grp", "node"), None),
        P(("grp", "node"), None),
        P("grp", None, None),
        P("grp", None, "node"),
        P("grp", None, "node"),
        P("grp", "node", None),
    )
    out_specs = P(("grp", "node"), None)
    return jax.shard_map(local, mesh=mesh, in_specs=in_specs, out_specs=out_specs, check_vma=False)
```

profile of v0, /device:TPU:1, one launch (start us, length us, event | category | flops | bytes accessed | tf_op | source)
XLA Modules:
  0.0 540.6 jit_solution(7068374503675767134)
XLA Ops:
  6.5 0.0 copy-start
  6.5 0.8 broadcast_compare_fusion
  7.3 0.7 broadcast_add_fusion
  8.0 0.8 select_reduce_fusion.1
  8.8 0.7 copy.14
  9.5 20.4 %all-to-all-start = ((s32[32,2,2]{1,2,0:T(2,128)}), s32[32,2,2]{1,2,0:T(2,128)S(1)}, u32[]{:S(2)}, u32[]{:S(2)}) async-start(s32[32,2,2]{1,2,0:T(2,128)} %copy.14), calls=%async_computation | async-start | bytes 65536 | tf_op jit(solution)/shard_map/all_to_all | solution.py:25
  29.9 0.8 fusion.35
  30.7 0.1 copy.15
  30.8 2.4 broadcast_select_fusion
  33.2 8.9 %all-to-all-done = s32[32,2,2]{1,2,0:T(2,128)S(1)} async-done(((s32[32,2,2]{1,2,0:T(2,128)}), s32[32,2,2]{1,2,0:T(2,128)S(1)}, u32[]{:S(2)}, u32[]{:S(2)}) %all-to-all-start) | async-done | bytes 544 | tf_op jit(solution)/shard_map/all_to_all | solution.py:25
  42.0 4.7 all-to-all-start.1
  46.7 0.0 all-gather.2.cloned.1.call-start
  46.8 0.1 sub.26
  46.9 50.1 %all-to-all-done.1 = bf16[32,2,7168]{2,1,0:T(2,128)(2,1)S(1)} async-done(((bf16[32,2,7168]{2,1,0:T(2,128)(2,1)}), bf16[32,2,7168]{2,1,0:T(2,128)(2,1)S(1)}, u32[]{:S(2)}, u32[]{:S(2)}) %all-to-all-start.1) | async-done | bytes 917536 | tf_op jit(solution)/shard_map/all_to_all | solution.py:24
  97.0 0.3 reshape.31
  97.4 0.9 convolution_convert_fusion.1
  98.3 0.0 copy-start.2
  98.3 0.0 all-gather.2.cloned.1.call-update
  98.3 0.0 reduce-scatter.2.cloned.1.call-start
  98.4 1.3 dynamic-slice
  100.4 0.0 copy-start.1
  100.4 5.7 %fusion = f32[512,64]{0,1:T(8,128)S(1)} fusion(bf16[1,512,7168]{2,1,0:T(8,128)(2,1)} %param.12, bf16[1,7168,64]{1,2,0:T(8,128)(2,1)} %param.13), kind=kOutput, calls=%fused_computation.3 | convolution fusion | flops 469762048 | bytes 8388608 | tf_op jit(solution)/shard_map/dot_general | solution.py:43
  106.1 0.1 fusion.32
  106.1 0.1 reshape.38
  106.2 0.1 fusion.20
  106.4 0.2 dynamic-update-slice
  106.6 61.9 %all-reduce = bf16[512]{0:T(512)(128)(2,1)S(1)} all-reduce(bf16[512]{0:T(512)(128)(2,1)S(1)} %dynamic-update-slice), channel_id=1, replica_groups=mesh['grp'=32,'node'=32] {'node'}, use_global_device_ids=true, to_apply=%add | all-reduce | flops 512 | bytes 2048
  168.5 30.2 %all-gather.2.cloned.1.call-done = bf16[512,7168]{1,0:T(8,128)(2,1)} async-done(((bf16[16,7168]{1,0:T(8,128)(2,1)}), bf16[512,7168]{1,0:T(8,128)(2,1)}) %all-gather.2.cloned.1.call-update) | async-done | bytes 7340048 | tf_op jit(solution)/shard_map/all_gather | solution.py:36
  198.7 0.0 copy-done.2
  198.8 5.4 %convolution_multiply_fusion = f32[512,64]{0,1:T(8,128)S(1)} fusion(bf16[512,7168]{1,0:T(8,128)(2,1)} %all-gather.2.cloned.1.call-done, bf16[1,64,7168]{2,1,0:T(8,128)(2,1)S(1)} %copy-done.2, f32[512]{0:T(512)S(1)} %convert_element_type.35), kind=kOutput, calls=%fused_computation.8 | convolution fusion | flops 469794816 | bytes 8390656 | tf_op jit(solution)/shard_map/dot_general | solution.py:46
  204.2 0.0 copy-done
  204.2 0.0 copy-done.1
  204.2 12.7 %fusion.17 = f32[512,7168]{1,0:T(8,128)} fusion(f32[512,64]{0,1:T(8,128)S(1)} %convolution_multiply_fusion, bf16[1,512,7168]{2,1,0:T(8,128)(2,1)} %param.12, bf16[1,7168,64]{1,2,0:T(8,128)(2,1)S(1)} %copy-done.1, bf16[1,7168,64]{1,2,0:T(8,128)(2,1)S(1)} %copy-done, f32[512,64]{0,1:T(8,128)S(1)} %fusion), kind=kOutput, calls=%fused_computation.13 | convolution fusion | flops 939851776 | bytes 24117248 | tf_op jit(solution)/shard_map/dot_general | solution.py:55
  216.9 10.2 %add_convert_fusion = bf16[512,7168]{1,0:T(8,128)(2,1)} fusion(f32[512,7168]{1,0:T(8,128)} %fusion.17, bf16[1,7168,64]{1,2,0:T(8,128)(2,1)S(1)} %copy-done, f32[512,64]{0,1:T(8,128)S(1)} %convolution_multiply_fusion, f32[512,64]{0,1:T(8,128)S(1)} %fusion), kind=kOutput, calls=%fused_computation | convolution fusion | flops 477298688 | bytes 23199744 | tf_op jit(solution)/shard_map/dot_general | solution.py:59
  227.2 0.0 reduce-scatter.2.cloned.1.call-update
  227.2 235.3 %reduce-scatter.2.cloned.1.call-done = bf16[16,7168]{1,0:T(8,128)(2,1)} async-done(((bf16[512,7168]{1,0:T(8,128)(2,1)}), bf16[16,7168]{1,0:T(8,128)(2,1)}) %reduce-scatter.2.cloned.1.call-update) | async-done | bytes 229392 | tf_op jit(solution)/shard_map/reduce_scatter | solution.py:56
  462.5 1.4 convolution_convert_fusion
  463.9 0.3 reshape.32
  464.3 68.1 %all_to_all.15 = bf16[32,2,7168]{2,1,0:T(2,128)(2,1)S(1)} all-to-all(bf16[32,2,7168]{2,1,0:T(2,128)(2,1)S(1)} %reshape.32), channel_id=1, replica_groups=mesh['grp'=32,'node'=32] {'grp'}, dimensions={0} | all-to-all | bytes 1835008 | tf_op jit(solution)/shard_map/all_to_all | solution.py:69
  532.4 1.4 reduce_sum.32
  (5 shorter events, 0.1 us)
Async XLA Ops:
  6.5 197.6 %copy-start = (bf16[1,7168,64]{1,2,0:T(8,128)(2,1)S(1)}, bf16[1,7168,64]{1,2,0:T(8,128)(2,1)}, u32[]{:S(2)}) copy-start(bf16[1,7168,64]{1,2,0:T(8,128)(2,1)} %param.14) | copy-start | bytes 2752516
  9.5 32.5 %all-to-all-start = ((s32[32,2,2]{1,2,0:T(2,128)}), s32[32,2,2]{1,2,0:T(2,128)S(1)}, u32[]{:S(2)}, u32[]{:S(2)}) async-start(s32[32,2,2]{1,2,0:T(2,128)} %copy.14), calls=%async_computation | async-start | bytes 65536 | tf_op jit(solution)/shard_map/all_to_all | solution.py:25
  42.0 55.0 %all-to-all-start.1 = ((bf16[32,2,7168]{2,1,0:T(2,128)(2,1)}), bf16[32,2,7168]{2,1,0:T(2,128)(2,1)S(1)}, u32[]{:S(2)}, u32[]{:S(2)}) async-start(bf16[32,2,7168]{2,1,0:T(2,128)(2,1)} %broadcast_select_fusion), calls=%async_computation.1 | async-start | bytes 1835008 | tf_op jit(solution)/shard_map/all_to_all | solution.py:24
  46.7 152.0 %all-gather.2.cloned.1.call-start = ((), (), s32[]{:S(2)}) async-start(), calls=%async_computation.4 | async-start | bytes 7569408 | tf_op jit(solution)/shard_map/all_gather | solution.py:36
  98.3 100.5 %copy-start.2 = (bf16[1,64,7168]{2,1,0:T(8,128)(2,1)S(1)}, bf16[1,64,7168]{2,1,0:T(8,128)(2,1)}, u32[]{:S(2)}) copy-start(bf16[1,64,7168]{2,1,0:T(8,128)(2,1)} %param.15) | copy-start | bytes 2752516
  98.3 364.2 %reduce-scatter.2.cloned.1.call-start = ((), (), s32[]{:S(2)}) async-start(), calls=%async_computation.5 | async-start | bytes 7569408 | tf_op jit(solution)/shard_map/reduce_scatter | solution.py:56
  100.4 103.8 %copy-start.1 = (bf16[1,7168,64]{1,2,0:T(8,128)(2,1)S(1)}, bf16[1,7168,64]{1,2,0:T(8,128)(2,1)}, u32[]{:S(2)}) copy-start(bf16[1,7168,64]{1,2,0:T(8,128)(2,1)} %param.13) | copy-start | bytes 2752516
Sparse Core Ops, SparseCore 0:
  98.4 100.2 all-gather.1
  227.3 235.1 reduce-scatter.1
where the time goes:
time: 541 us
  waiting for transfers between devices  325 us (60%)
  blocking collectives  130 us (24%)
  matrix products  36.5 us (7%)
  starting transfers between devices  25.2 us (5%)
  between operations  14.2 us (3%)
  other arithmetic  6.91 us (1%)
    reduce_scatter x1, waiting for transfers between devices, local(): lax.psum_scatter((term + lax.dot_general(grad_up, up_proj, contract_last,...  235 us
    all_to_all x1, blocking collectives, local(): lax.all_to_all(back_rows.reshape(row_count, tok_count, model_width), 'grp...  68.1 us
    unnamed x1, blocking collectives  61.9 us
    all_to_all x1, waiting for transfers between devices, local(): lax.all_to_all(outgoing, 'grp', split_axis=0, concat_axis=0, tiled=True)  50.1 us
    all_gather x1, waiting for transfers between devices, local(): lax.all_gather(rows_block, 'node', axis=0, tiled=True)  30.2 us
    all_to_all x1, starting transfers between devices, local(): lax.all_to_all(meta_data, 'grp', split_axis=0, concat_axis=0, tiled=True)  20.4 us
    dot_general x1, matrix products, local(): lax.dot_general(grad_gate, gate_proj, contract_last, preferred_element_ty...  12.7 us
  transfers between devices with their start and end apart: 4, of which 4 were waited for; matrix products, arithmetic and copies ran while one was open for 2% of the time, Pallas kernels for 0%

commit v1 on v0

v1 whole, which is shorter than its diff:
```python
import jax
import jax.numpy as jnp
from jax import lax
from jax.sharding import PartitionSpec as P

X_DEV = 4
C_DEV = 2
META = 128


def groups(axis_size, inner):
    outer = axis_size // inner
    along_outer = [[o * inner + i for o in range(outer)] for i in range(inner)]
    along_inner = [[o * inner + i for i in range(inner)] for o in range(outer)]
    return along_outer, along_inner


def swap(a, axis, members):
    return lax.all_to_all(a, axis, 0, 0, axis_index_groups=members, tiled=True)


def local(out_grad, expert_ids, slot_ids, gate_q, saved_x, w_gate, w_up, w_down):
    f32, bf16 = jnp.float32, jnp.bfloat16
    n_grp, n_node = lax.axis_size("grp"), lax.axis_size("node")
    my_expert, my_node = lax.axis_index("grp"), lax.axis_index("node")
    n_y, n_z = n_node // X_DEV, n_grp // C_DEV
    along_y, along_x = groups(n_node, X_DEV)
    along_z, along_c = groups(n_grp, C_DEV)
    n_tok, width = out_grad.shape
    part = width // n_y
    n_slot = saved_x.shape[1]
    per_node = n_slot // n_node
    n_hid = w_down.shape[1]
    n_pick = expert_ids.shape[1]

    down = w_down[0].reshape(n_hid, n_y, part).transpose(1, 0, 2)
    both_cut = jnp.concatenate(
        [
            w[0].T.reshape(n_hid, n_y, part).transpose(1, 0, 2)
            for w in (w_gate, w_up)
        ],
        axis=1,
    )
    down_y = swap(down, "node", along_y).reshape(n_y * n_hid, part)
    both_y = swap(both_cut, "node", along_y).reshape(n_y * 2 * n_hid, part)

    slot_here = jnp.where(slot_ids >= 0, slot_ids - my_node * per_node, -1)
    meta = jnp.concatenate([expert_ids, slot_here, gate_q], axis=1).astype(bf16)
    meta = jnp.pad(meta, ((0, 0), (0, META - 3 * n_pick)))
    cut = out_grad.reshape(n_tok, n_y, part).transpose(1, 0, 2)
    payload = jnp.concatenate(
        [cut, jnp.broadcast_to(meta[None], (n_y, n_tok, META))], axis=2
    )
    payload = swap(payload, "node", along_y).reshape(n_y * n_tok, part + META)
    tokens = lax.all_gather(payload, "grp", axis=0, tiled=True)
    n_all = n_grp * n_y * n_tok
    rout = tokens[:, part:].astype(f32)
    hit = rout[:, :n_pick] == my_expert.astype(f32)
    slot_of = rout[:, n_pick : 2 * n_pick]
    hit = hit & (slot_of >= 0)
    place = jnp.sum(jnp.where(hit, slot_of + 1, 0), axis=1).astype(jnp.int32) - 1
    gate = jnp.sum(jnp.where(hit, rout[:, 2 * n_pick : 3 * n_pick], 0), axis=1) / 256.0
    from_y = (jnp.arange(n_all, dtype=jnp.int32) // n_tok) % n_y
    place = jnp.where(place >= 0, place + from_y * per_node, -1)
    n_own = n_y * per_node
    one_hot = place[:, None] == jnp.arange(n_own, dtype=jnp.int32)[None, :]
    back_hot = jnp.where(one_hot, gate[:, None], 0.0).astype(bf16)
    back_hot = back_hot.reshape(n_z, C_DEV, n_y * n_tok, n_own).transpose(1, 0, 2, 3)
    back_hot = back_hot.reshape(n_all, n_own)
    rows = lax.dot_general(
        one_hot.astype(bf16),
        tokens[:, :part],
        (((0,), (0,)), ((), ())),
        preferred_element_type=f32,
    ).astype(bf16)

    all_rows = lax.all_gather(rows, "node", axis=0, axis_index_groups=along_x, tiled=True)
    last = (((1,), (1,)), ((), ()))
    hidden = lax.dot_general(down_y, all_rows, last, preferred_element_type=f32)
    hidden = swap(hidden.astype(bf16), "node", along_y)
    hidden = jnp.sum(hidden.reshape(n_y, n_hid, n_slot).astype(f32), axis=0)

    def forward(w):
        pre = jnp.dot(saved_x[0], w[0], preferred_element_type=f32)
        pre = pre.reshape(n_y, X_DEV, per_node, n_hid).transpose(1, 0, 2, 3)
        return pre.reshape(n_slot, n_hid).T

    pre_gate, pre_up = forward(w_gate), forward(w_up)
    squash = jax.nn.sigmoid(pre_gate)
    grad_gate = hidden * pre_up * squash * (1.0 + pre_gate * (1.0 - squash))
    grad_up = hidden * pre_gate * squash
    grads = jnp.concatenate([grad_gate, grad_up], axis=0).astype(bf16)
    all_grads = lax.all_gather(grads, "node", axis=0, axis_index_groups=along_y, tiled=True)

    slot_dx = lax.dot_general(
        all_grads, both_y, (((0,), (0,)), ((), ())), preferred_element_type=f32
    ).astype(bf16)
    slot_dx = swap(slot_dx, "node", along_x).reshape(X_DEV, n_own, part)
    slot_dx = jnp.sum(slot_dx.astype(f32), axis=0).astype(bf16)

    back = jnp.dot(back_hot, slot_dx, preferred_element_type=f32).astype(bf16)
    back = swap(back, "grp", along_c).reshape(C_DEV, n_all // C_DEV, part)
    back = jnp.sum(back.astype(f32), axis=0).astype(bf16)
    back = swap(back, "grp", along_z).reshape(n_z, n_y * n_tok, part)
    back = jnp.sum(back.astype(f32), axis=0).astype(bf16)
    back = swap(back.reshape(n_y, n_tok, part), "node", along_y)
    return back.transpose(1, 0, 2).reshape(n_tok, width)


def solution(mesh):
    in_specs = (
        P(("grp", "node"), None),
        P(("grp", "node"), None),
        P(("grp", "node"), None),
        P(("grp", "node"), None),
        P("grp", None, None),
        P("grp", None, "node"),
        P("grp", None, "node"),
        P("grp", "node", None),
    )
    out_specs = P(("grp", "node"), None)
    return jax.shard_map(local, mesh=mesh, in_specs=in_specs, out_specs=out_specs, check_vma=False)
```

time: 541 us -> 286 us (0.53)
  the two profiles are of different devices: /device:TPU:1 before, /device:TPU:2 now
where the time goes in v1:
time: 286 us
  waiting for transfers between devices  140 us (49%)
  blocking collectives  83.5 us (29%)
  starting transfers between devices  19 us (7%)
  matrix products  17.5 us (6%)
  between operations  13.6 us (5%)
  local copies, waits for them, and re-layouts  6.16 us (2%)
  other arithmetic  5.73 us (2%)
    all_gather x1, waiting for transfers between devices, local(): tokens = lax.all_gather(payload, 'grp', axis=0, tiled=True)  71.2 us
    all_to_all x4, blocking collectives, swap(): return lax.all_to_all(a, axis, 0, 0, axis_index_groups=members, tiled=True)  68.5 us
    all_to_all x4, waiting for transfers between devices, swap(): return lax.all_to_all(a, axis, 0, 0, axis_index_groups=members, tiled=True)  56 us
    all_to_all x4, starting transfers between devices, swap(): return lax.all_to_all(a, axis, 0, 0, axis_index_groups=members, tiled=True)  18.9 us
    all_gather x1, blocking collectives, local(): lax.all_gather(rows, 'node', axis=0, axis_index_groups=along_x, tiled=True)  15 us
    all_gather x1, waiting for transfers between devices, local(): lax.all_gather(grads, 'node', axis=0, axis_index_groups=along_y, tiled=True)  12.8 us
    dot_general x2, matrix products, forward(): pre = jnp.dot(saved_x[0], w[0], preferred_element_type=f32)  10.4 us
  transfers between devices with their start and end apart: 6, of which 5 were waited for; matrix products, arithmetic and copies ran while one was open for 7% of the time, Pallas kernels for 0%

profile of v1, /device:TPU:2, one launch (start us, length us, event | category | flops | bytes accessed | tf_op | source)
XLA Modules:
  0.0 285.5 jit_solution(3240154537072466250)
XLA Ops:
  6.5 0.7 convert.18
  7.2 0.7 convert.20
  7.9 0.7 fusion.29
  8.6 0.1 fusion.34
  8.7 0.8 pad_maximum_fusion.2
  9.5 14.9 %all_to_all.56 = bf16[8,2,1024]{2,1,0:T(2,128)(2,1)S(1)} all-to-all(bf16[8,2,1024]{2,1,0:T(2,128)(2,1)S(1)} %pad_maximum_fusion.2), channel_id=1, replica_groups={{0,4,8,12,16,20,24,28},{1,5,9,13,17,21,25,29},{2,6,10,14,18,22,26,30},{..., dimensions={0} | all-to-all | bytes 65536 | tf_op jit(solution)/shard_map/all_to_all | solution.py:19
  24.4 0.6 reshape.117
  25.0 1.3 copy.39
  26.4 1.1 copy.31
  27.5 3.6 %all-to-all-start.1 = ((bf16[8,64,896]{2,1,0:T(8,128)(2,1)}), bf16[8,64,896]{2,1,0:T(8,128)(2,1)S(1)}, u32[]{:S(2)}, u32[]{:S(2)}) async-start(bf16[8,64,896]{2,1,0:T(8,128)(2,1)} %copy.31), calls=%async_computation.1 | async-start | bytes 1835008 | tf_op jit(solution)/shard_map/all_to_all | solution.py:19
  31.0 71.2 %all-gather.3.cloned.1.call-done = bf16[512,1024]{1,0:T(8,128)(2,1)} async-done(((bf16[16,1024]{1,0:T(8,128)(2,1)}), bf16[512,1024]{1,0:T(8,128)(2,1)}) %all-gather.3.cloned.1.call-update) | async-done | bytes 1048592 | tf_op jit(solution)/shard_map/all_gather | solution.py:55
  102.2 0.9 slice_convert_fusion
  103.1 0.4 fusion.3
  103.5 1.7 convolution_convert_fusion.3
  105.2 15.0 %all_gather.10 = bf16[512,896]{1,0:T(8,128)(2,1)S(1)} all-gather(bf16[128,896]{1,0:T(8,128)(2,1)S(1)} %convolution_convert_fusion.3), channel_id=1, replica_groups={{0,1,2,3},{4,5,6,7},{8,9,10,11},{12,13,14,15},{16,17,18,19},{20,21,22,2..., dimensions={0}, use_global_device_ids=true | all-gather | bytes 1146880 | tf_op jit(solution)/shard_map/all_gather | solution.py:77
  120.2 1.6 convolution_convert_fusion.2
  121.7 6.9 %all-to-all-start.2 = ((bf16[8,64,512]{2,1,0:T(8,128)(2,1)}), bf16[8,64,512]{2,1,0:T(8,128)(2,1)S(1)}, u32[]{:S(2)}, u32[]{:S(2)}) async-start(bf16[8,64,512]{2,1,0:T(8,128)(2,1)} %bitcast.104), calls=%async_computation.2 | async-start | bytes 1048576 | tf_op jit(solution)/shard_map/all_to_all | solution.py:19
  128.6 0.1 copy.41
  128.8 0.1 copy.40
  128.9 0.2 pad_maximum_fusion
  129.1 1.6 copy.36
  130.7 13.1 %all-to-all-done.2 = bf16[8,64,512]{2,1,0:T(8,128)(2,1)S(1)} async-done(((bf16[8,64,512]{2,1,0:T(8,128)(2,1)}), bf16[8,64,512]{2,1,0:T(8,128)(2,1)S(1)}, u32[]{:S(2)}, u32[]{:S(2)}) %all-to-all-start.2) | async-done | bytes 524320 | tf_op jit(solution)/shard_map/all_to_all | solution.py:19
  143.8 3.6 %all-to-all-start.3 = ((bf16[8,128,896]{2,1,0:T(8,128)(2,1)}), bf16[8,128,896]{2,1,0:T(8,128)(2,1)S(1)}, u32[]{:S(2)}, u32[]{:S(2)}) async-start(bf16[8,128,896]{2,1,0:T(8,128)(2,1)} %copy.36), calls=%async_computation.3 | async-start | bytes 3670016 | tf_op jit(solution)/shard_map/all_to_all | solution.py:19
  147.4 5.1 %convolution_bitcast_fusion = f32[4,8,16,64]{3,2,0,1:T(8,128)S(1)} fusion(bf16[8,4,16,7168]{3,2,1,0:T(8,128)(2,1)} %bitcast.108, bf16[1,7168,64]{1,2,0:T(8,128)(2,1)S(1)} %copy-done), kind=kOutput, calls=%fused_computation.5 | convolution fusion | flops 469762048 | bytes 8388608 | tf_op jit(solution)/shard_map/dot_general | solution.py:84
  152.6 0.1 copy.35
  152.7 5.3 %convolution_bitcast_fusion.1 = f32[4,8,16,64]{3,2,0,1:T(8,128)S(1)} fusion(bf16[8,4,16,7168]{3,2,1,0:T(8,128)(2,1)} %bitcast.109, bf16[1,7168,64]{1,2,0:T(8,128)(2,1)} %param.14), kind=kOutput, calls=%fused_computation.6 | convolution fusion | flops 469762048 | bytes 8388608 | tf_op jit(solution)/shard_map/dot_general | solution.py:84
  158.1 0.1 copy.33
  158.2 0.1 convert_reduce_fusion
  158.3 0.1 fusion.10
  158.3 0.7 pad_maximum_fusion.1
  159.0 33.4 %all-to-all-done.3 = bf16[8,128,896]{2,1,0:T(8,128)(2,1)S(1)} async-done(((bf16[8,128,896]{2,1,0:T(8,128)(2,1)}), bf16[8,128,896]{2,1,0:T(8,128)(2,1)S(1)}, u32[]{:S(2)}, u32[]{:S(2)}) %all-to-all-start.3) | async-done | bytes 1835040 | tf_op jit(solution)/shard_map/all_to_all | solution.py:19
  192.4 12.8 %all-gather.5.cloned.1.call-done = bf16[1024,512]{1,0:T(8,128)(2,1)} async-done(((bf16[128,512]{1,0:T(8,128)(2,1)}), bf16[1024,512]{1,0:T(8,128)(2,1)}) %all-gather.5.cloned.1.call-update) | async-done | bytes 1048592 | tf_op jit(solution)/shard_map/all_gather | solution.py:93
  205.2 3.4 %convolution_convert_fusion.1 = bf16[512,896]{1,0:T(8,128)(2,1)} fusion(bf16[1024,512]{1,0:T(8,128)(2,1)} %all-gather.5.cloned.1.call-done, bf16[1024,896]{1,0:T(8,128)(2,1)S(1)} %bitcast.96), kind=kOutput, calls=%fused_computation.2 | convolution fusion | flops 939982848 | bytes 3801088 | tf_op jit(solution)/shard_map/dot_general | solution.py:95
  208.7 4.9 %all-to-all-start.4 = ((bf16[4,128,896]{2,1,0:T(8,128)(2,1)}), bf16[4,128,896]{2,1,0:T(8,128)(2,1)S(1)}, u32[]{:S(2)}, u32[]{:S(2)}) async-start(bf16[4,128,896]{2,1,0:T(8,128)(2,1)} %bitcast.26), calls=%async_computation.4 | async-start | bytes 1835008 | tf_op jit(solution)/shard_map/all_to_all | solution.py:19
  213.6 0.1 div.22
  213.6 0.1 broadcast_in_dim.37
  213.7 0.1 sub.26
  213.8 0.1 fusion.18
  213.9 0.1 eq.37
  214.0 9.5 %all-to-all-done.4 = bf16[4,128,896]{2,1,0:T(8,128)(2,1)S(1)} async-done(((bf16[4,128,896]{2,1,0:T(8,128)(2,1)}), bf16[4,128,896]{2,1,0:T(8,128)(2,1)S(1)}, u32[]{:S(2)}, u32[]{:S(2)}) %all-to-all-start.4) | async-done | bytes 917536 | tf_op jit(solution)/shard_map/all_to_all | solution.py:19
  223.5 0.1 reduce_sum.66
  223.7 0.5 convolution_convert_fusion
  224.1 4.5 %all_to_all.57 = bf16[2,256,896]{2,1,0:T(8,128)(2,1)S(1)} all-to-all(bf16[2,256,896]{2,1,0:T(8,128)(2,1)S(1)} %bitcast.95), channel_id=1, replica_groups={{0,32},{64,96},{128,160},{192,224},{256,288},{320,352},{384,416},{448,4..., dimensions={0} | all-to-all | bytes 1835008 | tf_op jit(solution)/shard_map/all_to_all | solution.py:19
  228.6 0.2 reduce_sum.67
  228.8 37.6 %all_to_all.58 = bf16[16,16,896]{2,1,0:T(8,128)(2,1)S(1)} all-to-all(bf16[16,16,896]{2,1,0:T(8,128)(2,1)S(1)} %bitcast.97), channel_id=1, replica_groups={{0,64,128,192,256,320,384,448,512,576,640,704,768,832,896,960},{32,96,1..., dimensions={0} | all-to-all | bytes 917504 | tf_op jit(solution)/shard_map/all_to_all | solution.py:19
  266.4 0.1 reduce_sum.68
  266.5 11.6 %all_to_all.59 = bf16[8,2,896]{2,1,0:T(2,128)(2,1)S(1)} all-to-all(bf16[8,2,896]{2,1,0:T(2,128)(2,1)S(1)} %reshape.124), channel_id=1, replica_groups={{0,4,8,12,16,20,24,28},{1,5,9,13,17,21,25,29},{2,6,10,14,18,22,26,30},{..., dimensions={0} | all-to-all | bytes 57344 | tf_op jit(solution)/shard_map/all_to_all | solution.py:19
  278.1 0.6 copy.43
  (17 shorter events, 0.2 us)
Async XLA Ops:
  6.5 95.7 %all-gather.3.cloned.1.call-start = ((), (), s32[]{:S(2)}) async-start(), calls=%async_computation.8 | async-start | bytes 1081344 | tf_op jit(solution)/shard_map/all_gather | solution.py:55
  27.5 92.7 %all-to-all-start.1 = ((bf16[8,64,896]{2,1,0:T(8,128)(2,1)}), bf16[8,64,896]{2,1,0:T(8,128)(2,1)S(1)}, u32[]{:S(2)}, u32[]{:S(2)}) async-start(bf16[8,64,896]{2,1,0:T(8,128)(2,1)} %copy.31), calls=%async_computation.1 | async-start | bytes 1835008 | tf_op jit(solution)/shard_map/all_to_all | solution.py:19
  120.2 8.4 %copy-start.1 = (bf16[1,7168,64]{1,2,0:T(8,128)(2,1)S(1)}, bf16[1,7168,64]{1,2,0:T(8,128)(2,1)}, u32[]{:S(2)}) copy-start(bf16[1,7168,64]{1,2,0:T(8,128)(2,1)} %param.14) | copy-start | bytes 2752516
  121.7 7.0 %copy-start = (bf16[1,7168,64]{1,2,0:T(8,128)(2,1)S(1)}, bf16[1,7168,64]{1,2,0:T(8,128)(2,1)}, u32[]{:S(2)}) copy-start(bf16[1,7168,64]{1,2,0:T(8,128)(2,1)} %param.13) | copy-start | bytes 2752516
  121.7 22.1 %all-to-all-start.2 = ((bf16[8,64,512]{2,1,0:T(8,128)(2,1)}), bf16[8,64,512]{2,1,0:T(8,128)(2,1)S(1)}, u32[]{:S(2)}, u32[]{:S(2)}) async-start(bf16[8,64,512]{2,1,0:T(8,128)(2,1)} %bitcast.104), calls=%async_computation.2 | async-start | bytes 1048576 | tf_op jit(solution)/shard_map/all_to_all | solution.py:19
  143.8 48.6 %all-to-all-start.3 = ((bf16[8,128,896]{2,1,0:T(8,128)(2,1)}), bf16[8,128,896]{2,1,0:T(8,128)(2,1)S(1)}, u32[]{:S(2)}, u32[]{:S(2)}) async-start(bf16[8,128,896]{2,1,0:T(8,128)(2,1)} %copy.36), calls=%async_computation.3 | async-start | bytes 3670016 | tf_op jit(solution)/shard_map/all_to_all | solution.py:19
  147.4 57.8 %all-gather.5.cloned.1.call-start = ((), (), s32[]{:S(2)}) async-start(), calls=%async_computation.9 | async-start | bytes 1179648 | tf_op jit(solution)/shard_map/all_gather | solution.py:93
  208.7 14.9 %all-to-all-start.4 = ((bf16[4,128,896]{2,1,0:T(8,128)(2,1)}), bf16[4,128,896]{2,1,0:T(8,128)(2,1)S(1)}, u32[]{:S(2)}, u32[]{:S(2)}) async-start(bf16[4,128,896]{2,1,0:T(8,128)(2,1)} %bitcast.26), calls=%async_computation.4 | async-start | bytes 1835008 | tf_op jit(solution)/shard_map/all_to_all | solution.py:19
Sparse Core Ops, SparseCore 0:
  25.1 76.9 all-gather.2
  159.2 46.0 all-gather.4

commit v2 on v1

v2 whole, which is shorter than its diff:
```python
import functools

import jax
import jax.numpy as jnp
from jax import lax
from jax.experimental import pallas as pl
from jax.experimental.pallas import tpu as pltpu
from jax.sharding import PartitionSpec as P

SPLIT = 8
C_DEV = 2
Z_NEAR = 4
META = 128
VMEM = 48 * 1024 * 1024
f32, bf16 = jnp.float32, jnp.bfloat16


def call(body, out_shape, cost, **kw):
    flops, moved = cost
    return pl.pallas_call(
        body,
        out_shape=out_shape,
        compiler_params=pltpu.CompilerParams(vmem_limit_bytes=VMEM),
        cost_estimate=pl.CostEstimate(
            flops=flops, bytes_accessed=moved, transcendentals=0
        ),
        **kw,
    )


def swap(a, axis, members):
    return lax.all_to_all(a, axis, 0, 0, axis_index_groups=members, tiled=True)


def rounds(blocks, axis, moves):
    return [blocks[0]] + [
        lax.ppermute(block, axis, move) for block, move in zip(blocks[1:], moves)
    ]


def total(blocks):
    return functools.reduce(lambda p, q: p + q, [b.astype(f32) for b in blocks]).astype(bf16)


def cut_body(gate_ref, up_ref, down_ref, out_ref):
    n = gate_ref.shape[0]
    out_ref[0, :n] = gate_ref[...]
    out_ref[0, n : 2 * n] = up_ref[...]
    out_ref[0, 2 * n :] = down_ref[...]


def cut_weights(gate, up, down):
    n_hid, width = gate.shape
    part = width // SPLIT
    spec = pl.BlockSpec((n_hid, part), lambda i: (0, i))
    return call(
        cut_body,
        jax.ShapeDtypeStruct((SPLIT, 3 * n_hid, part), bf16),
        (0, 12 * n_hid * width),
        grid=(SPLIT,),
        in_specs=[spec] * 3,
        out_specs=pl.BlockSpec((1, 3 * n_hid, part), lambda i: (i, 0, 0)),
    )(gate, up, down)


def forward_body(x_ref, gate_ref, up_ref, out_ref, acc):
    step = pl.program_id(0)
    n = gate_ref.shape[0]
    both = jnp.concatenate([gate_ref[...], up_ref[...]], axis=0)
    term = lax.dot_general(
        both, x_ref[...], (((1,), (1,)), ((), ())), preferred_element_type=f32
    )

    @pl.when(step == 0)
    def _():
        acc[...] = term

    @pl.when(step > 0)
    def _():
        acc[...] += term

    @pl.when(step == pl.num_programs(0) - 1)
    def _():
        pre_gate, pre_up = acc[:n], acc[n:]
        squash = jax.nn.sigmoid(pre_gate)
        out_ref[:n] = pre_up * squash * (1.0 + pre_gate * (1.0 - squash))
        out_ref[n:] = pre_gate * squash


def forward(x, gate, up):
    n_slot, width = x.shape
    n_hid = gate.shape[0]
    part = width // 8
    spec = pl.BlockSpec((n_hid, part), lambda i: (0, i))
    return call(
        forward_body,
        jax.ShapeDtypeStruct((2 * n_hid, n_slot), f32),
        (4 * n_hid * n_slot * width, 2 * (n_slot + 2 * n_hid) * width),
        grid=(8,),
        in_specs=[pl.BlockSpec((n_slot, part), lambda i: (0, i)), spec, spec],
        out_specs=pl.BlockSpec((2 * n_hid, n_slot), lambda i: (0, 0)),
        scratch_shapes=[pltpu.VMEM((2 * n_hid, n_slot), f32)],
    )(x, gate, up)


def select_body(n_tok, per_node, n_pick, expert_ref, here_ref, there_ref, rows_ref, hot_ref):
    part = rows_ref.shape[1]
    tok = jnp.concatenate([here_ref[...], there_ref[...]], axis=0)
    rout = tok[:, part:].astype(f32)
    lane = lax.broadcasted_iota(jnp.int32, rout.shape, 1)
    row = lax.broadcasted_iota(jnp.int32, rout.shape, 0)
    slot = pltpu.roll(rout, META - n_pick, 1)
    gate = pltpu.roll(rout, META - 2 * n_pick, 1)
    hit = (lane < n_pick) & (rout == expert_ref[0].astype(f32)) & (slot >= 0)
    found = jnp.sum(jnp.where(hit, slot + 1.0, 0.0), axis=1, keepdims=True)
    scale = jnp.sum(jnp.where(hit, gate, 0.0), axis=1, keepdims=True) * (1.0 / 256.0)
    found = found.astype(jnp.int32) - 1
    node = (row // n_tok) % SPLIT
    one_hot = (found >= 0) & (node * per_node + found == lane)
    hot_ref[...] = jnp.where(one_hot, scale, 0.0).astype(bf16)
    pick = jnp.where(one_hot, 1.0, 0.0).T.astype(bf16)
    rows_ref[...] = jnp.dot(pick, tok[:, :part], preferred_element_type=f32).astype(bf16)


def select(expert, here, there, n_tok, per_node, n_pick):
    n_all, wide = 2 * here.shape[0], here.shape[1]
    part = wide - META
    n_own = SPLIT * per_node
    return call(
        functools.partial(select_body, n_tok, per_node, n_pick),
        (
            jax.ShapeDtypeStruct((n_own, part), bf16),
            jax.ShapeDtypeStruct((n_all, n_own), bf16),
        ),
        (2 * n_all * n_own * part, 2 * n_all * wide),
        in_specs=[
            pl.BlockSpec(memory_space=pltpu.SMEM),
            pl.BlockSpec(memory_space=pltpu.VMEM),
            pl.BlockSpec(memory_space=pltpu.VMEM),
        ],
        out_specs=[pl.BlockSpec(memory_space=pltpu.VMEM)] * 2,
    )(expert, here, there)


def hidden_body(w_ref, rows_ref, out_ref):
    n, h, part = w_ref.shape
    got = lax.dot_general(
        w_ref[...].reshape(n * h, part),
        rows_ref[...],
        (((1,), (1,)), ((), ())),
        preferred_element_type=f32,
    )
    out_ref[...] = got.astype(bf16)


def hidden_part(weights, rows):
    n, h3, part = weights.shape
    h = h3 // 3
    n_slot = rows.shape[0]
    half = n_slot // 2
    return call(
        hidden_body,
        jax.ShapeDtypeStruct((n * h, n_slot), bf16),
        (2 * n * h * n_slot * part, 2 * (n * h + n_slot) * part),
        grid=(2,),
        in_specs=[
            pl.BlockSpec((n, h, part), lambda i: (0, 2, 0)),
            pl.BlockSpec((half, part), lambda i: (i, 0)),
        ],
        out_specs=pl.BlockSpec((n * h, half), lambda i: (0, i)),
    )(weights, rows)


def grads_body(parts_ref, coef_ref, out_ref):
    n, h, _ = parts_ref.shape
    total = jnp.sum(parts_ref[...].astype(f32), axis=0)
    grads = jnp.concatenate([total * coef_ref[:h], total * coef_ref[h:]], axis=0)
    grads = grads.T.astype(bf16)
    for i in range(n):
        out_ref[i] = grads


def grads_of(parts, coef):
    n, h, n_slot = parts.shape
    return call(
        grads_body,
        jax.ShapeDtypeStruct((n, n_slot, 2 * h), bf16),
        (2 * n * h * n_slot, 6 * n * h * n_slot),
    )(parts, coef)


def slot_body(grads_ref, w_ref, out_ref):
    n, h, part = w_ref.shape
    grads = jnp.concatenate([grads_ref[i] for i in range(n)], axis=1)
    got = jnp.dot(grads, w_ref[...].reshape(n * h, part), preferred_element_type=f32)
    out_ref[...] = got.astype(bf16)


def slot_part(grads, weights):
    n, n_slot, h2 = grads.shape
    part = weights.shape[2]
    half = n_slot // 2
    return call(
        slot_body,
        jax.ShapeDtypeStruct((n_slot, part), bf16),
        (2 * n * h2 * n_slot * part, 2 * (n * h2 * (n_slot + part) + n_slot * part)),
        grid=(2,),
        in_specs=[
            pl.BlockSpec((n, half, h2), lambda i: (0, i, 0)),
            pl.BlockSpec((n, h2, part), lambda i: (0, 0, 0)),
        ],
        out_specs=pl.BlockSpec((half, part), lambda i: (i, 0)),
    )(grads, weights)


def back_body(hot_ref, parts_ref, here_ref, there_ref):
    own = jnp.sum(parts_ref[...].astype(f32), axis=0).astype(bf16)
    got = jnp.dot(hot_ref[...], own, preferred_element_type=f32).astype(bf16)
    half = here_ref.shape[0]
    here_ref[...] = got[:half]
    there_ref[...] = got[half:]


def back_rows(hot, parts):
    n_all, n_own = hot.shape
    part = parts.shape[2]
    return call(
        back_body,
        (jax.ShapeDtypeStruct((n_all // 2, part), bf16),) * 2,
        (2 * n_all * n_own * part, 2 * (n_all * part + parts.size)),
    )(hot, parts)


def local(out_grad, expert_ids, slot_ids, gate_q, saved_x, w_gate, w_up, w_down):
    n_grp, n_node = lax.axis_size("grp"), lax.axis_size("node")
    my_expert, my_node = lax.axis_index("grp"), lax.axis_index("node")
    n_rest, n_z = n_node // SPLIT, n_grp // C_DEV
    z_far = n_z // Z_NEAR
    block = [[h * SPLIT + d for d in range(SPLIT)] for h in range(n_rest)]
    rest = [[h * SPLIT + d for h in range(n_rest)] for d in range(SPLIT)]
    at = lambda far, near, c: (far * Z_NEAR + near) * C_DEV + c
    devices = [(f, n, c) for f in range(z_far) for n in range(Z_NEAR) for c in range(C_DEV)]
    far = [[(at(f, n, c), at((f + k) % z_far, n, c)) for f, n, c in devices] for k in range(1, z_far)]
    near = [[(at(f, n, c), at(f, (n + j) % Z_NEAR, c)) for f, n, c in devices] for j in range(1, Z_NEAR)]
    other = [(at(f, n, c), at(f, n, C_DEV - 1 - c)) for f, n, c in devices]
    undo = lambda moves: [[(to, frm) for frm, to in move] for move in moves]
    n_tok, width = out_grad.shape
    part = width // SPLIT
    n_slot = saved_x.shape[1]
    per_node = n_slot // n_node
    n_hid = w_down.shape[1]
    n_pick = expert_ids.shape[1]
    n_own = SPLIT * per_node
    gate, up, down = w_gate[0].T, w_up[0].T, w_down[0]

    slot_here = jnp.where(slot_ids >= 0, slot_ids - my_node * per_node, -1)
    meta = jnp.concatenate([expert_ids, slot_here, gate_q], axis=1).astype(bf16)
    meta = jnp.pad(meta, ((0, 0), (0, META - 3 * n_pick)))
    cols = out_grad.reshape(n_tok, SPLIT, part).transpose(1, 0, 2)
    payload = jnp.concatenate(
        [cols, jnp.broadcast_to(meta[None], (SPLIT, n_tok, META))], axis=2
    )
    payload = swap(payload, "node", block).reshape(SPLIT * n_tok, part + META)

    weights = cut_weights(gate, up, down)
    payload, weights = lax.optimization_barrier((payload, weights))
    weights = swap(weights, "node", block)

    tokens = jnp.concatenate(rounds([payload] * z_far, "grp", far), axis=0)
    tokens = jnp.concatenate(rounds([tokens] * Z_NEAR, "grp", near), axis=0)
    there = lax.ppermute(tokens, "grp", other)
    expert = my_expert.astype(jnp.int32).reshape(1)
    rows, hot = select(expert, tokens, there, n_tok, per_node, n_pick)
    rows = lax.all_gather(rows, "node", axis=0, axis_index_groups=rest, tiled=True)

    hidden = hidden_part(weights, rows)
    hidden = swap(hidden, "node", block).reshape(SPLIT, n_hid, n_slot)
    coef = forward(saved_x[0], gate, up)
    grads = swap(grads_of(hidden, coef), "node", block)
    parts = swap(slot_part(grads, weights), "node", rest)

    here, there = back_rows(hot, parts.reshape(n_rest, n_own, part))
    back = total([here, lax.ppermute(there, "grp", other)])
    back = total(rounds(jnp.split(back, Z_NEAR), "grp", undo(near)))
    back = total(rounds(jnp.split(back, z_far), "grp", undo(far)))
    back = swap(back.reshape(SPLIT, n_tok, part), "node", block)
    return back.transpose(1, 0, 2).reshape(n_tok, width)


def solution(mesh):
    in_specs = (
        P(("grp", "node"), None),
        P(("grp", "node"), None),
        P(("grp", "node"), None),
        P(("grp", "node"), None),
        P("grp", None, None),
        P("grp", None, "node"),
        P("grp", None, "node"),
        P("grp", "node", None),
    )
    out_specs = P(("grp", "node"), None)
    return jax.shard_map(local, mesh=mesh, in_specs=in_specs, out_specs=out_specs, check_vma=False)
```

time: 286 us -> 222 us (0.78)
  waiting for transfers between devices: 140 us -> 32.4 us
  starting transfers between devices: 19 us -> 86.2 us
  matrix products: 17.5 us -> 0 us
  between operations: 13.6 us -> 0.34 us
  Pallas kernels: 0 us -> 13.1 us
  blocking collectives: 83.5 us -> 74.6 us
  local copies, waits for them, and re-layouts: 6.16 us -> 10.7 us
    all_gather x2 -> x0, waiting for transfers between devices: 84 us -> none  [the longest x1 71.2 us: local(): tokens = lax.all_gather(payload, 'grp', axis=0, tiled=True)]
    ppermute x0 -> x14, starting transfers between devices: none -> 58.3 us  [the longest x12 54.5 us: rounds(): lax.ppermute(block, axis, move)]
    all_to_all x4 -> x3, waiting for transfers between devices: 56 us -> 5.72 us  [swap(): return lax.all_to_all(a, axis, 0, 0, axis_index_groups=members, tiled=True)]
    ppermute x0 -> x14, waiting for transfers between devices: none -> 26.7 us  [the longest x12 22.9 us: rounds(): lax.ppermute(block, axis, move)]
    dot_general x6 -> x0, matrix products: 17.5 us -> none  [the longest x2 10.4 us: forward(): pre = jnp.dot(saved_x[0], w[0], preferred_element_type=f32)]
    all_to_all x4 -> x3, blocking collectives: 68.5 us -> 53.6 us  [swap(): return lax.all_to_all(a, axis, 0, 0, axis_index_groups=members, tiled=True)]
    pallas_call x0 -> x7, Pallas kernels: none -> 13.1 us  [the longest x1 7.31 us: forward(): call(forward_body, jax.ShapeDtypeStruct((2 * n_hid, n_slot), f32), (4 * n...]
    all_to_all x4 -> x3, starting transfers between devices: 18.9 us -> 27.8 us  [swap(): return lax.all_to_all(a, axis, 0, 0, axis_index_groups=members, tiled=True)]
  transfers between devices with their start and end apart: 6 -> 17, of which waited for: 5 -> 9; matrix products, arithmetic and copies ran while one was open for 7% -> 0% of each run, Pallas kernels for 0% -> 4%
where the time goes in v2:
time: 222 us; the launch traced here: 221 us
  starting transfers between devices  86.2 us (39%)
  blocking collectives  74.6 us (34%)
  waiting for transfers between devices  32.4 us (15%)
  Pallas kernels  13.1 us (6%)
  local copies, waits for them, and re-layouts  10.7 us (5%)
  other arithmetic  3.7 us (2%)
    ppermute x12, starting transfers between devices, rounds(): lax.ppermute(block, axis, move)  54.5 us
    all_to_all x3, blocking collectives, swap(): return lax.all_to_all(a, axis, 0, 0, axis_index_groups=members, tiled=True)  53.6 us
    all_to_all x3, starting transfers between devices, swap(): return lax.all_to_all(a, axis, 0, 0, axis_index_groups=members, tiled=True)  27.8 us
    ppermute x12, waiting for transfers between devices, rounds(): lax.ppermute(block, axis, move)  22.9 us
    all_gather x1, blocking collectives, local(): lax.all_gather(rows, 'node', axis=0, axis_index_groups=rest, tiled=True)  21.1 us
    unnamed x26, local copies, waits for them, and re-layouts  10.6 us
    pallas_call x1, Pallas kernels, forward(): call(forward_body, jax.ShapeDtypeStruct((2 * n_hid, n_slot), f32), (4 * n...  7.31 us
    all_to_all x3, waiting for transfers between devices, swap(): return lax.all_to_all(a, axis, 0, 0, axis_index_groups=members, tiled=True)  5.72 us
  transfers between devices with their start and end apart: 17, of which 9 were waited for; matrix products, arithmetic and copies ran while one was open for 0% of the time, Pallas kernels for 4%

profile of v2, /device:TPU:2, one launch (start us, length us, event | category | flops | bytes accessed | tf_op | source)
XLA Modules:
  0.0 221.1 jit_solution(11425875008726023794)
XLA Ops:
  0.0 0.7 convert.9
  0.7 0.7 convert.11
  1.4 0.7 fusion
  2.1 1.4 pad_maximum_fusion
  3.5 16.4 %all-to-all-start = ((bf16[8,2,1024]{2,1,0:T(2,128)(2,1)}), bf16[8,2,1024]{2,1,0:T(2,128)(2,1)S(1)}, u32[]{:S(2)}, u32[]{:S(2)}) async-start(bf16[8,2,1024]{2,1,0:T(2,128)(2,1)} %pad_maximum_fusion), calls=%async_computation | async-start | bytes 65536 | tf_op jit(solution)/shard_map/all_to_all | solution.py:32
  19.9 1.2 copy-done.1
  21.1 1.2 copy-done.3
  22.3 1.2 copy-done.7
  23.5 0.7 shard_map.82
  24.1 1.5 copy-done
  25.6 5.7 %all-to-all-done = bf16[8,2,1024]{2,1,0:T(2,128)(2,1)S(1)} async-done(((bf16[8,2,1024]{2,1,0:T(2,128)(2,1)}), bf16[8,2,1024]{2,1,0:T(2,128)(2,1)S(1)}, u32[]{:S(2)}, u32[]{:S(2)}) %all-to-all-start) | async-done | bytes 32800 | tf_op jit(solution)/shard_map/all_to_all | solution.py:32
  31.4 3.9 %all-to-all-start.1 = ((bf16[8,192,896]{2,1,0:T(8,128)(2,1)}), bf16[8,192,896]{2,1,0:T(8,128)(2,1)S(1)}, u32[]{:S(2)}, u32[]{:S(2)}) async-start(bf16[8,192,896]{2,1,0:T(8,128)(2,1)} %copy-done), calls=%async_computation.1 | async-start | bytes 5505024 | tf_op jit(solution)/shard_map/all_to_all | solution.py:32
  35.3 3.8 %collective-permute-start.2 = (bf16[16,1024]{1,0:T(8,128)(2,1)S(1)}, bf16[16,1024]{1,0:T(8,128)(2,1)S(1)}, u32[]{:S(2)}, u32[]{:S(2)}) collective-permute-start(bf16[16,1024]{1,0:T(8,128)(2,1)S(1)} %reshape.26), channel_id=1, source_target_pairs={{0,768},{32,800},{64,832},{96,864},{128,896},{160,928},{192,960},{... | collective-permute-start | bytes 98312 | tf_op jit(solution)/shard_map/ppermute | solution.py:37
  39.0 3.1 %collective-permute-start.1 = (bf16[16,1024]{1,0:T(8,128)(2,1)S(1)}, bf16[16,1024]{1,0:T(8,128)(2,1)S(1)}, u32[]{:S(2)}, u32[]{:S(2)}) collective-permute-start(bf16[16,1024]{1,0:T(8,128)(2,1)S(1)} %reshape.26), channel_id=1, source_target_pairs={{0,512},{32,544},{64,576},{96,608},{128,640},{160,672},{192,704},{... | collective-permute-start | bytes 98312 | tf_op jit(solution)/shard_map/ppermute | solution.py:37
  42.1 7.8 %collective-permute-start = (bf16[16,1024]{1,0:T(8,128)(2,1)S(1)}, bf16[16,1024]{1,0:T(8,128)(2,1)S(1)}, u32[]{:S(2)}, u32[]{:S(2)}) collective-permute-start(bf16[16,1024]{1,0:T(8,128)(2,1)S(1)} %reshape.26), channel_id=1, source_target_pairs={{0,256},{32,288},{64,320},{96,352},{128,384},{160,416},{192,448},{... | collective-permute-start | bytes 98312 | tf_op jit(solution)/shard_map/ppermute | solution.py:37
  50.0 5.3 %collective-permute-done = bf16[16,1024]{1,0:T(8,128)(2,1)S(1)} collective-permute-done((bf16[16,1024]{1,0:T(8,128)(2,1)S(1)}, bf16[16,1024]{1,0:T(8,128)(2,1)S(1)}, u32[]{:S(2)}, u32[]{:S(2)}) %collective-permute-start) | collective-permute-done | bytes 32800 | tf_op jit(solution)/shard_map/ppermute | solution.py:37
  55.4 1.9 collective-permute-start.3
  57.3 4.0 %collective-permute-start.4 = (bf16[64,1024]{1,0:T(8,128)(2,1)S(1)}, bf16[64,1024]{1,0:T(8,128)(2,1)S(1)}, u32[]{:S(2)}, u32[]{:S(2)}) collective-permute-start(bf16[64,1024]{1,0:T(8,128)(2,1)S(1)} %get-tuple-element.23), channel_id=1, source_target_pairs={{0,128},{32,160},{64,192},{96,224},{128,0},{160,32},{192,64},{224,... | collective-permute-start | bytes 393224 | tf_op jit(solution)/shard_map/ppermute | solution.py:37
  61.3 4.5 %collective-permute-start.5 = (bf16[64,1024]{1,0:T(8,128)(2,1)S(1)}, bf16[64,1024]{1,0:T(8,128)(2,1)S(1)}, u32[]{:S(2)}, u32[]{:S(2)}) collective-permute-start(bf16[64,1024]{1,0:T(8,128)(2,1)S(1)} %get-tuple-element.23), channel_id=1, source_target_pairs={{0,192},{32,224},{64,0},{96,32},{128,64},{160,96},{192,128},{224,1... | collective-permute-start | bytes 393224 | tf_op jit(solution)/shard_map/ppermute | solution.py:37
  65.8 2.4 %collective-permute-done.4 = bf16[64,1024]{1,0:T(8,128)(2,1)S(1)} collective-permute-done((bf16[64,1024]{1,0:T(8,128)(2,1)S(1)}, bf16[64,1024]{1,0:T(8,128)(2,1)S(1)}, u32[]{:S(2)}, u32[]{:S(2)}) %collective-permute-start.4) | collective-permute-done | bytes 131104 | tf_op jit(solution)/shard_map/ppermute | solution.py:37
  68.2 1.1 collective-permute-done.5
  69.3 1.9 collective-permute-start.6
  71.2 2.0 collective-permute-done.6.there_ref
  73.2 1.7 shard_map.83
  75.0 0.6 copy-done.8
  75.6 21.1 %all_gather.3.rows_ref = bf16[512,896]{1,0:T(8,128)(2,1)} all-gather(bf16[128,896]{1,0:T(8,128)(2,1)S(1)} %get-tuple-element.14), channel_id=1, replica_groups={{0,8,16,24},{1,9,17,25},{2,10,18,26},{3,11,19,27},{4,12,20,28},{5,13,21..., dimensions={0}, use_global_device_ids=true | all-gather | bytes 1146880 | tf_op jit(solution)/shard_map/all_gather | solution.py:274
  96.7 1.2 copy-done.5
  97.9 1.1 shard_map.84
  99.0 0.8 copy-done.6
  99.8 7.6 %all-to-all-start.2 = ((bf16[8,64,512]{2,1,0:T(8,128)(2,1)}), bf16[8,64,512]{2,1,0:T(8,128)(2,1)S(1)}, u32[]{:S(2)}, u32[]{:S(2)}) async-start(bf16[8,64,512]{2,1,0:T(8,128)(2,1)} %bitcast.22), calls=%async_computation.2 | async-start | bytes 1048576 | tf_op jit(solution)/shard_map/all_to_all | solution.py:32
  107.3 1.2 copy-done.2
  108.5 1.2 copy-done.4
  109.7 7.3 %shard_map.85.coef_ref = f32[128,512]{1,0:T(8,128)S(1)} custom-call(bf16[512,7168]{1,0:T(8,128)(2,1)} %bitcast.24, bf16[64,7168]{1,0:T(8,128)(2,1)S(1)} %bitcast.18, bf16[64,7168]{1,0:T(8,128)(2,1)S(1)} %bitcast.20), custom_call_target="tpu_custom_call" | custom-call | flops 939524096 | bytes 9175040 | tf_op jit(solution)/shard_map/pallas_call | solution.py:95
  117.3 17.9 %all_to_all.38.grads_ref = bf16[8,512,128]{2,1,0:T(8,128)(2,1)S(1)} all-to-all(bf16[8,512,128]{2,1,0:T(8,128)(2,1)S(1)} %shard_map.86), channel_id=1, replica_groups={{0,1,2,3,4,5,6,7},{8,9,10,11,12,13,14,15},{16,17,18,19,20,21,22,23},{24..., dimensions={0} | all-to-all | bytes 2097152 | tf_op jit(solution)/shard_map/all_to_all | solution.py:32
  135.2 1.7 shard_map.87
  136.9 24.2 %all_to_all.39.parts_ref = bf16[4,128,896]{2,1,0:T(8,128)(2,1)S(1)} all-to-all(bf16[4,128,896]{2,1,0:T(8,128)(2,1)S(1)} %bitcast.21), channel_id=1, replica_groups={{0,8,16,24},{1,9,17,25},{2,10,18,26},{3,11,19,27},{4,12,20,28},{5,13,21..., dimensions={0} | all-to-all | bytes 1835008 | tf_op jit(solution)/shard_map/all_to_all | solution.py:32
  161.5 1.9 collective-permute-start.7
  163.5 1.8 collective-permute-done.7
  165.4 5.8 %collective-permute-start.8 = (bf16[64,896]{1,0:T(8,128)(2,1)S(1)}, bf16[64,896]{1,0:T(8,128)(2,1)S(1)}, u32[]{:S(2)}, u32[]{:S(2)}) collective-permute-start(bf16[64,896]{1,0:T(8,128)(2,1)S(1)} %get-tuple-element.17), channel_id=1, source_target_pairs={{64,0},{96,32},{128,64},{160,96},{192,128},{224,160},{0,192},{32,2... | collective-permute-start | bytes 344072 | tf_op jit(solution)/shard_map/ppermute | solution.py:37
  171.2 1.9 collective-permute-start.10
  173.1 2.5 %collective-permute-start.9 = (bf16[64,896]{1,0:T(8,128)(2,1)S(1)}, bf16[64,896]{1,0:T(8,128)(2,1)S(1)}, u32[]{:S(2)}, u32[]{:S(2)}) collective-permute-start(bf16[64,896]{1,0:T(8,128)(2,1)S(1)} %get-tuple-element.19), channel_id=1, source_target_pairs={{128,0},{160,32},{192,64},{224,96},{0,128},{32,160},{64,192},{96,2... | collective-permute-start | bytes 344072 | tf_op jit(solution)/shard_map/ppermute | solution.py:37
  175.6 4.8 %collective-permute-done.10 = bf16[64,896]{1,0:T(8,128)(2,1)S(1)} collective-permute-done((bf16[64,896]{1,0:T(8,128)(2,1)S(1)}, bf16[64,896]{1,0:T(8,128)(2,1)S(1)}, u32[]{:S(2)}, u32[]{:S(2)}) %collective-permute-start.10) | collective-permute-done | bytes 114720 | tf_op jit(solution)/shard_map/ppermute | solution.py:37
  180.4 4.3 %collective-permute-done.9 = bf16[64,896]{1,0:T(8,128)(2,1)S(1)} collective-permute-done((bf16[64,896]{1,0:T(8,128)(2,1)S(1)}, bf16[64,896]{1,0:T(8,128)(2,1)S(1)}, u32[]{:S(2)}, u32[]{:S(2)}) %collective-permute-start.9) | collective-permute-done | bytes 114720 | tf_op jit(solution)/shard_map/ppermute | solution.py:37
  184.8 6.0 %collective-permute-start.11 = (bf16[16,896]{1,0:T(8,128)(2,1)S(1)}, bf16[16,896]{1,0:T(8,128)(2,1)S(1)}, u32[]{:S(2)}, u32[]{:S(2)}) collective-permute-start(bf16[16,896]{1,0:T(8,128)(2,1)S(1)} %get-tuple-element.20), channel_id=1, source_target_pairs={{256,0},{288,32},{320,64},{352,96},{384,128},{416,160},{448,192},{... | collective-permute-start | bytes 86024 | tf_op jit(solution)/shard_map/ppermute | solution.py:37
  190.8 3.8 %collective-permute-start.13 = (bf16[16,896]{1,0:T(8,128)(2,1)S(1)}, bf16[16,896]{1,0:T(8,128)(2,1)S(1)}, u32[]{:S(2)}, u32[]{:S(2)}) collective-permute-start(bf16[16,896]{1,0:T(8,128)(2,1)S(1)} %get-tuple-element.21), channel_id=1, source_target_pairs={{768,0},{800,32},{832,64},{864,96},{896,128},{928,160},{960,192},{... | collective-permute-start | bytes 86024 | tf_op jit(solution)/shard_map/ppermute | solution.py:37
  194.6 9.5 %collective-permute-start.12 = (bf16[16,896]{1,0:T(8,128)(2,1)S(1)}, bf16[16,896]{1,0:T(8,128)(2,1)S(1)}, u32[]{:S(2)}, u32[]{:S(2)}) collective-permute-start(bf16[16,896]{1,0:T(8,128)(2,1)S(1)} %get-tuple-element.22), channel_id=1, source_target_pairs={{512,0},{544,32},{576,64},{608,96},{640,128},{672,160},{704,192},{... | collective-permute-start | bytes 86024 | tf_op jit(solution)/shard_map/ppermute | solution.py:37
  204.1 5.0 %collective-permute-done.12 = bf16[16,896]{1,0:T(8,128)(2,1)S(1)} collective-permute-done((bf16[16,896]{1,0:T(8,128)(2,1)S(1)}, bf16[16,896]{1,0:T(8,128)(2,1)S(1)}, u32[]{:S(2)}, u32[]{:S(2)}) %collective-permute-start.12) | collective-permute-done | bytes 28704 | tf_op jit(solution)/shard_map/ppermute | solution.py:37
  209.1 11.4 %all_to_all.40 = bf16[8,2,896]{2,1,0:T(2,128)(2,1)S(1)} all-to-all(bf16[8,2,896]{2,1,0:T(2,128)(2,1)S(1)} %reshape.27), channel_id=1, replica_groups={{0,1,2,3,4,5,6,7},{8,9,10,11,12,13,14,15},{16,17,18,19,20,21,22,23},{24..., dimensions={0} | all-to-all | bytes 57344 | tf_op jit(solution)/shard_map/all_to_all | solution.py:32
  (38 shorter events, 1.7 us)
Async XLA Ops:
  3.5 27.8 %all-to-all-start = ((bf16[8,2,1024]{2,1,0:T(2,128)(2,1)}), bf16[8,2,1024]{2,1,0:T(2,128)(2,1)S(1)}, u32[]{:S(2)}, u32[]{:S(2)}) async-start(bf16[8,2,1024]{2,1,0:T(2,128)(2,1)} %pad_maximum_fusion), calls=%async_computation | async-start | bytes 65536 | tf_op jit(solution)/shard_map/all_to_all | solution.py:32
  19.9 1.2 copy-start.1
  21.1 1.2 copy-start.3
  22.3 1.2 copy-start.7
  24.1 1.5 copy-start
  31.4 65.3 %all-to-all-start.1 = ((bf16[8,192,896]{2,1,0:T(8,128)(2,1)}), bf16[8,192,896]{2,1,0:T(8,128)(2,1)S(1)}, u32[]{:S(2)}, u32[]{:S(2)}) async-start(bf16[8,192,896]{2,1,0:T(8,128)(2,1)} %copy-done), calls=%async_computation.1 | async-start | bytes 5505024 | tf_op jit(solution)/shard_map/all_to_all | solution.py:32
  35.3 20.1 %collective-permute-start.2 = (bf16[16,1024]{1,0:T(8,128)(2,1)S(1)}, bf16[16,1024]{1,0:T(8,128)(2,1)S(1)}, u32[]{:S(2)}, u32[]{:S(2)}) collective-permute-start(bf16[16,1024]{1,0:T(8,128)(2,1)S(1)} %reshape.26), channel_id=1, source_target_pairs={{0,768},{32,800},{64,832},{96,864},{128,896},{160,928},{192,960},{... | collective-permute-start | bytes 98312 | tf_op jit(solution)/shard_map/ppermute | solution.py:37
  39.0 16.3 %collective-permute-start.1 = (bf16[16,1024]{1,0:T(8,128)(2,1)S(1)}, bf16[16,1024]{1,0:T(8,128)(2,1)S(1)}, u32[]{:S(2)}, u32[]{:S(2)}) collective-permute-start(bf16[16,1024]{1,0:T(8,128)(2,1)S(1)} %reshape.26), channel_id=1, source_target_pairs={{0,512},{32,544},{64,576},{96,608},{128,640},{160,672},{192,704},{... | collective-permute-start | bytes 98312 | tf_op jit(solution)/shard_map/ppermute | solution.py:37
  42.1 13.2 %collective-permute-start = (bf16[16,1024]{1,0:T(8,128)(2,1)S(1)}, bf16[16,1024]{1,0:T(8,128)(2,1)S(1)}, u32[]{:S(2)}, u32[]{:S(2)}) collective-permute-start(bf16[16,1024]{1,0:T(8,128)(2,1)S(1)} %reshape.26), channel_id=1, source_target_pairs={{0,256},{32,288},{64,320},{96,352},{128,384},{160,416},{192,448},{... | collective-permute-start | bytes 98312 | tf_op jit(solution)/shard_map/ppermute | solution.py:37
  55.4 10.4 %collective-permute-start.3 = (bf16[64,1024]{1,0:T(8,128)(2,1)S(1)}, bf16[64,1024]{1,0:T(8,128)(2,1)S(1)}, u32[]{:S(2)}, u32[]{:S(2)}) collective-permute-start(bf16[64,1024]{1,0:T(8,128)(2,1)S(1)} %get-tuple-element.23), channel_id=1, source_target_pairs={{0,64},{32,96},{64,128},{96,160},{128,192},{160,224},{192,0},{224,... | collective-permute-start | bytes 393224 | tf_op jit(solution)/shard_map/ppermute | solution.py:37
  57.3 10.9 %collective-permute-start.4 = (bf16[64,1024]{1,0:T(8,128)(2,1)S(1)}, bf16[64,1024]{1,0:T(8,128)(2,1)S(1)}, u32[]{:S(2)}, u32[]{:S(2)}) collective-permute-start(bf16[64,1024]{1,0:T(8,128)(2,1)S(1)} %get-tuple-element.23), channel_id=1, source_target_pairs={{0,128},{32,160},{64,192},{96,224},{128,0},{160,32},{192,64},{224,... | collective-permute-start | bytes 393224 | tf_op jit(solution)/shard_map/ppermute | solution.py:37
  61.3 8.0 %collective-permute-start.5 = (bf16[64,1024]{1,0:T(8,128)(2,1)S(1)}, bf16[64,1024]{1,0:T(8,128)(2,1)S(1)}, u32[]{:S(2)}, u32[]{:S(2)}) collective-permute-start(bf16[64,1024]{1,0:T(8,128)(2,1)S(1)} %get-tuple-element.23), channel_id=1, source_target_pairs={{0,192},{32,224},{64,0},{96,32},{128,64},{160,96},{192,128},{224,1... | collective-permute-start | bytes 393224 | tf_op jit(solution)/shard_map/ppermute | solution.py:37
  69.3 3.9 %collective-permute-start.6 = (bf16[256,1024]{1,0:T(8,128)(2,1)S(1)}, bf16[256,1024]{1,0:T(8,128)(2,1)}, u32[]{:S(2)}, u32[]{:S(2)}) collective-permute-start(bf16[256,1024]{1,0:T(8,128)(2,1)S(1)} %constant_dynamic-update-slice_fusion.4.here_ref), channel_id=1, source_target_pairs={{0,32},{32,0},{64,96},{96,64},{128,160},{160,128},{192,224},{224,1... | collective-permute-start | bytes 1572872 | tf_op jit(solution)/shard_map/ppermute | solution.py:271
  75.0 0.6 copy-start.8
  96.7 1.2 copy-start.5
  99.0 0.8 copy-start.6
  99.8 17.2 %all-to-all-start.2 = ((bf16[8,64,512]{2,1,0:T(8,128)(2,1)}), bf16[8,64,512]{2,1,0:T(8,128)(2,1)S(1)}, u32[]{:S(2)}, u32[]{:S(2)}) async-start(bf16[8,64,512]{2,1,0:T(8,128)(2,1)} %bitcast.22), calls=%async_computation.2 | async-start | bytes 1048576 | tf_op jit(solution)/shard_map/all_to_all | solution.py:32
  107.3 1.2 copy-start.2
  108.5 1.2 copy-start.4
  135.2 25.9 %copy-start.9 = (bf16[512,128]{1,0:T(8,128)(2,1)S(1)}, bf16[512,128]{1,0:T(8,128)(2,1)}, u32[]{:S(2)}) copy-start(bf16[512,128]{1,0:T(8,128)(2,1)} %copy-done.8) | copy-start | bytes 393220
  161.5 3.7 %collective-permute-start.7 = (bf16[256,896]{1,0:T(8,128)(2,1)S(1)}, bf16[256,896]{1,0:T(8,128)(2,1)S(1)}, u32[]{:S(2)}, u32[]{:S(2)}) collective-permute-start(bf16[256,896]{1,0:T(8,128)(2,1)S(1)} %get-tuple-element.16), channel_id=1, source_target_pairs={{0,32},{32,0},{64,96},{96,64},{128,160},{160,128},{192,224},{224,1... | collective-permute-start | bytes 1376264 | tf_op jit(solution)/shard_map/ppermute | solution.py:283
  165.4 10.2 %collective-permute-start.8 = (bf16[64,896]{1,0:T(8,128)(2,1)S(1)}, bf16[64,896]{1,0:T(8,128)(2,1)S(1)}, u32[]{:S(2)}, u32[]{:S(2)}) collective-permute-start(bf16[64,896]{1,0:T(8,128)(2,1)S(1)} %get-tuple-element.17), channel_id=1, source_target_pairs={{64,0},{96,32},{128,64},{160,96},{192,128},{224,160},{0,192},{32,2... | collective-permute-start | bytes 344072 | tf_op jit(solution)/shard_map/ppermute | solution.py:37
  171.2 9.3 %collective-permute-start.10 = (bf16[64,896]{1,0:T(8,128)(2,1)S(1)}, bf16[64,896]{1,0:T(8,128)(2,1)S(1)}, u32[]{:S(2)}, u32[]{:S(2)}) collective-permute-start(bf16[64,896]{1,0:T(8,128)(2,1)S(1)} %get-tuple-element.18), channel_id=1, source_target_pairs={{192,0},{224,32},{0,64},{32,96},{64,128},{96,160},{128,192},{160,2... | collective-permute-start | bytes 344072 | tf_op jit(solution)/shard_map/ppermute | solution.py:37
  173.1 11.6 %collective-permute-start.9 = (bf16[64,896]{1,0:T(8,128)(2,1)S(1)}, bf16[64,896]{1,0:T(8,128)(2,1)S(1)}, u32[]{:S(2)}, u32[]{:S(2)}) collective-permute-start(bf16[64,896]{1,0:T(8,128)(2,1)S(1)} %get-tuple-element.19), channel_id=1, source_target_pairs={{128,0},{160,32},{192,64},{224,96},{0,128},{32,160},{64,192},{96,2... | collective-permute-start | bytes 344072 | tf_op jit(solution)/shard_map/ppermute | solution.py:37
  184.8 19.3 %collective-permute-start.11 = (bf16[16,896]{1,0:T(8,128)(2,1)S(1)}, bf16[16,896]{1,0:T(8,128)(2,1)S(1)}, u32[]{:S(2)}, u32[]{:S(2)}) collective-permute-start(bf16[16,896]{1,0:T(8,128)(2,1)S(1)} %get-tuple-element.20), channel_id=1, source_target_pairs={{256,0},{288,32},{320,64},{352,96},{384,128},{416,160},{448,192},{... | collective-permute-start | bytes 86024 | tf_op jit(solution)/shard_map/ppermute | solution.py:37
  190.8 13.3 %collective-permute-start.13 = (bf16[16,896]{1,0:T(8,128)(2,1)S(1)}, bf16[16,896]{1,0:T(8,128)(2,1)S(1)}, u32[]{:S(2)}, u32[]{:S(2)}) collective-permute-start(bf16[16,896]{1,0:T(8,128)(2,1)S(1)} %get-tuple-element.21), channel_id=1, source_target_pairs={{768,0},{800,32},{832,64},{864,96},{896,128},{928,160},{960,192},{... | collective-permute-start | bytes 86024 | tf_op jit(solution)/shard_map/ppermute | solution.py:37
  194.6 14.5 %collective-permute-start.12 = (bf16[16,896]{1,0:T(8,128)(2,1)S(1)}, bf16[16,896]{1,0:T(8,128)(2,1)S(1)}, u32[]{:S(2)}, u32[]{:S(2)}) collective-permute-start(bf16[16,896]{1,0:T(8,128)(2,1)S(1)} %get-tuple-element.22), channel_id=1, source_target_pairs={{512,0},{544,32},{576,64},{608,96},{640,128},{672,160},{704,192},{... | collective-permute-start | bytes 86024 | tf_op jit(solution)/shard_map/ppermute | solution.py:37

commit v3 on v2

--- a/solution.py
+++ b/solution.py
@@ -9,7 +9,6 @@
 
 SPLIT = 8
 C_DEV = 2
-Z_NEAR = 4
 META = 128
 VMEM = 48 * 1024 * 1024
 f32, bf16 = jnp.float32, jnp.bfloat16
@@ -28,18 +27,45 @@
     )
 
 
+def hbm(*arrays):
+    return [pltpu.with_memory_space_constraint(a, pltpu.HBM) for a in arrays]
+
+
 def swap(a, axis, members):
     return lax.all_to_all(a, axis, 0, 0, axis_index_groups=members, tiled=True)
 
 
-def rounds(blocks, axis, moves):
-    return [blocks[0]] + [
-        lax.ppermute(block, axis, move) for block, move in zip(blocks[1:], moves)
-    ]
-
-
 def total(blocks):
     return functools.reduce(lambda p, q: p + q, [b.astype(f32) for b in blocks]).astype(bf16)
+
+
+def pack_body(per_node, node_ref, grad_ref, ids_ref, slots_ref, gates_ref, out_ref, held):
+    n_tok, n_pick = ids_ref.shape
+    part = out_ref.shape[1] - META
+    slots = slots_ref[...]
+    slots = jnp.where(slots >= 0, slots - node_ref[0] * per_node, -1)
+    held[...] = jnp.zeros_like(held)
+    grad = grad_ref[...].astype(f32)
+    for i in range(SPLIT):
+        rows = slice(i * n_tok, (i + 1) * n_tok)
+        held[rows, :part] = grad[:, i * part : (i + 1) * part]
+        for j, field in enumerate((ids_ref[...], slots, gates_ref[...])):
+            held[rows, part + j * n_pick : part + (j + 1) * n_pick] = field.astype(f32)
+    out_ref[...] = held[...].astype(bf16)
+
+
+def pack(node, grad, ids, slots, gates, per_node):
+    n_tok, width = grad.shape
+    shape = (SPLIT * n_tok, width // SPLIT + META)
+    return call(
+        functools.partial(pack_body, per_node),
+        jax.ShapeDtypeStruct(shape, bf16),
+        (0, 4 * n_tok * width),
+        in_specs=[pl.BlockSpec(memory_space=pltpu.SMEM)]
+        + [pl.BlockSpec(memory_space=pltpu.VMEM)] * 4,
+        out_specs=pl.BlockSpec(memory_space=pltpu.VMEM),
+        scratch_shapes=[pltpu.VMEM(shape, f32)],
+    )(node, grad, ids, slots, gates)
 
 
 def cut_body(gate_ref, up_ref, down_ref, out_ref):
@@ -55,12 +81,12 @@
     spec = pl.BlockSpec((n_hid, part), lambda i: (0, i))
     return call(
         cut_body,
-        jax.ShapeDtypeStruct((SPLIT, 3 * n_hid, part), bf16),
+        pltpu.HBM((SPLIT, 3 * n_hid, part), bf16),
         (0, 12 * n_hid * width),
         grid=(SPLIT,),
         in_specs=[spec] * 3,
         out_specs=pl.BlockSpec((1, 3 * n_hid, part), lambda i: (i, 0, 0)),
-    )(gate, up, down)
+    )(*hbm(gate, up, down))
 
 
 def forward_body(x_ref, gate_ref, up_ref, out_ref, acc):
@@ -100,7 +126,7 @@
         in_specs=[pl.BlockSpec((n_slot, part), lambda i: (0, i)), spec, spec],
         out_specs=pl.BlockSpec((2 * n_hid, n_slot), lambda i: (0, 0)),
         scratch_shapes=[pltpu.VMEM((2 * n_hid, n_slot), f32)],
-    )(x, gate, up)
+    )(*hbm(x, gate, up))
 
 
 def select_body(n_tok, per_node, n_pick, expert_ref, here_ref, there_ref, rows_ref, hot_ref):
@@ -119,18 +145,20 @@
     one_hot = (found >= 0) & (node * per_node + found == lane)
     hot_ref[...] = jnp.where(one_hot, scale, 0.0).astype(bf16)
     pick = jnp.where(one_hot, 1.0, 0.0).T.astype(bf16)
-    rows_ref[...] = jnp.dot(pick, tok[:, :part], preferred_element_type=f32).astype(bf16)
-
-
-def select(expert, here, there, n_tok, per_node, n_pick):
+    rows = jnp.dot(pick, tok[:, :part], preferred_element_type=f32).astype(bf16)
+    for i in range(rows_ref.shape[0] // rows.shape[0]):
+        rows_ref[i * rows.shape[0] : (i + 1) * rows.shape[0]] = rows
+
+
+def select(expert, here, there, n_rest, n_tok, per_node, n_pick):
     n_all, wide = 2 * here.shape[0], here.shape[1]
     part = wide - META
     n_own = SPLIT * per_node
     return call(
         functools.partial(select_body, n_tok, per_node, n_pick),
         (
-            jax.ShapeDtypeStruct((n_own, part), bf16),
-            jax.ShapeDtypeStruct((n_all, n_own), bf16),
+            pltpu.HBM((n_rest * n_own, part), bf16),
+            pltpu.HBM((n_all, n_own), bf16),
         ),
         (2 * n_all * n_own * part, 2 * n_all * wide),
         in_specs=[
@@ -160,7 +188,7 @@
     half = n_slot // 2
     return call(
         hidden_body,
-        jax.ShapeDtypeStruct((n * h, n_slot), bf16),
+        pltpu.HBM((n * h, n_slot), bf16),
         (2 * n * h * n_slot * part, 2 * (n * h + n_slot) * part),
         grid=(2,),
         in_specs=[
@@ -231,19 +259,28 @@
     )(hot, parts)
 
 
+def unpack_body(parts_ref, out_ref):
+    n_tok = out_ref.shape[0]
+    added = jnp.sum(parts_ref[...].astype(f32), axis=0)
+    pieces = [added[i * n_tok : (i + 1) * n_tok] for i in range(SPLIT)]
+    out_ref[...] = jnp.concatenate(pieces, axis=1).astype(bf16)
+
+
+def unpack(parts, n_tok):
+    return call(
+        unpack_body,
+        jax.ShapeDtypeStruct((n_tok, SPLIT * parts.shape[2]), bf16),
+        (parts.size, 2 * parts.size),
+    )(parts)
+
+
 def local(out_grad, expert_ids, slot_ids, gate_q, saved_x, w_gate, w_up, w_down):
     n_grp, n_node = lax.axis_size("grp"), lax.axis_size("node")
     my_expert, my_node = lax.axis_index("grp"), lax.axis_index("node")
     n_rest, n_z = n_node // SPLIT, n_grp // C_DEV
-    z_far = n_z // Z_NEAR
     block = [[h * SPLIT + d for d in range(SPLIT)] for h in range(n_rest)]
-    rest = [[h * SPLIT + d for h in range(n_rest)] for d in range(SPLIT)]
-    at = lambda far, near, c: (far * Z_NEAR + near) * C_DEV + c
-    devices = [(f, n, c) for f in range(z_far) for n in range(Z_NEAR) for c in range(C_DEV)]
-    far = [[(at(f, n, c), at((f + k) % z_far, n, c)) for f, n, c in devices] for k in range(1, z_far)]
-    near = [[(at(f, n, c), at(f, (n + j) % Z_NEAR, c)) for f, n, c in devices] for j in range(1, Z_NEAR)]
-    other = [(at(f, n, c), at(f, n, C_DEV - 1 - c)) for f, n, c in devices]
-    undo = lambda moves: [[(to, frm) for frm, to in move] for move in moves]
+    along_z = [[z * C_DEV + c for z in range(n_z)] for c in range(C_DEV)]
+    other = [(z * C_DEV + c, z * C_DEV + 1 - c) for z in range(n_z) for c in range(C_DEV)]
     n_tok, width = out_grad.shape
     part = width // SPLIT
     n_slot = saved_x.shape[1]
@@ -253,38 +290,29 @@
     n_own = SPLIT * per_node
     gate, up, down = w_gate[0].T, w_up[0].T, w_down[0]
 
-    slot_here = jnp.where(slot_ids >= 0, slot_ids - my_node * per_node, -1)
-    meta = jnp.concatenate([expert_ids, slot_here, gate_q], axis=1).astype(bf16)
-    meta = jnp.pad(meta, ((0, 0), (0, META - 3 * n_pick)))
-    cols = out_grad.reshape(n_tok, SPLIT, part).transpose(1, 0, 2)
-    payload = jnp.concatenate(
-        [cols, jnp.broadcast_to(meta[None], (SPLIT, n_tok, META))], axis=2
-    )
-    payload = swap(payload, "node", block).reshape(SPLIT * n_tok, part + META)
+    payload = pack(my_node.astype(jnp.int32).reshape(1), out_grad, expert_ids, slot_ids, gate_q, per_node)
 
     weights = cut_weights(gate, up, down)
     payload, weights = lax.optimization_barrier((payload, weights))
     weights = swap(weights, "node", block)
 
-    tokens = jnp.concatenate(rounds([payload] * z_far, "grp", far), axis=0)
-    tokens = jnp.concatenate(rounds([tokens] * Z_NEAR, "grp", near), axis=0)
-    there = lax.ppermute(tokens, "grp", other)
+    here = lax.all_gather(payload, "grp", axis=0, axis_index_groups=along_z, tiled=True)
+    there = lax.ppermute(here, "grp", other)
     expert = my_expert.astype(jnp.int32).reshape(1)
-    rows, hot = select(expert, tokens, there, n_tok, per_node, n_pick)
-    rows = lax.all_gather(rows, "node", axis=0, axis_index_groups=rest, tiled=True)
-
-    hidden = hidden_part(weights, rows)
+    rows, hot = select(expert, here, there, n_rest, n_tok, per_node, n_pick)
+    rows, weights = lax.optimization_barrier((rows, weights))
+    rows = lax.all_to_all(rows, "node", 0, 0, tiled=True)
+
+    coef = forward(saved_x[0], gate, up)
+    hidden, coef = lax.optimization_barrier((hidden_part(weights, rows), coef))
     hidden = swap(hidden, "node", block).reshape(SPLIT, n_hid, n_slot)
-    coef = forward(saved_x[0], gate, up)
     grads = swap(grads_of(hidden, coef), "node", block)
-    parts = swap(slot_part(grads, weights), "node", rest)
+    parts = lax.all_to_all(slot_part(grads, weights), "node", 0, 0, tiled=True)
 
     here, there = back_rows(hot, parts.reshape(n_rest, n_own, part))
     back = total([here, lax.ppermute(there, "grp", other)])
-    back = total(rounds(jnp.split(back, Z_NEAR), "grp", undo(near)))
-    back = total(rounds(jnp.split(back, z_far), "grp", undo(far)))
-    back = swap(back.reshape(SPLIT, n_tok, part), "node", block)
-    return back.transpose(1, 0, 2).reshape(n_tok, width)
+    back = swap(back, "grp", along_z).reshape(n_z, SPLIT * n_tok, part)
+    return unpack(back, n_tok)
 
 
 def solution(mesh):

time: 222 us -> 197 us (0.89)
  starting transfers between devices: 86.2 us -> 29.8 us
  blocking collectives: 74.6 us -> 122 us
  local copies, waits for them, and re-layouts: 10.7 us -> 0.02 us
  waiting for transfers between devices: 32.4 us -> 21.8 us
  Pallas kernels: 13.1 us -> 22.2 us
  other arithmetic: 3.7 us -> 0.11 us
    ppermute x13 -> x1, starting transfers between devices: 56.4 us -> 1.91 us  [local(): there = lax.ppermute(here, 'grp', other)]
    all_to_all x0 -> x1, blocking collectives: none -> 28.3 us  [local(): parts = lax.all_to_all(slot_part(grads, weights), 'node', 0, 0, tiled=True)]
    ppermute x13 -> x1, waiting for transfers between devices: 24.9 us -> 2 us  [local(): there = lax.ppermute(here, 'grp', other)]
    all_to_all x0 -> x1, waiting for transfers between devices: none -> 18.1 us  [local(): rows = lax.all_to_all(rows, 'node', 0, 0, tiled=True)]
    all_gather x1, blocking collectives: 21.1 us -> 34.7 us  [local(): lax.all_gather(payload, 'grp', axis=0, axis_index_groups=along_z, tiled=T...]
    all_to_all x3 -> x1, starting transfers between devices: 27.8 us -> 16.7 us  [swap(): return lax.all_to_all(a, axis, 0, 0, axis_index_groups=members, tiled=True)]
    unnamed x26 -> x10, local copies, waits for them, and re-layouts: 10.6 us -> 0.02 us
    all_to_all x0 -> x1, starting transfers between devices: none -> 9.24 us  [local(): rows = lax.all_to_all(rows, 'node', 0, 0, tiled=True)]
  transfers between devices with their start and end apart: 17 -> 4, of which waited for: 9 -> 3; matrix products, arithmetic and copies ran while one was open for 0% -> 0% of each run, Pallas kernels for 4% -> 5%
where the time goes in v3:
time: 197 us; the launch traced here: 196 us
  blocking collectives  122 us (62%)
  starting transfers between devices  29.8 us (15%)
  Pallas kernels  22.2 us (11%)
  waiting for transfers between devices  21.8 us (11%)
    all_to_all x3, blocking collectives, swap(): return lax.all_to_all(a, axis, 0, 0, axis_index_groups=members, tiled=True)  59 us
    all_gather x1, blocking collectives, local(): lax.all_gather(payload, 'grp', axis=0, axis_index_groups=along_z, tiled=T...  34.7 us
    all_to_all x1, blocking collectives, local(): parts = lax.all_to_all(slot_part(grads, weights), 'node', 0, 0, tiled=True)  28.3 us
    all_to_all x1, waiting for transfers between devices, local(): rows = lax.all_to_all(rows, 'node', 0, 0, tiled=True)  18.1 us
    all_to_all x1, starting transfers between devices, swap(): return lax.all_to_all(a, axis, 0, 0, axis_index_groups=members, tiled=True)  16.7 us
    all_to_all x1, starting transfers between devices, local(): rows = lax.all_to_all(rows, 'node', 0, 0, tiled=True)  9.24 us
    pallas_call x1, Pallas kernels, forward(): call(forward_body, jax.ShapeDtypeStruct((2 * n_hid, n_slot), f32), (4 * n...  7.55 us
    pallas_call x1, Pallas kernels, cut_weights(): call(cut_body, pltpu.HBM((SPLIT, 3 * n_hid, part), bf16), (0, 12 * n_hid...  6.13 us
  transfers between devices with their start and end apart: 4, of which 3 were waited for; matrix products, arithmetic and copies ran while one was open for 0% of the time, Pallas kernels for 5%

profile of v3, /device:TPU:2, one launch (start us, length us, event | category | flops | bytes accessed | tf_op | source)
XLA Modules:
  0.0 196.1 jit_solution(4511093119871198494)
XLA Ops:
  0.0 0.0 copy-start.1
  0.0 0.0 copy-start.2
  0.0 0.0 copy-start.3
  0.0 0.0 copy-start.4
  0.0 6.1 %shard_map.83 = bf16[8,192,896]{2,1,0:T(8,128)(2,1)} custom-call(bf16[64,7168]{1,0:T(8,128)(2,1)} %bitcast.19, bf16[64,7168]{1,0:T(8,128)(2,1)} %bitcast.21, bf16[64,7168]{1,0:T(8,128)(2,1)} %bitcast.26), custom_call_target="tpu_custom_call" | custom-call | bytes 5505024 | tf_op jit(solution)/shard_map/pallas_call | solution.py:82
  6.1 0.0 copy-done.1
  6.1 0.0 copy-done.2
  6.2 0.0 copy-done.3
  6.2 0.0 copy-done.4
  6.2 0.1 shard_map.82
  6.3 16.7 %all-to-all-start = ((bf16[8,192,896]{2,1,0:T(8,128)(2,1)}), bf16[8,192,896]{2,1,0:T(8,128)(2,1)S(1)}, u32[]{:S(2)}, u32[]{:S(2)}) async-start(bf16[8,192,896]{2,1,0:T(8,128)(2,1)} %shard_map.83), calls=%async_computation | async-start | bytes 5505024 | tf_op jit(solution)/shard_map/all_to_all | solution.py:35
  23.0 34.7 %all_gather.3.here_ref = bf16[256,1024]{1,0:T(8,128)(2,1)S(1)} all-gather(bf16[16,1024]{1,0:T(8,128)(2,1)S(1)} %shard_map.82), channel_id=1, replica_groups={{0,64,128,192,256,320,384,448,512,576,640,704,768,832,896,960},{32,96,1..., dimensions={0}, use_global_device_ids=true | all-gather | bytes 557056 | tf_op jit(solution)/shard_map/all_gather | solution.py:299
  57.7 1.9 collective-permute-start
  59.6 2.0 %collective-permute-done.there_ref = bf16[256,1024]{1,0:T(8,128)(2,1)} collective-permute-done((bf16[256,1024]{1,0:T(8,128)(2,1)S(1)}, bf16[256,1024]{1,0:T(8,128)(2,1)}, u32[]{:S(2)}, u32[]{:S(2)}) %collective-permute-start) | collective-permute-done | bytes 524320 | tf_op jit(solution)/shard_map/ppermute | solution.py:300
  61.6 2.7 %shard_map.84 = (bf16[512,896]{1,0:T(8,128)(2,1)}, bf16[512,128]{1,0:T(8,128)(2,1)}) custom-call(s32[1]{0:T(128)} %bitcast.expert_ref, bf16[256,1024]{1,0:T(8,128)(2,1)S(1)} %all_gather.3.here_ref, bf16[256,1024]{1,0:T(8,128)(2,1)} %collective-permute-done.there_ref), custom_call_target="tpu_custom_call" | custom-call | flops 117440512 | bytes 1048576 | tf_op jit(solution)/shard_map/pallas_call | solution.py:157
  64.3 0.0 all-to-all-done.w_ref
  64.3 9.2 %all-to-all-start.1 = ((bf16[32,16,896]{2,1,0:T(8,128)(2,1)}), bf16[32,16,896]{2,1,0:T(8,128)(2,1)}, u32[]{:S(2)}, u32[]{:S(2)}) async-start(bf16[32,16,896]{2,1,0:T(8,128)(2,1)} %bitcast.25), calls=%async_computation.1 | async-start | bytes 1835008 | tf_op jit(solution)/shard_map/all_to_all | solution.py:304
  73.6 7.6 %shard_map.86.coef_ref = f32[128,512]{1,0:T(8,128)S(1)} custom-call(bf16[512,7168]{1,0:T(8,128)(2,1)} %bitcast.18, bf16[64,7168]{1,0:T(8,128)(2,1)} %bitcast.20, bf16[64,7168]{1,0:T(8,128)(2,1)} %bitcast.22), custom_call_target="tpu_custom_call" | custom-call | flops 939524096 | bytes 9175040 | tf_op jit(solution)/shard_map/pallas_call | solution.py:121
  81.1 18.1 %all-to-all-done.1 = bf16[32,16,896]{2,1,0:T(8,128)(2,1)} async-done(((bf16[32,16,896]{2,1,0:T(8,128)(2,1)}), bf16[32,16,896]{2,1,0:T(8,128)(2,1)}, u32[]{:S(2)}, u32[]{:S(2)}) %all-to-all-start.1) | async-done | bytes 917536 | tf_op jit(solution)/shard_map/all_to_all | solution.py:304
  99.2 2.7 %shard_map.85 = bf16[512,512]{1,0:T(8,128)(2,1)} custom-call(bf16[8,192,896]{2,1,0:T(8,128)(2,1)S(1)} %all-to-all-done.w_ref, bf16[512,896]{1,0:T(8,128)(2,1)} %bitcast.8.rows_ref), custom_call_target="tpu_custom_call" | custom-call | flops 469762048 | bytes 1835008 | tf_op jit(solution)/shard_map/pallas_call | solution.py:189
  101.9 11.9 %all_to_all.48.parts_ref = bf16[8,64,512]{2,1,0:T(8,128)(2,1)S(1)} all-to-all(bf16[8,64,512]{2,1,0:T(8,128)(2,1)} %bitcast.23), channel_id=1, replica_groups={{0,1,2,3,4,5,6,7},{8,9,10,11,12,13,14,15},{16,17,18,19,20,21,22,23},{24..., dimensions={0} | all-to-all | bytes 1048576 | tf_op jit(solution)/shard_map/all_to_all | solution.py:35
  113.8 0.2 shard_map.87
  114.0 16.5 %all_to_all.49.grads_ref = bf16[8,512,128]{2,1,0:T(8,128)(2,1)S(1)} all-to-all(bf16[8,512,128]{2,1,0:T(8,128)(2,1)S(1)} %shard_map.87), channel_id=1, replica_groups={{0,1,2,3,4,5,6,7},{8,9,10,11,12,13,14,15},{16,17,18,19,20,21,22,23},{24..., dimensions={0} | all-to-all | bytes 2097152 | tf_op jit(solution)/shard_map/all_to_all | solution.py:35
  130.5 0.0 copy-start
  130.5 1.7 shard_map.88
  132.2 28.3 %all_to_all.50 = bf16[32,16,896]{2,1,0:T(8,128)(2,1)S(1)} all-to-all(bf16[32,16,896]{2,1,0:T(8,128)(2,1)S(1)} %bitcast.16), channel_id=1, replica_groups=mesh['grp'=32,'node'=32] {'node'}, dimensions={0} | all-to-all | bytes 1835008 | tf_op jit(solution)/shard_map/all_to_all | solution.py:310
  160.5 0.0 copy-done
  160.5 0.4 shard_map.89
  161.0 1.9 collective-permute-start.1
  162.9 1.8 collective-permute-done.1
  164.7 0.1 add_convert_fusion
  164.8 30.6 %all_to_all.51.parts_ref = bf16[16,16,896]{2,1,0:T(8,128)(2,1)S(1)} all-to-all(bf16[16,16,896]{2,1,0:T(8,128)(2,1)S(1)} %bitcast.24), channel_id=1, replica_groups={{0,64,128,192,256,320,384,448,512,576,640,704,768,832,896,960},{32,96,1..., dimensions={0} | all-to-all | bytes 917504 | tf_op jit(solution)/shard_map/all_to_all | solution.py:35
  195.4 0.7 shard_map.90
Async XLA Ops:
  0.0 6.1 %copy-start.1 = (bf16[2,7168]{1,0:T(2,128)(2,1)S(1)}, bf16[2,7168]{1,0:T(2,128)(2,1)}, u32[]{:S(2)}) copy-start(bf16[2,7168]{1,0:T(2,128)(2,1)} %grad_ref.1) | copy-start | bytes 86020
  0.0 6.1 %copy-start.2 = (s32[2,8]{1,0:T(2,128)S(1)}, s32[2,8]{1,0:T(2,128)}, u32[]{:S(2)}) copy-start(s32[2,8]{1,0:T(2,128)} %ids_ref.1) | copy-start | bytes 196
  0.0 6.1 %copy-start.3 = (s32[2,8]{1,0:T(2,128)S(1)}, s32[2,8]{1,0:T(2,128)}, u32[]{:S(2)}) copy-start(s32[2,8]{1,0:T(2,128)} %slots_ref.1) | copy-start | bytes 196
  0.0 6.1 %copy-start.4 = (s32[2,8]{1,0:T(2,128)S(1)}, s32[2,8]{1,0:T(2,128)}, u32[]{:S(2)}) copy-start(s32[2,8]{1,0:T(2,128)} %gates_ref.1) | copy-start | bytes 196
  6.3 58.1 %all-to-all-start = ((bf16[8,192,896]{2,1,0:T(8,128)(2,1)}), bf16[8,192,896]{2,1,0:T(8,128)(2,1)S(1)}, u32[]{:S(2)}, u32[]{:S(2)}) async-start(bf16[8,192,896]{2,1,0:T(8,128)(2,1)} %shard_map.83), calls=%async_computation | async-start | bytes 5505024 | tf_op jit(solution)/shard_map/all_to_all | solution.py:35
  57.7 3.9 %collective-permute-start = (bf16[256,1024]{1,0:T(8,128)(2,1)S(1)}, bf16[256,1024]{1,0:T(8,128)(2,1)}, u32[]{:S(2)}, u32[]{:S(2)}) collective-permute-start(bf16[256,1024]{1,0:T(8,128)(2,1)S(1)} %all_gather.3.here_ref), channel_id=1, source_target_pairs={{0,32},{32,0},{64,96},{96,64},{128,160},{160,128},{192,224},{224,1... | collective-permute-start | bytes 1572872 | tf_op jit(solution)/shard_map/ppermute | solution.py:300
  64.3 34.9 %all-to-all-start.1 = ((bf16[32,16,896]{2,1,0:T(8,128)(2,1)}), bf16[32,16,896]{2,1,0:T(8,128)(2,1)}, u32[]{:S(2)}, u32[]{:S(2)}) async-start(bf16[32,16,896]{2,1,0:T(8,128)(2,1)} %bitcast.25), calls=%async_computation.1 | async-start | bytes 1835008 | tf_op jit(solution)/shard_map/all_to_all | solution.py:304
  130.5 30.0 %copy-start = (bf16[512,128]{1,0:T(8,128)(2,1)S(1)}, bf16[512,128]{1,0:T(8,128)(2,1)}, u32[]{:S(2)}) copy-start(bf16[512,128]{1,0:T(8,128)(2,1)} %get-tuple-element.16.hot_ref) | copy-start | bytes 393220
  161.0 3.7 %collective-permute-start.1 = (bf16[256,896]{1,0:T(8,128)(2,1)S(1)}, bf16[256,896]{1,0:T(8,128)(2,1)S(1)}, u32[]{:S(2)}, u32[]{:S(2)}) collective-permute-start(bf16[256,896]{1,0:T(8,128)(2,1)S(1)} %get-tuple-element.24), channel_id=1, source_target_pairs={{0,32},{32,0},{64,96},{96,64},{128,160},{160,128},{192,224},{224,1... | collective-permute-start | bytes 1376264 | tf_op jit(solution)/shard_map/ppermute | solution.py:313

commit v4 on v3

--- a/solution.py
+++ b/solution.py
@@ -68,71 +68,83 @@
     )(node, grad, ids, slots, gates)
 
 
-def cut_body(gate_ref, up_ref, down_ref, out_ref):
+def cut_body(gate_ref, up_ref, down_ref, out_ref, held, sem_in, sem_out):
     n = gate_ref.shape[0]
-    out_ref[0, :n] = gate_ref[...]
-    out_ref[0, n : 2 * n] = up_ref[...]
-    out_ref[0, 2 * n :] = down_ref[...]
+    part = out_ref.shape[2]
+    come = [
+        [
+            pltpu.make_async_copy(
+                ref.at[:, pl.ds(i * part, part)],
+                held.at[i, pl.ds(j * n, n)],
+                sem_in.at[i, j],
+            )
+            for j, ref in enumerate((gate_ref, up_ref, down_ref))
+        ]
+        for i in range(SPLIT)
+    ]
+    leave = [
+        pltpu.make_async_copy(held.at[i], out_ref.at[i], sem_out.at[i])
+        for i in range(SPLIT)
+    ]
+    for copies in come:
+        for copy in copies:
+            copy.start()
+    for i in range(SPLIT):
+        for copy in come[i]:
+            copy.wait()
+        leave[i].start()
+    for copy in leave:
+        copy.wait()
 
 
 def cut_weights(gate, up, down):
     n_hid, width = gate.shape
-    part = width // SPLIT
-    spec = pl.BlockSpec((n_hid, part), lambda i: (0, i))
+    shape = (SPLIT, 3 * n_hid, width // SPLIT)
     return call(
         cut_body,
-        pltpu.HBM((SPLIT, 3 * n_hid, part), bf16),
+        pltpu.HBM(shape, bf16),
         (0, 12 * n_hid * width),
-        grid=(SPLIT,),
-        in_specs=[spec] * 3,
-        out_specs=pl.BlockSpec((1, 3 * n_hid, part), lambda i: (i, 0, 0)),
+        in_specs=[pl.BlockSpec(memory_space=pl.ANY)] * 3,
+        out_specs=pl.BlockSpec(memory_space=pl.ANY),
+        scratch_shapes=[
+            pltpu.VMEM(shape, bf16),
+            pltpu.SemaphoreType.DMA((SPLIT, 3)),
+            pltpu.SemaphoreType.DMA((SPLIT,)),
+        ],
     )(*hbm(gate, up, down))
 
 
-def forward_body(x_ref, gate_ref, up_ref, out_ref, acc):
-    step = pl.program_id(0)
+def forward_body(x_ref, gate_ref, up_ref, out_ref):
     n = gate_ref.shape[0]
     both = jnp.concatenate([gate_ref[...], up_ref[...]], axis=0)
-    term = lax.dot_general(
-        both, x_ref[...], (((1,), (1,)), ((), ())), preferred_element_type=f32
-    )
-
-    @pl.when(step == 0)
-    def _():
-        acc[...] = term
-
-    @pl.when(step > 0)
-    def _():
-        acc[...] += term
-
-    @pl.when(step == pl.num_programs(0) - 1)
-    def _():
-        pre_gate, pre_up = acc[:n], acc[n:]
-        squash = jax.nn.sigmoid(pre_gate)
-        out_ref[:n] = pre_up * squash * (1.0 + pre_gate * (1.0 - squash))
-        out_ref[n:] = pre_gate * squash
+    pre = lax.dot_general(
+        x_ref[...], both, (((1,), (1,)), ((), ())), preferred_element_type=f32
+    ).T
+    pre_gate, pre_up = pre[:n], pre[n:]
+    squash = jax.nn.sigmoid(pre_gate)
+    out_ref[:n] = pre_up * squash * (1.0 + pre_gate * (1.0 - squash))
+    out_ref[n:] = pre_gate * squash
 
 
 def forward(x, gate, up):
     n_slot, width = x.shape
     n_hid = gate.shape[0]
-    part = width // 8
-    spec = pl.BlockSpec((n_hid, part), lambda i: (0, i))
+    half = n_slot // 2
+    spec = pl.BlockSpec((n_hid, width), lambda i: (0, 0))
     return call(
         forward_body,
         jax.ShapeDtypeStruct((2 * n_hid, n_slot), f32),
         (4 * n_hid * n_slot * width, 2 * (n_slot + 2 * n_hid) * width),
-        grid=(8,),
-        in_specs=[pl.BlockSpec((n_slot, part), lambda i: (0, i)), spec, spec],
-        out_specs=pl.BlockSpec((2 * n_hid, n_slot), lambda i: (0, 0)),
-        scratch_shapes=[pltpu.VMEM((2 * n_hid, n_slot), f32)],
+        grid=(2,),
+        in_specs=[pl.BlockSpec((half, width), lambda i: (i, 0)), spec, spec],
+        out_specs=pl.BlockSpec((2 * n_hid, half), lambda i: (0, i)),
     )(*hbm(x, gate, up))
 
 
-def select_body(n_tok, per_node, n_pick, expert_ref, here_ref, there_ref, rows_ref, hot_ref):
+def select_body(n_tok, per_node, n_pick, expert_ref, tok_ref, *refs):
+    rows_ref, hot_ref = refs[-2:]
     part = rows_ref.shape[1]
-    tok = jnp.concatenate([here_ref[...], there_ref[...]], axis=0)
-    rout = tok[:, part:].astype(f32)
+    rout = tok_ref[:, part:].astype(f32)
     lane = lax.broadcasted_iota(jnp.int32, rout.shape, 1)
     row = lax.broadcasted_iota(jnp.int32, rout.shape, 0)
     slot = pltpu.roll(rout, META - n_pick, 1)
@@ -145,29 +157,28 @@
     one_hot = (found >= 0) & (node * per_node + found == lane)
     hot_ref[...] = jnp.where(one_hot, scale, 0.0).astype(bf16)
     pick = jnp.where(one_hot, 1.0, 0.0).T.astype(bf16)
-    rows = jnp.dot(pick, tok[:, :part], preferred_element_type=f32).astype(bf16)
+    rows = jnp.dot(pick, tok_ref[:, :part], preferred_element_type=f32).astype(bf16)
+    if len(refs) == 3:
+        rows = rows + refs[0][...]
     for i in range(rows_ref.shape[0] // rows.shape[0]):
         rows_ref[i * rows.shape[0] : (i + 1) * rows.shape[0]] = rows
 
 
-def select(expert, here, there, n_rest, n_tok, per_node, n_pick):
-    n_all, wide = 2 * here.shape[0], here.shape[1]
+def select(expert, tokens, before, copies, n_tok, per_node, n_pick):
+    n_all, wide = tokens.shape
     part = wide - META
     n_own = SPLIT * per_node
     return call(
         functools.partial(select_body, n_tok, per_node, n_pick),
         (
-            pltpu.HBM((n_rest * n_own, part), bf16),
+            (pltpu.HBM if before else jax.ShapeDtypeStruct)((copies * n_own, part), bf16),
             pltpu.HBM((n_all, n_own), bf16),
         ),
         (2 * n_all * n_own * part, 2 * n_all * wide),
-        in_specs=[
-            pl.BlockSpec(memory_space=pltpu.SMEM),
-            pl.BlockSpec(memory_space=pltpu.VMEM),
-            pl.BlockSpec(memory_space=pltpu.VMEM),
-        ],
+        in_specs=[pl.BlockSpec(memory_space=pltpu.SMEM)]
+        + [pl.BlockSpec(memory_space=pltpu.VMEM)] * (1 + len(before)),
         out_specs=[pl.BlockSpec(memory_space=pltpu.VMEM)] * 2,
-    )(expert, here, there)
+    )(expert, tokens, *before)
 
 
 def hidden_body(w_ref, rows_ref, out_ref):
@@ -241,22 +252,21 @@
     )(grads, weights)
 
 
-def back_body(hot_ref, parts_ref, here_ref, there_ref):
+def back_body(hot_here_ref, hot_there_ref, parts_ref, here_ref, there_ref):
     own = jnp.sum(parts_ref[...].astype(f32), axis=0).astype(bf16)
-    got = jnp.dot(hot_ref[...], own, preferred_element_type=f32).astype(bf16)
-    half = here_ref.shape[0]
-    here_ref[...] = got[:half]
-    there_ref[...] = got[half:]
-
-
-def back_rows(hot, parts):
-    n_all, n_own = hot.shape
+    for hot_ref, out_ref in ((hot_there_ref, there_ref), (hot_here_ref, here_ref)):
+        got = jnp.dot(hot_ref[...], own, preferred_element_type=f32)
+        out_ref[...] = got.astype(bf16)
+
+
+def back_rows(hot_here, hot_there, parts):
+    half, n_own = hot_here.shape
     part = parts.shape[2]
     return call(
         back_body,
-        (jax.ShapeDtypeStruct((n_all // 2, part), bf16),) * 2,
-        (2 * n_all * n_own * part, 2 * (n_all * part + parts.size)),
-    )(hot, parts)
+        (jax.ShapeDtypeStruct((half, part), bf16),) * 2,
+        (4 * half * n_own * part, 4 * half * part + 2 * parts.size),
+    )(hot_here, hot_there, parts)
 
 
 def unpack_body(parts_ref, out_ref):
@@ -299,17 +309,19 @@
     here = lax.all_gather(payload, "grp", axis=0, axis_index_groups=along_z, tiled=True)
     there = lax.ppermute(here, "grp", other)
     expert = my_expert.astype(jnp.int32).reshape(1)
-    rows, hot = select(expert, here, there, n_rest, n_tok, per_node, n_pick)
+    rows, hot_here = select(expert, here, (), 1, n_tok, per_node, n_pick)
+    rows, hot_there = select(expert, there, (rows,), n_rest, n_tok, per_node, n_pick)
     rows, weights = lax.optimization_barrier((rows, weights))
     rows = lax.all_to_all(rows, "node", 0, 0, tiled=True)
 
+    gate, rows = lax.optimization_barrier((gate, rows))
+    hidden = swap(hidden_part(weights, rows), "node", block)
+    hidden = hidden.reshape(SPLIT, n_hid, n_slot)
     coef = forward(saved_x[0], gate, up)
-    hidden, coef = lax.optimization_barrier((hidden_part(weights, rows), coef))
-    hidden = swap(hidden, "node", block).reshape(SPLIT, n_hid, n_slot)
     grads = swap(grads_of(hidden, coef), "node", block)
     parts = lax.all_to_all(slot_part(grads, weights), "node", 0, 0, tiled=True)
 
-    here, there = back_rows(hot, parts.reshape(n_rest, n_own, part))
+    here, there = back_rows(hot_here, hot_there, parts.reshape(n_rest, n_own, part))
     back = total([here, lax.ppermute(there, "grp", other)])
     back = swap(back, "grp", along_z).reshape(n_z, SPLIT * n_tok, part)
     return unpack(back, n_tok)

time: 197 us -> 195 us (0.990)
  blocking collectives: 122 us -> 148 us
  waiting for transfers between devices: 21.8 us -> 4.74 us
  Pallas kernels: 22.2 us -> 16.2 us
  starting transfers between devices: 29.8 us -> 25.4 us
    all_to_all x0 -> x1, blocking collectives: none -> 34.7 us  [local(): rows = lax.all_to_all(rows, 'node', 0, 0, tiled=True)]
    all_to_all x1 -> x0, waiting for transfers between devices: 18.1 us -> none  [local(): rows = lax.all_to_all(rows, 'node', 0, 0, tiled=True)]
    all_to_all x3 -> x2, blocking collectives: 59 us -> 48 us  [swap(): return lax.all_to_all(a, axis, 0, 0, axis_index_groups=members, tiled=True)]
    all_to_all x1 -> x0, starting transfers between devices: 9.24 us -> none  [local(): rows = lax.all_to_all(rows, 'node', 0, 0, tiled=True)]
    all_to_all x1 -> x2, starting transfers between devices: 16.7 us -> 21.6 us  [swap(): return lax.all_to_all(a, axis, 0, 0, axis_index_groups=members, tiled=True)]
    pallas_call x1, Pallas kernels: 7.55 us -> 4.96 us  [forward(): call(forward_body, jax.ShapeDtypeStruct((2 * n_hid, n_slot), f32), (4 * n...]
    pallas_call x3 -> x4, Pallas kernels: 9.23 us -> 6.79 us  [the longest x2 3.41 us: select(): call(functools.partial(select_body, n_tok, per_node, n_pick), ((pltpu.HBM...]
  transfers between devices with their start and end apart: 4 -> 4, of which waited for: 3 -> 3; matrix products, arithmetic and copies ran while one was open for 0% -> 0% of each run, Pallas kernels for 5% -> 4%
where the time goes in v4:
time: 195 us; the launch traced here: 194 us
  blocking collectives  148 us (76%)
  starting transfers between devices  25.4 us (13%)
  Pallas kernels  16.2 us (8%)
  waiting for transfers between devices  4.74 us (2%)
    all_to_all x2, blocking collectives, swap(): return lax.all_to_all(a, axis, 0, 0, axis_index_groups=members, tiled=True)  48 us
    all_to_all x1, blocking collectives, local(): rows = lax.all_to_all(rows, 'node', 0, 0, tiled=True)  34.7 us
    all_gather x1, blocking collectives, local(): lax.all_gather(payload, 'grp', axis=0, axis_index_groups=along_z, tiled=T...  34.7 us
    all_to_all x1, blocking collectives, local(): parts = lax.all_to_all(slot_part(grads, weights), 'node', 0, 0, tiled=True)  30 us
    all_to_all x2, starting transfers between devices, swap(): return lax.all_to_all(a, axis, 0, 0, axis_index_groups=members, tiled=True)  21.6 us
    pallas_call x1, Pallas kernels, forward(): call(forward_body, jax.ShapeDtypeStruct((2 * n_hid, n_slot), f32), (4 * n...  4.96 us
  transfers between devices with their start and end apart: 4, of which 3 were waited for; matrix products, arithmetic and copies ran while one was open for 0% of the time, Pallas kernels for 4%

profile of v4, /device:TPU:2, one launch (start us, length us, event | category | flops | bytes accessed | tf_op | source)
XLA Modules:
  0.0 194.1 jit_solution(10952620261876630797)
XLA Ops:
  0.0 0.0 copy-start.2
  0.0 0.0 copy-start.3
  0.0 0.0 copy-start.4
  0.0 0.0 copy-start.5
  0.0 2.9 %shard_map.83 = bf16[8,192,896]{2,1,0:T(8,128)(2,1)} custom-call(bf16[64,7168]{1,0:T(8,128)(2,1)} %bitcast.20, bf16[64,7168]{1,0:T(8,128)(2,1)} %bitcast.22, bf16[64,7168]{1,0:T(8,128)(2,1)} %bitcast.27), custom_call_target="tpu_custom_call" | custom-call | bytes 5505024 | tf_op jit(solution)/shard_map/pallas_call | solution.py:103
  3.0 0.0 copy-done.2
  3.0 0.0 copy-done.3
  3.0 0.0 copy-done.4
  3.0 0.0 copy-done.5
  3.0 0.1 shard_map.82
  3.1 16.7 %all-to-all-start = ((bf16[8,192,896]{2,1,0:T(8,128)(2,1)}), bf16[8,192,896]{2,1,0:T(8,128)(2,1)S(1)}, u32[]{:S(2)}, u32[]{:S(2)}) async-start(bf16[8,192,896]{2,1,0:T(8,128)(2,1)} %shard_map.83), calls=%async_computation | async-start | bytes 5505024 | tf_op jit(solution)/shard_map/all_to_all | solution.py:35
  19.8 34.7 %all_gather.3.tok_ref = bf16[256,1024]{1,0:T(8,128)(2,1)S(1)} all-gather(bf16[16,1024]{1,0:T(8,128)(2,1)S(1)} %shard_map.82), channel_id=1, replica_groups={{0,64,128,192,256,320,384,448,512,576,640,704,768,832,896,960},{32,96,1..., dimensions={0}, use_global_device_ids=true | all-gather | bytes 557056 | tf_op jit(solution)/shard_map/all_gather | solution.py:309
  54.6 1.9 collective-permute-start
  56.5 1.0 shard_map.84
  57.5 1.0 collective-permute-done.tok_ref
  58.5 2.4 %shard_map.85 = (bf16[512,896]{1,0:T(8,128)(2,1)}, bf16[256,128]{1,0:T(8,128)(2,1)}) custom-call(s32[1]{0:T(128)} %bitcast.expert_ref, bf16[256,1024]{1,0:T(8,128)(2,1)} %collective-permute-done.tok_ref, bf16[128,896]{1,0:T(8,128)(2,1)S(1)} %get-tuple-element.19.refs_0_), custom_call_target="tpu_custom_call" | custom-call | flops 58720256 | bytes 524288 | tf_op jit(solution)/shard_map/pallas_call | solution.py:171
  60.9 0.0 all-to-all-done.w_ref
  60.9 34.7 %all_to_all.49 = bf16[32,16,896]{2,1,0:T(8,128)(2,1)S(1)} all-to-all(bf16[32,16,896]{2,1,0:T(8,128)(2,1)} %bitcast.26), channel_id=1, replica_groups=mesh['grp'=32,'node'=32] {'node'}, dimensions={0} | all-to-all | bytes 1835008 | tf_op jit(solution)/shard_map/all_to_all | solution.py:315
  95.7 1.7 shard_map.86
  97.4 4.8 %all-to-all-start.2 = ((bf16[8,64,512]{2,1,0:T(8,128)(2,1)}), bf16[8,64,512]{2,1,0:T(8,128)(2,1)S(1)}, u32[]{:S(2)}, u32[]{:S(2)}) async-start(bf16[8,64,512]{2,1,0:T(8,128)(2,1)} %bitcast.24), calls=%async_computation.2 | async-start | bytes 1048576 | tf_op jit(solution)/shard_map/all_to_all | solution.py:35
  102.2 5.0 %shard_map.87.coef_ref = f32[128,512]{1,0:T(8,128)S(1)} custom-call(bf16[512,7168]{1,0:T(8,128)(2,1)} %bitcast.19, bf16[64,7168]{1,0:T(8,128)(2,1)} %bitcast.21, bf16[64,7168]{1,0:T(8,128)(2,1)} %bitcast.23), custom_call_target="tpu_custom_call" | custom-call | flops 939524096 | bytes 9175040 | tf_op jit(solution)/shard_map/pallas_call | solution.py:134
  107.2 1.9 all-to-all-done.2.parts_ref
  109.1 0.2 shard_map.88
  109.4 17.4 %all_to_all.50.grads_ref = bf16[8,512,128]{2,1,0:T(8,128)(2,1)S(1)} all-to-all(bf16[8,512,128]{2,1,0:T(8,128)(2,1)S(1)} %shard_map.88), channel_id=1, replica_groups={{0,1,2,3,4,5,6,7},{8,9,10,11,12,13,14,15},{16,17,18,19,20,21,22,23},{24..., dimensions={0} | all-to-all | bytes 2097152 | tf_op jit(solution)/shard_map/all_to_all | solution.py:35
  126.7 0.0 copy-start
  126.7 0.0 copy-start.1
  126.7 1.7 shard_map.89
  128.4 30.0 %all_to_all.51 = bf16[32,16,896]{2,1,0:T(8,128)(2,1)S(1)} all-to-all(bf16[32,16,896]{2,1,0:T(8,128)(2,1)S(1)} %bitcast.16), channel_id=1, replica_groups=mesh['grp'=32,'node'=32] {'node'}, dimensions={0} | all-to-all | bytes 1835008 | tf_op jit(solution)/shard_map/all_to_all | solution.py:322
  158.4 0.0 copy-done
  158.4 0.0 copy-done.1
  158.4 0.4 shard_map.90
  158.9 1.9 collective-permute-start.1
  160.8 1.8 collective-permute-done.1
  162.6 0.1 add_convert_fusion
  162.7 30.7 %all_to_all.52.parts_ref = bf16[16,16,896]{2,1,0:T(8,128)(2,1)S(1)} all-to-all(bf16[16,16,896]{2,1,0:T(8,128)(2,1)S(1)} %bitcast.25), channel_id=1, replica_groups={{0,64,128,192,256,320,384,448,512,576,640,704,768,832,896,960},{32,96,1..., dimensions={0} | all-to-all | bytes 917504 | tf_op jit(solution)/shard_map/all_to_all | solution.py:35
  193.4 0.7 shard_map.91
Async XLA Ops:
  0.0 3.0 %copy-start.2 = (bf16[2,7168]{1,0:T(2,128)(2,1)S(1)}, bf16[2,7168]{1,0:T(2,128)(2,1)}, u32[]{:S(2)}) copy-start(bf16[2,7168]{1,0:T(2,128)(2,1)} %grad_ref.1) | copy-start | bytes 86020
  0.0 3.0 %copy-start.3 = (s32[2,8]{1,0:T(2,128)S(1)}, s32[2,8]{1,0:T(2,128)}, u32[]{:S(2)}) copy-start(s32[2,8]{1,0:T(2,128)} %ids_ref.1) | copy-start | bytes 196
  0.0 3.0 %copy-start.4 = (s32[2,8]{1,0:T(2,128)S(1)}, s32[2,8]{1,0:T(2,128)}, u32[]{:S(2)}) copy-start(s32[2,8]{1,0:T(2,128)} %slots_ref.1) | copy-start | bytes 196
  0.0 3.0 %copy-start.5 = (s32[2,8]{1,0:T(2,128)S(1)}, s32[2,8]{1,0:T(2,128)}, u32[]{:S(2)}) copy-start(s32[2,8]{1,0:T(2,128)} %gates_ref.1) | copy-start | bytes 196
  3.1 57.8 %all-to-all-start = ((bf16[8,192,896]{2,1,0:T(8,128)(2,1)}), bf16[8,192,896]{2,1,0:T(8,128)(2,1)S(1)}, u32[]{:S(2)}, u32[]{:S(2)}) async-start(bf16[8,192,896]{2,1,0:T(8,128)(2,1)} %shard_map.83), calls=%async_computation | async-start | bytes 5505024 | tf_op jit(solution)/shard_map/all_to_all | solution.py:35
  54.6 3.9 %collective-permute-start = (bf16[256,1024]{1,0:T(8,128)(2,1)S(1)}, bf16[256,1024]{1,0:T(8,128)(2,1)}, u32[]{:S(2)}, u32[]{:S(2)}) collective-permute-start(bf16[256,1024]{1,0:T(8,128)(2,1)S(1)} %all_gather.3.tok_ref), channel_id=1, source_target_pairs={{0,32},{32,0},{64,96},{96,64},{128,160},{160,128},{192,224},{224,1... | collective-permute-start | bytes 1572872 | tf_op jit(solution)/shard_map/ppermute | solution.py:310
  97.4 11.7 %all-to-all-start.2 = ((bf16[8,64,512]{2,1,0:T(8,128)(2,1)}), bf16[8,64,512]{2,1,0:T(8,128)(2,1)S(1)}, u32[]{:S(2)}, u32[]{:S(2)}) async-start(bf16[8,64,512]{2,1,0:T(8,128)(2,1)} %bitcast.24), calls=%async_computation.2 | async-start | bytes 1048576 | tf_op jit(solution)/shard_map/all_to_all | solution.py:35
  126.7 31.7 %copy-start = (bf16[256,128]{1,0:T(8,128)(2,1)S(1)}, bf16[256,128]{1,0:T(8,128)(2,1)}, u32[]{:S(2)}) copy-start(bf16[256,128]{1,0:T(8,128)(2,1)} %get-tuple-element.18.hot_here_ref) | copy-start | bytes 196612
  126.7 31.7 %copy-start.1 = (bf16[256,128]{1,0:T(8,128)(2,1)S(1)}, bf16[256,128]{1,0:T(8,128)(2,1)}, u32[]{:S(2)}) copy-start(bf16[256,128]{1,0:T(8,128)(2,1)} %get-tuple-element.20.hot_there_ref) | copy-start | bytes 196612
  158.9 3.7 %collective-permute-start.1 = (bf16[256,896]{1,0:T(8,128)(2,1)S(1)}, bf16[256,896]{1,0:T(8,128)(2,1)S(1)}, u32[]{:S(2)}, u32[]{:S(2)}) collective-permute-start(bf16[256,896]{1,0:T(8,128)(2,1)S(1)} %get-tuple-element.28), channel_id=1, source_target_pairs={{0,32},{32,0},{64,96},{96,64},{128,160},{160,128},{192,224},{224,1... | collective-permute-start | bytes 1376264 | tf_op jit(solution)/shard_map/ppermute | solution.py:325

commit v5 on v4

--- a/solution.py
+++ b/solution.py
@@ -171,7 +171,7 @@
     return call(
         functools.partial(select_body, n_tok, per_node, n_pick),
         (
-            (pltpu.HBM if before else jax.ShapeDtypeStruct)((copies * n_own, part), bf16),
+            jax.ShapeDtypeStruct((copies * n_own, part), bf16),
             pltpu.HBM((n_all, n_own), bf16),
         ),
         (2 * n_all * n_own * part, 2 * n_all * wide),
@@ -289,7 +289,9 @@
     my_expert, my_node = lax.axis_index("grp"), lax.axis_index("node")
     n_rest, n_z = n_node // SPLIT, n_grp // C_DEV
     block = [[h * SPLIT + d for d in range(SPLIT)] for h in range(n_rest)]
-    along_z = [[z * C_DEV + c for z in range(n_z)] for c in range(C_DEV)]
+    along_z = [
+        [z * C_DEV + (c + z // 2) % C_DEV for z in range(n_z)] for c in range(C_DEV)
+    ]
     other = [(z * C_DEV + c, z * C_DEV + 1 - c) for z in range(n_z) for c in range(C_DEV)]
     n_tok, width = out_grad.shape
     part = width // SPLIT
@@ -307,11 +309,10 @@
     weights = swap(weights, "node", block)
 
     here = lax.all_gather(payload, "grp", axis=0, axis_index_groups=along_z, tiled=True)
-    there = lax.ppermute(here, "grp", other)
+    there, weights = lax.optimization_barrier((lax.ppermute(here, "grp", other), weights))
     expert = my_expert.astype(jnp.int32).reshape(1)
     rows, hot_here = select(expert, here, (), 1, n_tok, per_node, n_pick)
     rows, hot_there = select(expert, there, (rows,), n_rest, n_tok, per_node, n_pick)
-    rows, weights = lax.optimization_barrier((rows, weights))
     rows = lax.all_to_all(rows, "node", 0, 0, tiled=True)
 
     gate, rows = lax.optimization_barrier((gate, rows))

time: 195 us -> 192 us (0.985)
  blocking collectives: 148 us -> 144 us
    all_gather x1, blocking collectives: 34.7 us -> 30.2 us  [local(): lax.all_gather(payload, 'grp', axis=0, axis_index_groups=along_z, tiled=T...]
    all_to_all x2, blocking collectives: 48 us -> 50.2 us  [swap(): return lax.all_to_all(a, axis, 0, 0, axis_index_groups=members, tiled=True)]
  transfers between devices with their start and end apart: 4 -> 4, of which waited for: 3 -> 3; matrix products, arithmetic and copies ran while one was open for 0% -> 0% of each run, Pallas kernels for 4% -> 3%
where the time goes in v5:
time: 192 us
  blocking collectives  144 us (75%)
  starting transfers between devices  26.3 us (14%)
  Pallas kernels  15.8 us (8%)
  waiting for transfers between devices  4.86 us (3%)
    all_to_all x2, blocking collectives, swap(): return lax.all_to_all(a, axis, 0, 0, axis_index_groups=members, tiled=True)  50.2 us
    all_to_all x1, blocking collectives, local(): rows = lax.all_to_all(rows, 'node', 0, 0, tiled=True)  35 us
    all_gather x1, blocking collectives, local(): lax.all_gather(payload, 'grp', axis=0, axis_index_groups=along_z, tiled=T...  30.2 us
    all_to_all x1, blocking collectives, local(): parts = lax.all_to_all(slot_part(grads, weights), 'node', 0, 0, tiled=True)  28.9 us
    all_to_all x2, starting transfers between devices, swap(): return lax.all_to_all(a, axis, 0, 0, axis_index_groups=members, tiled=True)  21.6 us
    pallas_call x1, Pallas kernels, forward(): call(forward_body, jax.ShapeDtypeStruct((2 * n_hid, n_slot), f32), (4 * n...  4.96 us
  transfers between devices with their start and end apart: 4, of which 3 were waited for; matrix products, arithmetic and copies ran while one was open for 0% of the time, Pallas kernels for 3%

profile of v5, /device:TPU:2, one launch (start us, length us, event | category | flops | bytes accessed | tf_op | source)
XLA Modules:
  0.0 191.6 jit_solution(3888109348481675368)
XLA Ops:
  0.0 0.0 copy-start.2
  0.0 0.0 copy-start.3
  0.0 0.0 copy-start.4
  0.0 0.0 copy-start.5
  0.0 2.9 %shard_map.83 = bf16[8,192,896]{2,1,0:T(8,128)(2,1)} custom-call(bf16[64,7168]{1,0:T(8,128)(2,1)} %bitcast.21, bf16[64,7168]{1,0:T(8,128)(2,1)} %bitcast.23, bf16[64,7168]{1,0:T(8,128)(2,1)} %bitcast.27), custom_call_target="tpu_custom_call" | custom-call | bytes 5505024 | tf_op jit(solution)/shard_map/pallas_call | solution.py:103
  3.0 0.0 copy-done.2
  3.0 0.0 copy-done.3
  3.0 0.0 copy-done.4
  3.0 0.0 copy-done.5
  3.0 0.1 shard_map.82
  3.1 16.7 %all-to-all-start = ((bf16[8,192,896]{2,1,0:T(8,128)(2,1)}), bf16[8,192,896]{2,1,0:T(8,128)(2,1)S(1)}, u32[]{:S(2)}, u32[]{:S(2)}) async-start(bf16[8,192,896]{2,1,0:T(8,128)(2,1)} %shard_map.83), calls=%async_computation | async-start | bytes 5505024 | tf_op jit(solution)/shard_map/all_to_all | solution.py:35
  19.8 30.2 %all_gather.3.tok_ref = bf16[256,1024]{1,0:T(8,128)(2,1)S(1)} all-gather(bf16[16,1024]{1,0:T(8,128)(2,1)S(1)} %shard_map.82), channel_id=1, replica_groups={{0,64,160,224,256,320,416,480,512,576,672,736,768,832,928,992},{32,96,1..., dimensions={0}, use_global_device_ids=true | all-gather | bytes 557056 | tf_op jit(solution)/shard_map/all_gather | solution.py:311
  50.1 2.9 %collective-permute-start = (bf16[256,1024]{1,0:T(8,128)(2,1)S(1)}, bf16[256,1024]{1,0:T(8,128)(2,1)}, u32[]{:S(2)}, u32[]{:S(2)}) collective-permute-start(bf16[256,1024]{1,0:T(8,128)(2,1)S(1)} %all_gather.3.tok_ref), channel_id=1, source_target_pairs={{0,32},{32,0},{64,96},{96,64},{128,160},{160,128},{192,224},{224,1... | collective-permute-start | bytes 1572872 | tf_op jit(solution)/shard_map/ppermute | solution.py:312
  52.9 1.0 shard_map.84
  53.9 0.7 collective-permute-done.tok_ref
  54.6 0.0 all-to-all-done.w_ref
  54.6 2.0 %shard_map.85 = (bf16[512,896]{1,0:T(8,128)(2,1)S(1)}, bf16[256,128]{1,0:T(8,128)(2,1)}) custom-call(s32[1]{0:T(128)} %bitcast.expert_ref, bf16[256,1024]{1,0:T(8,128)(2,1)} %collective-permute-done.tok_ref, bf16[128,896]{1,0:T(8,128)(2,1)S(1)} %get-tuple-element.21.refs_0_), custom_call_target="tpu_custom_call" | custom-call | flops 58720256 | bytes 524288 | tf_op jit(solution)/shard_map/pallas_call | solution.py:171
  56.6 35.0 %all_to_all.49 = bf16[32,16,896]{2,1,0:T(8,128)(2,1)S(1)} all-to-all(bf16[32,16,896]{2,1,0:T(8,128)(2,1)S(1)} %bitcast.19), channel_id=1, replica_groups=mesh['grp'=32,'node'=32] {'node'}, dimensions={0} | all-to-all | bytes 1835008 | tf_op jit(solution)/shard_map/all_to_all | solution.py:316
  91.6 1.7 shard_map.86
  93.4 4.8 %all-to-all-start.2 = ((bf16[8,64,512]{2,1,0:T(8,128)(2,1)}), bf16[8,64,512]{2,1,0:T(8,128)(2,1)S(1)}, u32[]{:S(2)}, u32[]{:S(2)}) async-start(bf16[8,64,512]{2,1,0:T(8,128)(2,1)} %bitcast.25), calls=%async_computation.2 | async-start | bytes 1048576 | tf_op jit(solution)/shard_map/all_to_all | solution.py:35
  98.2 5.0 %shard_map.87.coef_ref = f32[128,512]{1,0:T(8,128)S(1)} custom-call(bf16[512,7168]{1,0:T(8,128)(2,1)} %bitcast.20, bf16[64,7168]{1,0:T(8,128)(2,1)} %bitcast.22, bf16[64,7168]{1,0:T(8,128)(2,1)} %bitcast.24), custom_call_target="tpu_custom_call" | custom-call | flops 939524096 | bytes 9175040 | tf_op jit(solution)/shard_map/pallas_call | solution.py:134
  103.2 2.4 %all-to-all-done.2.parts_ref = bf16[8,64,512]{2,1,0:T(8,128)(2,1)S(1)} async-done(((bf16[8,64,512]{2,1,0:T(8,128)(2,1)}), bf16[8,64,512]{2,1,0:T(8,128)(2,1)S(1)}, u32[]{:S(2)}, u32[]{:S(2)}) %all-to-all-start.2) | async-done | bytes 524320 | tf_op jit(solution)/shard_map/all_to_all | solution.py:35
  105.6 0.2 shard_map.88
  105.8 17.9 %all_to_all.50.grads_ref = bf16[8,512,128]{2,1,0:T(8,128)(2,1)S(1)} all-to-all(bf16[8,512,128]{2,1,0:T(8,128)(2,1)S(1)} %shard_map.88), channel_id=1, replica_groups={{0,1,2,3,4,5,6,7},{8,9,10,11,12,13,14,15},{16,17,18,19,20,21,22,23},{24..., dimensions={0} | all-to-all | bytes 2097152 | tf_op jit(solution)/shard_map/all_to_all | solution.py:35
  123.7 0.0 copy-start
  123.7 0.0 copy-start.1
  123.7 1.7 shard_map.89
  125.4 28.9 %all_to_all.51 = bf16[32,16,896]{2,1,0:T(8,128)(2,1)S(1)} all-to-all(bf16[32,16,896]{2,1,0:T(8,128)(2,1)S(1)} %bitcast.16), channel_id=1, replica_groups=mesh['grp'=32,'node'=32] {'node'}, dimensions={0} | all-to-all | bytes 1835008 | tf_op jit(solution)/shard_map/all_to_all | solution.py:323
  154.3 0.0 copy-done
  154.3 0.0 copy-done.1
  154.3 0.4 shard_map.90
  154.7 1.9 %collective-permute-start.1 = (bf16[256,896]{1,0:T(8,128)(2,1)S(1)}, bf16[256,896]{1,0:T(8,128)(2,1)S(1)}, u32[]{:S(2)}, u32[]{:S(2)}) collective-permute-start(bf16[256,896]{1,0:T(8,128)(2,1)S(1)} %get-tuple-element.28), channel_id=1, source_target_pairs={{0,32},{32,0},{64,96},{96,64},{128,160},{160,128},{192,224},{224,1... | collective-permute-start | bytes 1376264 | tf_op jit(solution)/shard_map/ppermute | solution.py:326
  156.7 1.8 collective-permute-done.1
  158.4 0.1 add_convert_fusion
  158.6 32.3 %all_to_all.52.parts_ref = bf16[16,16,896]{2,1,0:T(8,128)(2,1)S(1)} all-to-all(bf16[16,16,896]{2,1,0:T(8,128)(2,1)S(1)} %bitcast.26), channel_id=1, replica_groups={{0,64,160,224,256,320,416,480,512,576,672,736,768,832,928,992},{32,96,1..., dimensions={0} | all-to-all | bytes 917504 | tf_op jit(solution)/shard_map/all_to_all | solution.py:35
  190.9 0.7 shard_map.91
Async XLA Ops:
  0.0 3.0 %copy-start.2 = (bf16[2,7168]{1,0:T(2,128)(2,1)S(1)}, bf16[2,7168]{1,0:T(2,128)(2,1)}, u32[]{:S(2)}) copy-start(bf16[2,7168]{1,0:T(2,128)(2,1)} %grad_ref.1) | copy-start | bytes 86020
  0.0 3.0 %copy-start.3 = (s32[2,8]{1,0:T(2,128)S(1)}, s32[2,8]{1,0:T(2,128)}, u32[]{:S(2)}) copy-start(s32[2,8]{1,0:T(2,128)} %ids_ref.1) | copy-start | bytes 196
  0.0 3.0 %copy-start.4 = (s32[2,8]{1,0:T(2,128)S(1)}, s32[2,8]{1,0:T(2,128)}, u32[]{:S(2)}) copy-start(s32[2,8]{1,0:T(2,128)} %slots_ref.1) | copy-start | bytes 196
  0.0 3.0 %copy-start.5 = (s32[2,8]{1,0:T(2,128)S(1)}, s32[2,8]{1,0:T(2,128)}, u32[]{:S(2)}) copy-start(s32[2,8]{1,0:T(2,128)} %gates_ref.1) | copy-start | bytes 196
  3.1 51.5 %all-to-all-start = ((bf16[8,192,896]{2,1,0:T(8,128)(2,1)}), bf16[8,192,896]{2,1,0:T(8,128)(2,1)S(1)}, u32[]{:S(2)}, u32[]{:S(2)}) async-start(bf16[8,192,896]{2,1,0:T(8,128)(2,1)} %shard_map.83), calls=%async_computation | async-start | bytes 5505024 | tf_op jit(solution)/shard_map/all_to_all | solution.py:35
  50.1 4.5 %collective-permute-start = (bf16[256,1024]{1,0:T(8,128)(2,1)S(1)}, bf16[256,1024]{1,0:T(8,128)(2,1)}, u32[]{:S(2)}, u32[]{:S(2)}) collective-permute-start(bf16[256,1024]{1,0:T(8,128)(2,1)S(1)} %all_gather.3.tok_ref), channel_id=1, source_target_pairs={{0,32},{32,0},{64,96},{96,64},{128,160},{160,128},{192,224},{224,1... | collective-permute-start | bytes 1572872 | tf_op jit(solution)/shard_map/ppermute | solution.py:312
  93.4 12.2 %all-to-all-start.2 = ((bf16[8,64,512]{2,1,0:T(8,128)(2,1)}), bf16[8,64,512]{2,1,0:T(8,128)(2,1)S(1)}, u32[]{:S(2)}, u32[]{:S(2)}) async-start(bf16[8,64,512]{2,1,0:T(8,128)(2,1)} %bitcast.25), calls=%async_computation.2 | async-start | bytes 1048576 | tf_op jit(solution)/shard_map/all_to_all | solution.py:35
  123.7 30.6 %copy-start = (bf16[256,128]{1,0:T(8,128)(2,1)S(1)}, bf16[256,128]{1,0:T(8,128)(2,1)}, u32[]{:S(2)}) copy-start(bf16[256,128]{1,0:T(8,128)(2,1)} %get-tuple-element.18.hot_here_ref) | copy-start | bytes 196612
  123.7 30.6 %copy-start.1 = (bf16[256,128]{1,0:T(8,128)(2,1)S(1)}, bf16[256,128]{1,0:T(8,128)(2,1)}, u32[]{:S(2)}) copy-start(bf16[256,128]{1,0:T(8,128)(2,1)} %get-tuple-element.22.hot_there_ref) | copy-start | bytes 196612
  154.7 3.7 %collective-permute-start.1 = (bf16[256,896]{1,0:T(8,128)(2,1)S(1)}, bf16[256,896]{1,0:T(8,128)(2,1)S(1)}, u32[]{:S(2)}, u32[]{:S(2)}) collective-permute-start(bf16[256,896]{1,0:T(8,128)(2,1)S(1)} %get-tuple-element.28), channel_id=1, source_target_pairs={{0,32},{32,0},{64,96},{96,64},{128,160},{160,128},{192,224},{224,1... | collective-permute-start | bytes 1376264 | tf_op jit(solution)/shard_map/ppermute | solution.py:326

commit v6 on v4

--- a/solution.py
+++ b/solution.py
@@ -196,17 +196,16 @@
     n, h3, part = weights.shape
     h = h3 // 3
     n_slot = rows.shape[0]
-    half = n_slot // 2
     return call(
         hidden_body,
         pltpu.HBM((n * h, n_slot), bf16),
         (2 * n * h * n_slot * part, 2 * (n * h + n_slot) * part),
-        grid=(2,),
+        grid=(1,),
         in_specs=[
             pl.BlockSpec((n, h, part), lambda i: (0, 2, 0)),
-            pl.BlockSpec((half, part), lambda i: (i, 0)),
+            pl.BlockSpec((n_slot, part), lambda i: (0, 0)),
         ],
-        out_specs=pl.BlockSpec((n * h, half), lambda i: (0, i)),
+        out_specs=pl.BlockSpec((n * h, n_slot), lambda i: (0, 0)),
     )(weights, rows)
 
 
@@ -289,7 +288,9 @@
     my_expert, my_node = lax.axis_index("grp"), lax.axis_index("node")
     n_rest, n_z = n_node // SPLIT, n_grp // C_DEV
     block = [[h * SPLIT + d for d in range(SPLIT)] for h in range(n_rest)]
-    along_z = [[z * C_DEV + c for z in range(n_z)] for c in range(C_DEV)]
+    along_z = [
+        [z * C_DEV + (c + z // 2) % C_DEV for z in range(n_z)] for c in range(C_DEV)
+    ]
     other = [(z * C_DEV + c, z * C_DEV + 1 - c) for z in range(n_z) for c in range(C_DEV)]
     n_tok, width = out_grad.shape
     part = width // SPLIT

time: 195 us -> 193 us (0.990)
  blocking collectives: 148 us -> 145 us
    all_gather x1, blocking collectives: 34.7 us -> 30.2 us  [local(): lax.all_gather(payload, 'grp', axis=0, axis_index_groups=along_z, tiled=T...]
    all_to_all x2, blocking collectives: 48 us -> 50.2 us  [swap(): return lax.all_to_all(a, axis, 0, 0, axis_index_groups=members, tiled=True)]
where the time goes in v6:
time: 193 us; the launch traced here: 192 us
  blocking collectives  145 us (75%)
  starting transfers between devices  26.3 us (14%)
  Pallas kernels  16 us (8%)
  waiting for transfers between devices  4.87 us (3%)
    all_to_all x2, blocking collectives, swap(): return lax.all_to_all(a, axis, 0, 0, axis_index_groups=members, tiled=True)  50.2 us
    all_to_all x1, blocking collectives, local(): rows = lax.all_to_all(rows, 'node', 0, 0, tiled=True)  35.2 us
    all_gather x1, blocking collectives, local(): lax.all_gather(payload, 'grp', axis=0, axis_index_groups=along_z, tiled=T...  30.2 us
    all_to_all x1, blocking collectives, local(): parts = lax.all_to_all(slot_part(grads, weights), 'node', 0, 0, tiled=True)  28.9 us
    all_to_all x2, starting transfers between devices, swap(): return lax.all_to_all(a, axis, 0, 0, axis_index_groups=members, tiled=True)  21.6 us
    pallas_call x1, Pallas kernels, forward(): call(forward_body, jax.ShapeDtypeStruct((2 * n_hid, n_slot), f32), (4 * n...  4.96 us
  transfers between devices with their start and end apart: 4, of which 3 were waited for; matrix products, arithmetic and copies ran while one was open for 0% of the time, Pallas kernels for 4%

profile of v6, /device:TPU:2, one launch (start us, length us, event | category | flops | bytes accessed | tf_op | source)
XLA Modules:
  0.0 192.0 jit_solution(13162114981449295634)
XLA Ops:
  0.0 0.0 copy-start.2
  0.0 0.0 copy-start.3
  0.0 0.0 copy-start.4
  0.0 0.0 copy-start.5
  0.0 2.9 %shard_map.83 = bf16[8,192,896]{2,1,0:T(8,128)(2,1)} custom-call(bf16[64,7168]{1,0:T(8,128)(2,1)} %bitcast.20, bf16[64,7168]{1,0:T(8,128)(2,1)} %bitcast.22, bf16[64,7168]{1,0:T(8,128)(2,1)} %bitcast.27), custom_call_target="tpu_custom_call" | custom-call | bytes 5505024 | tf_op jit(solution)/shard_map/pallas_call | solution.py:103
  3.0 0.0 copy-done.2
  3.0 0.0 copy-done.3
  3.0 0.0 copy-done.4
  3.0 0.0 copy-done.5
  3.0 0.1 shard_map.82
  3.1 16.7 %all-to-all-start = ((bf16[8,192,896]{2,1,0:T(8,128)(2,1)}), bf16[8,192,896]{2,1,0:T(8,128)(2,1)S(1)}, u32[]{:S(2)}, u32[]{:S(2)}) async-start(bf16[8,192,896]{2,1,0:T(8,128)(2,1)} %shard_map.83), calls=%async_computation | async-start | bytes 5505024 | tf_op jit(solution)/shard_map/all_to_all | solution.py:35
  19.8 30.2 %all_gather.3.tok_ref = bf16[256,1024]{1,0:T(8,128)(2,1)S(1)} all-gather(bf16[16,1024]{1,0:T(8,128)(2,1)S(1)} %shard_map.82), channel_id=1, replica_groups={{0,64,160,224,256,320,416,480,512,576,672,736,768,832,928,992},{32,96,1..., dimensions={0}, use_global_device_ids=true | all-gather | bytes 557056 | tf_op jit(solution)/shard_map/all_gather | solution.py:310
  50.1 2.9 %collective-permute-start = (bf16[256,1024]{1,0:T(8,128)(2,1)S(1)}, bf16[256,1024]{1,0:T(8,128)(2,1)}, u32[]{:S(2)}, u32[]{:S(2)}) collective-permute-start(bf16[256,1024]{1,0:T(8,128)(2,1)S(1)} %all_gather.3.tok_ref), channel_id=1, source_target_pairs={{0,32},{32,0},{64,96},{96,64},{128,160},{160,128},{192,224},{224,1... | collective-permute-start | bytes 1572872 | tf_op jit(solution)/shard_map/ppermute | solution.py:311
  52.9 1.0 shard_map.84
  53.9 0.7 collective-permute-done.tok_ref
  54.6 2.4 %shard_map.85 = (bf16[512,896]{1,0:T(8,128)(2,1)}, bf16[256,128]{1,0:T(8,128)(2,1)}) custom-call(s32[1]{0:T(128)} %bitcast.expert_ref, bf16[256,1024]{1,0:T(8,128)(2,1)} %collective-permute-done.tok_ref, bf16[128,896]{1,0:T(8,128)(2,1)S(1)} %get-tuple-element.19.refs_0_), custom_call_target="tpu_custom_call" | custom-call | flops 58720256 | bytes 524288 | tf_op jit(solution)/shard_map/pallas_call | solution.py:171
  57.0 0.0 all-to-all-done.w_ref
  57.0 35.2 %all_to_all.49 = bf16[32,16,896]{2,1,0:T(8,128)(2,1)S(1)} all-to-all(bf16[32,16,896]{2,1,0:T(8,128)(2,1)} %bitcast.26), channel_id=1, replica_groups=mesh['grp'=32,'node'=32] {'node'}, dimensions={0} | all-to-all | bytes 1835008 | tf_op jit(solution)/shard_map/all_to_all | solution.py:316
  92.3 1.5 shard_map.86
  93.8 4.8 %all-to-all-start.2 = ((bf16[8,64,512]{2,1,0:T(8,128)(2,1)}), bf16[8,64,512]{2,1,0:T(8,128)(2,1)S(1)}, u32[]{:S(2)}, u32[]{:S(2)}) async-start(bf16[8,64,512]{2,1,0:T(8,128)(2,1)} %bitcast.24), calls=%async_computation.2 | async-start | bytes 1048576 | tf_op jit(solution)/shard_map/all_to_all | solution.py:35
  98.6 5.0 %shard_map.87.coef_ref = f32[128,512]{1,0:T(8,128)S(1)} custom-call(bf16[512,7168]{1,0:T(8,128)(2,1)} %bitcast.19, bf16[64,7168]{1,0:T(8,128)(2,1)} %bitcast.21, bf16[64,7168]{1,0:T(8,128)(2,1)} %bitcast.23), custom_call_target="tpu_custom_call" | custom-call | flops 939524096 | bytes 9175040 | tf_op jit(solution)/shard_map/pallas_call | solution.py:134
  103.6 2.4 %all-to-all-done.2.parts_ref = bf16[8,64,512]{2,1,0:T(8,128)(2,1)S(1)} async-done(((bf16[8,64,512]{2,1,0:T(8,128)(2,1)}), bf16[8,64,512]{2,1,0:T(8,128)(2,1)S(1)}, u32[]{:S(2)}, u32[]{:S(2)}) %all-to-all-start.2) | async-done | bytes 524320 | tf_op jit(solution)/shard_map/all_to_all | solution.py:35
  106.0 0.2 shard_map.88
  106.3 17.9 %all_to_all.50.grads_ref = bf16[8,512,128]{2,1,0:T(8,128)(2,1)S(1)} all-to-all(bf16[8,512,128]{2,1,0:T(8,128)(2,1)S(1)} %shard_map.88), channel_id=1, replica_groups={{0,1,2,3,4,5,6,7},{8,9,10,11,12,13,14,15},{16,17,18,19,20,21,22,23},{24..., dimensions={0} | all-to-all | bytes 2097152 | tf_op jit(solution)/shard_map/all_to_all | solution.py:35
  124.2 0.0 copy-start
  124.2 0.0 copy-start.1
  124.2 1.7 shard_map.89
  125.9 28.9 %all_to_all.51 = bf16[32,16,896]{2,1,0:T(8,128)(2,1)S(1)} all-to-all(bf16[32,16,896]{2,1,0:T(8,128)(2,1)S(1)} %bitcast.16), channel_id=1, replica_groups=mesh['grp'=32,'node'=32] {'node'}, dimensions={0} | all-to-all | bytes 1835008 | tf_op jit(solution)/shard_map/all_to_all | solution.py:323
  154.7 0.0 copy-done
  154.7 0.0 copy-done.1
  154.7 0.4 shard_map.90
  155.2 1.9 %collective-permute-start.1 = (bf16[256,896]{1,0:T(8,128)(2,1)S(1)}, bf16[256,896]{1,0:T(8,128)(2,1)S(1)}, u32[]{:S(2)}, u32[]{:S(2)}) collective-permute-start(bf16[256,896]{1,0:T(8,128)(2,1)S(1)} %get-tuple-element.28), channel_id=1, source_target_pairs={{0,32},{32,0},{64,96},{96,64},{128,160},{160,128},{192,224},{224,1... | collective-permute-start | bytes 1376264 | tf_op jit(solution)/shard_map/ppermute | solution.py:326
  157.1 1.8 collective-permute-done.1
  158.9 0.1 add_convert_fusion
  159.0 32.3 %all_to_all.52.parts_ref = bf16[16,16,896]{2,1,0:T(8,128)(2,1)S(1)} all-to-all(bf16[16,16,896]{2,1,0:T(8,128)(2,1)S(1)} %bitcast.25), channel_id=1, replica_groups={{0,64,160,224,256,320,416,480,512,576,672,736,768,832,928,992},{32,96,1..., dimensions={0} | all-to-all | bytes 917504 | tf_op jit(solution)/shard_map/all_to_all | solution.py:35
  191.3 0.7 shard_map.91
Async XLA Ops:
  0.0 3.0 %copy-start.2 = (bf16[2,7168]{1,0:T(2,128)(2,1)S(1)}, bf16[2,7168]{1,0:T(2,128)(2,1)}, u32[]{:S(2)}) copy-start(bf16[2,7168]{1,0:T(2,128)(2,1)} %grad_ref.1) | copy-start | bytes 86020
  0.0 3.0 %copy-start.3 = (s32[2,8]{1,0:T(2,128)S(1)}, s32[2,8]{1,0:T(2,128)}, u32[]{:S(2)}) copy-start(s32[2,8]{1,0:T(2,128)} %ids_ref.1) | copy-start | bytes 196
  0.0 3.0 %copy-start.4 = (s32[2,8]{1,0:T(2,128)S(1)}, s32[2,8]{1,0:T(2,128)}, u32[]{:S(2)}) copy-start(s32[2,8]{1,0:T(2,128)} %slots_ref.1) | copy-start | bytes 196
  0.0 3.0 %copy-start.5 = (s32[2,8]{1,0:T(2,128)S(1)}, s32[2,8]{1,0:T(2,128)}, u32[]{:S(2)}) copy-start(s32[2,8]{1,0:T(2,128)} %gates_ref.1) | copy-start | bytes 196
  3.1 53.9 %all-to-all-start = ((bf16[8,192,896]{2,1,0:T(8,128)(2,1)}), bf16[8,192,896]{2,1,0:T(8,128)(2,1)S(1)}, u32[]{:S(2)}, u32[]{:S(2)}) async-start(bf16[8,192,896]{2,1,0:T(8,128)(2,1)} %shard_map.83), calls=%async_computation | async-start | bytes 5505024 | tf_op jit(solution)/shard_map/all_to_all | solution.py:35
  50.1 4.5 %collective-permute-start = (bf16[256,1024]{1,0:T(8,128)(2,1)S(1)}, bf16[256,1024]{1,0:T(8,128)(2,1)}, u32[]{:S(2)}, u32[]{:S(2)}) collective-permute-start(bf16[256,1024]{1,0:T(8,128)(2,1)S(1)} %all_gather.3.tok_ref), channel_id=1, source_target_pairs={{0,32},{32,0},{64,96},{96,64},{128,160},{160,128},{192,224},{224,1... | collective-permute-start | bytes 1572872 | tf_op jit(solution)/shard_map/ppermute | solution.py:311
  93.8 12.2 %all-to-all-start.2 = ((bf16[8,64,512]{2,1,0:T(8,128)(2,1)}), bf16[8,64,512]{2,1,0:T(8,128)(2,1)S(1)}, u32[]{:S(2)}, u32[]{:S(2)}) async-start(bf16[8,64,512]{2,1,0:T(8,128)(2,1)} %bitcast.24), calls=%async_computation.2 | async-start | bytes 1048576 | tf_op jit(solution)/shard_map/all_to_all | solution.py:35
  124.2 30.6 %copy-start = (bf16[256,128]{1,0:T(8,128)(2,1)S(1)}, bf16[256,128]{1,0:T(8,128)(2,1)}, u32[]{:S(2)}) copy-start(bf16[256,128]{1,0:T(8,128)(2,1)} %get-tuple-element.18.hot_here_ref) | copy-start | bytes 196612
  124.2 30.6 %copy-start.1 = (bf16[256,128]{1,0:T(8,128)(2,1)S(1)}, bf16[256,128]{1,0:T(8,128)(2,1)}, u32[]{:S(2)}) copy-start(bf16[256,128]{1,0:T(8,128)(2,1)} %get-tuple-element.20.hot_there_ref) | copy-start | bytes 196612
  155.2 3.7 %collective-permute-start.1 = (bf16[256,896]{1,0:T(8,128)(2,1)S(1)}, bf16[256,896]{1,0:T(8,128)(2,1)S(1)}, u32[]{:S(2)}, u32[]{:S(2)}) collective-permute-start(bf16[256,896]{1,0:T(8,128)(2,1)S(1)} %get-tuple-element.28), channel_id=1, source_target_pairs={{0,32},{32,0},{64,96},{96,64},{128,160},{160,128},{192,224},{224,1... | collective-permute-start | bytes 1376264 | tf_op jit(solution)/shard_map/ppermute | solution.py:326

commit v7 on v6

--- a/solution.py
+++ b/solution.py
@@ -9,6 +9,7 @@
 
 SPLIT = 8
 C_DEV = 2
+ROWS_AT_ONCE = 128
 META = 128
 VMEM = 48 * 1024 * 1024
 f32, bf16 = jnp.float32, jnp.bfloat16
@@ -114,31 +115,71 @@
     )(*hbm(gate, up, down))
 
 
-def forward_body(x_ref, gate_ref, up_ref, out_ref):
+def forward_body(run_ref, x_ref, gate_ref, up_ref, *refs):
+    done_ref = refs[0] if len(refs) == 6 else None
+    out_ref, held_x, held_w, sem_x, sem_w = refs[-5:]
     n = gate_ref.shape[0]
-    both = jnp.concatenate([gate_ref[...], up_ref[...]], axis=0)
-    pre = lax.dot_general(
-        x_ref[...], both, (((1,), (1,)), ((), ())), preferred_element_type=f32
-    ).T
-    pre_gate, pre_up = pre[:n], pre[n:]
-    squash = jax.nn.sigmoid(pre_gate)
-    out_ref[:n] = pre_up * squash * (1.0 + pre_gate * (1.0 - squash))
-    out_ref[n:] = pre_gate * squash
-
-
-def forward(x, gate, up):
+    n_slot = x_ref.shape[0]
+    rows = n_slot // sem_x.shape[0]
+    block = ROWS_AT_ONCE
+
+    @pl.when(run_ref[0] != 0)
+    def _():
+        weights = [
+            pltpu.make_async_copy(ref, held_w.at[pl.ds(j * n, n)], sem_w.at[j])
+            for j, ref in enumerate((gate_ref, up_ref))
+        ]
+        inputs = [
+            pltpu.make_async_copy(
+                x_ref.at[pl.ds(i * rows, rows)],
+                held_x.at[pl.ds(i * rows, rows)],
+                sem_x.at[i],
+            )
+            for i in range(n_slot // rows)
+        ]
+        for copy in weights + inputs:
+            copy.start()
+        for copy in weights:
+            copy.wait()
+        for start in range(0, n_slot, block):
+            for i in range(start // rows, (start + block) // rows):
+                inputs[i].wait()
+            pre = lax.dot_general(
+                held_w[...],
+                held_x[start : start + block],
+                (((1,), (1,)), ((), ())),
+                preferred_element_type=f32,
+            )
+            pre_gate, pre_up = pre[:n], pre[n:]
+            squash = jax.nn.sigmoid(pre_gate)
+            out_ref[:n, start : start + block] = (
+                pre_up * squash * (1.0 + pre_gate * (1.0 - squash))
+            )
+            out_ref[n:, start : start + block] = pre_gate * squash
+
+    @pl.when(run_ref[0] == 0)
+    def _():
+        out_ref[...] = jnp.zeros_like(out_ref) if done_ref is None else done_ref[...]
+
+
+def forward(run, x, gate, up, *done):
     n_slot, width = x.shape
     n_hid = gate.shape[0]
-    half = n_slot // 2
-    spec = pl.BlockSpec((n_hid, width), lambda i: (0, 0))
     return call(
         forward_body,
         jax.ShapeDtypeStruct((2 * n_hid, n_slot), f32),
         (4 * n_hid * n_slot * width, 2 * (n_slot + 2 * n_hid) * width),
-        grid=(2,),
-        in_specs=[pl.BlockSpec((half, width), lambda i: (i, 0)), spec, spec],
-        out_specs=pl.BlockSpec((2 * n_hid, half), lambda i: (0, i)),
-    )(*hbm(x, gate, up))
+        in_specs=[pl.BlockSpec(memory_space=pltpu.SMEM)]
+        + [pl.BlockSpec(memory_space=pl.ANY)] * 3
+        + [pl.BlockSpec(memory_space=pltpu.VMEM)] * len(done),
+        out_specs=pl.BlockSpec(memory_space=pltpu.VMEM),
+        scratch_shapes=[
+            pltpu.VMEM((n_slot, width), bf16),
+            pltpu.VMEM((2 * n_hid, width), bf16),
+            pltpu.SemaphoreType.DMA((16,)),
+            pltpu.SemaphoreType.DMA((2,)),
+        ],
+    )(run, *hbm(x, gate, up), *done)
 
 
 def select_body(n_tok, per_node, n_pick, expert_ref, tok_ref, *refs):
@@ -312,13 +353,16 @@
     expert = my_expert.astype(jnp.int32).reshape(1)
     rows, hot_here = select(expert, here, (), 1, n_tok, per_node, n_pick)
     rows, hot_there = select(expert, there, (rows,), n_rest, n_tok, per_node, n_pick)
-    rows, weights = lax.optimization_barrier((rows, weights))
+    late = (my_expert % C_DEV).astype(jnp.int32).reshape(1)
+    gate, rows = lax.optimization_barrier((gate, rows))
+    coef = forward(late, saved_x[0], gate, up)
+    rows, weights, coef = lax.optimization_barrier((rows, weights, coef))
     rows = lax.all_to_all(rows, "node", 0, 0, tiled=True)
 
     gate, rows = lax.optimization_barrier((gate, rows))
     hidden = swap(hidden_part(weights, rows), "node", block)
     hidden = hidden.reshape(SPLIT, n_hid, n_slot)
-    coef = forward(saved_x[0], gate, up)
+    coef = forward(1 - late, saved_x[0], gate, up, coef)
     grads = swap(grads_of(hidden, coef), "node", block)
     parts = lax.all_to_all(slot_part(grads, weights), "node", 0, 0, tiled=True)
 

time: 193 us -> 194 us (level)
  Pallas kernels: 16 us -> 19.3 us
  blocking collectives: 145 us -> 142 us
  waiting for transfers between devices: 4.87 us -> 2.45 us
    all_to_all x1, blocking collectives: 35.2 us -> 28.3 us  [local(): rows = lax.all_to_all(rows, 'node', 0, 0, tiled=True)]
    all_to_all x1, blocking collectives: 28.9 us -> 32.4 us  [local(): parts = lax.all_to_all(slot_part(grads, weights), 'node', 0, 0, tiled=True)]
    pallas_call x1 -> x2, Pallas kernels: 4.96 us -> 8.24 us  [forward(): call(forward_body, jax.ShapeDtypeStruct((2 * n_hid, n_slot), f32), (4 * n...]
    all_to_all x2, waiting for transfers between devices: 2.43 us -> 0.01 us  [swap(): return lax.all_to_all(a, axis, 0, 0, axis_index_groups=members, tiled=True)]
  transfers between devices with their start and end apart: 4 -> 4, of which waited for: 3 -> 2; matrix products, arithmetic and copies ran while one was open for 0% -> 0% of each run, Pallas kernels for 4% -> 6%
where the time goes in v7:
time: 194 us; the launch traced here: 193 us
  blocking collectives  142 us (73%)
  starting transfers between devices  27.3 us (14%)
  Pallas kernels  19.3 us (10%)
  waiting for transfers between devices  2.45 us (1%)
    all_to_all x2, blocking collectives, swap(): return lax.all_to_all(a, axis, 0, 0, axis_index_groups=members, tiled=True)  51.3 us
    all_to_all x1, blocking collectives, local(): parts = lax.all_to_all(slot_part(grads, weights), 'node', 0, 0, tiled=True)  32.4 us
    all_gather x1, blocking collectives, local(): lax.all_gather(payload, 'grp', axis=0, axis_index_groups=along_z, tiled=T...  30.2 us
    all_to_all x1, blocking collectives, local(): rows = lax.all_to_all(rows, 'node', 0, 0, tiled=True)  28.3 us
    all_to_all x2, starting transfers between devices, swap(): return lax.all_to_all(a, axis, 0, 0, axis_index_groups=members, tiled=True)  22.5 us
    pallas_call x2, Pallas kernels, forward(): call(forward_body, jax.ShapeDtypeStruct((2 * n_hid, n_slot), f32), (4 * n...  8.24 us
  transfers between devices with their start and end apart: 4, of which 2 were waited for; matrix products, arithmetic and copies ran while one was open for 0% of the time, Pallas kernels for 6%

profile of v7, /device:TPU:2, one launch (start us, length us, event | category | flops | bytes accessed | tf_op | source)
XLA Modules:
  0.0 193.2 jit_solution(14864094936668768458)
XLA Ops:
  0.0 0.0 copy-start.4
  0.0 0.0 copy-start.5
  0.0 0.0 copy-start.6
  0.0 0.0 copy-start.7
  0.0 2.9 %shard_map.83 = bf16[8,192,896]{2,1,0:T(8,128)(2,1)} custom-call(bf16[64,7168]{1,0:T(8,128)(2,1)} %bitcast.22, bf16[64,7168]{1,0:T(8,128)(2,1)} %bitcast.25, bf16[64,7168]{1,0:T(8,128)(2,1)} %bitcast.31), custom_call_target="tpu_custom_call" | custom-call | bytes 5505024 | tf_op jit(solution)/shard_map/pallas_call | solution.py:104
  3.0 0.0 copy-done.4
  3.0 0.0 copy-done.5
  3.0 0.0 copy-done.6
  3.0 0.0 copy-done.7
  3.0 0.1 shard_map.82
  3.1 16.7 %all-to-all-start = ((bf16[8,192,896]{2,1,0:T(8,128)(2,1)}), bf16[8,192,896]{2,1,0:T(8,128)(2,1)S(1)}, u32[]{:S(2)}, u32[]{:S(2)}) async-start(bf16[8,192,896]{2,1,0:T(8,128)(2,1)} %shard_map.83), calls=%async_computation | async-start | bytes 5505024 | tf_op jit(solution)/shard_map/all_to_all | solution.py:36
  19.8 30.2 %all_gather.3.tok_ref = bf16[256,1024]{1,0:T(8,128)(2,1)S(1)} all-gather(bf16[16,1024]{1,0:T(8,128)(2,1)S(1)} %shard_map.82), channel_id=1, replica_groups={{0,64,160,224,256,320,416,480,512,576,672,736,768,832,928,992},{32,96,1..., dimensions={0}, use_global_device_ids=true | all-gather | bytes 557056 | tf_op jit(solution)/shard_map/all_gather | solution.py:351
  50.1 2.9 %collective-permute-start = (bf16[256,1024]{1,0:T(8,128)(2,1)S(1)}, bf16[256,1024]{1,0:T(8,128)(2,1)}, u32[]{:S(2)}, u32[]{:S(2)}) collective-permute-start(bf16[256,1024]{1,0:T(8,128)(2,1)S(1)} %all_gather.3.tok_ref), channel_id=1, source_target_pairs={{0,32},{32,0},{64,96},{96,64},{128,160},{160,128},{192,224},{224,1... | collective-permute-start | bytes 1572872 | tf_op jit(solution)/shard_map/ppermute | solution.py:352
  53.0 1.0 shard_map.84
  53.9 0.7 collective-permute-done.tok_ref
  54.6 2.4 %shard_map.85 = (bf16[512,896]{1,0:T(8,128)(2,1)}, bf16[256,128]{1,0:T(8,128)(2,1)}) custom-call(s32[1]{0:T(128)} %bitcast.expert_ref, bf16[256,1024]{1,0:T(8,128)(2,1)} %collective-permute-done.tok_ref, bf16[128,896]{1,0:T(8,128)(2,1)S(1)} %get-tuple-element.22.refs_0_), custom_call_target="tpu_custom_call" | custom-call | flops 58720256 | bytes 524288 | tf_op jit(solution)/shard_map/pallas_call | solution.py:212
  57.0 0.2 shard_map.86.refs_0_
  57.2 0.0 all-to-all-done.w_ref
  57.2 28.3 %all_to_all.49 = bf16[32,16,896]{2,1,0:T(8,128)(2,1)S(1)} all-to-all(bf16[32,16,896]{2,1,0:T(8,128)(2,1)} %bitcast.30), channel_id=1, replica_groups=mesh['grp'=32,'node'=32] {'node'}, dimensions={0} | all-to-all | bytes 1835008 | tf_op jit(solution)/shard_map/all_to_all | solution.py:360
  85.5 1.6 shard_map.87
  87.1 5.8 %all-to-all-start.2 = ((bf16[8,64,512]{2,1,0:T(8,128)(2,1)}), bf16[8,64,512]{2,1,0:T(8,128)(2,1)S(1)}, u32[]{:S(2)}, u32[]{:S(2)}) async-start(bf16[8,64,512]{2,1,0:T(8,128)(2,1)} %bitcast.28), calls=%async_computation.2 | async-start | bytes 1048576 | tf_op jit(solution)/shard_map/all_to_all | solution.py:36
  92.8 8.1 %shard_map.88.coef_ref = f32[128,512]{1,0:T(8,128)S(1)} custom-call(s32[1]{0:T(128)S(6)} %sub.3.run_ref, bf16[512,7168]{1,0:T(8,128)(2,1)} %bitcast.21, bf16[64,7168]{1,0:T(8,128)(2,1)} %bitcast.24, bf16[64,7168]{1,0:T(8,128)(2,1)} %bitcast.27, f32[128,512]{1,0:T(8,128)S(1)} %shard_map.86.refs_0_), custom_call_target="tpu_custom_call" | custom-call | flops 939524096 | bytes 9175040 | tf_op jit(solution)/shard_map/pallas_call | solution.py:168
  100.9 0.0 copy-start
  100.9 0.7 copy-done
  101.6 0.0 all-to-all-done.2.parts_ref
  101.6 0.0 copy-start.1
  101.6 0.9 copy-done.1
  102.6 0.2 shard_map.89
  102.8 19.1 %all_to_all.50.grads_ref = bf16[8,512,128]{2,1,0:T(8,128)(2,1)S(1)} all-to-all(bf16[8,512,128]{2,1,0:T(8,128)(2,1)S(1)} %shard_map.89), channel_id=1, replica_groups={{0,1,2,3,4,5,6,7},{8,9,10,11,12,13,14,15},{16,17,18,19,20,21,22,23},{24..., dimensions={0} | all-to-all | bytes 2097152 | tf_op jit(solution)/shard_map/all_to_all | solution.py:36
  121.9 0.0 copy-start.2
  122.0 0.0 copy-start.3
  122.0 1.7 shard_map.90
  123.6 32.4 %all_to_all.51 = bf16[32,16,896]{2,1,0:T(8,128)(2,1)S(1)} all-to-all(bf16[32,16,896]{2,1,0:T(8,128)(2,1)S(1)} %bitcast.17), channel_id=1, replica_groups=mesh['grp'=32,'node'=32] {'node'}, dimensions={0} | all-to-all | bytes 1835008 | tf_op jit(solution)/shard_map/all_to_all | solution.py:367
  156.1 0.0 copy-done.2
  156.1 0.0 copy-done.3
  156.1 0.4 shard_map.91
  156.5 1.9 collective-permute-start.1
  158.4 1.8 collective-permute-done.1
  160.2 0.1 add_convert_fusion
  160.3 32.2 %all_to_all.52.parts_ref = bf16[16,16,896]{2,1,0:T(8,128)(2,1)S(1)} all-to-all(bf16[16,16,896]{2,1,0:T(8,128)(2,1)S(1)} %bitcast.29), channel_id=1, replica_groups={{0,64,160,224,256,320,416,480,512,576,672,736,768,832,928,992},{32,96,1..., dimensions={0} | all-to-all | bytes 917504 | tf_op jit(solution)/shard_map/all_to_all | solution.py:36
  192.5 0.7 shard_map.92
Async XLA Ops:
  0.0 3.0 %copy-start.4 = (bf16[2,7168]{1,0:T(2,128)(2,1)S(1)}, bf16[2,7168]{1,0:T(2,128)(2,1)}, u32[]{:S(2)}) copy-start(bf16[2,7168]{1,0:T(2,128)(2,1)} %grad_ref.1) | copy-start | bytes 86020
  0.0 3.0 %copy-start.5 = (s32[2,8]{1,0:T(2,128)S(1)}, s32[2,8]{1,0:T(2,128)}, u32[]{:S(2)}) copy-start(s32[2,8]{1,0:T(2,128)} %ids_ref.1) | copy-start | bytes 196
  0.0 3.0 %copy-start.6 = (s32[2,8]{1,0:T(2,128)S(1)}, s32[2,8]{1,0:T(2,128)}, u32[]{:S(2)}) copy-start(s32[2,8]{1,0:T(2,128)} %slots_ref.1) | copy-start | bytes 196
  0.0 3.0 %copy-start.7 = (s32[2,8]{1,0:T(2,128)S(1)}, s32[2,8]{1,0:T(2,128)}, u32[]{:S(2)}) copy-start(s32[2,8]{1,0:T(2,128)} %gates_ref.1) | copy-start | bytes 196
  3.1 54.1 %all-to-all-start = ((bf16[8,192,896]{2,1,0:T(8,128)(2,1)}), bf16[8,192,896]{2,1,0:T(8,128)(2,1)S(1)}, u32[]{:S(2)}, u32[]{:S(2)}) async-start(bf16[8,192,896]{2,1,0:T(8,128)(2,1)} %shard_map.83), calls=%async_computation | async-start | bytes 5505024 | tf_op jit(solution)/shard_map/all_to_all | solution.py:36
  50.1 4.5 %collective-permute-start = (bf16[256,1024]{1,0:T(8,128)(2,1)S(1)}, bf16[256,1024]{1,0:T(8,128)(2,1)}, u32[]{:S(2)}, u32[]{:S(2)}) collective-permute-start(bf16[256,1024]{1,0:T(8,128)(2,1)S(1)} %all_gather.3.tok_ref), channel_id=1, source_target_pairs={{0,32},{32,0},{64,96},{96,64},{128,160},{160,128},{192,224},{224,1... | collective-permute-start | bytes 1572872 | tf_op jit(solution)/shard_map/ppermute | solution.py:352
  87.1 14.6 %all-to-all-start.2 = ((bf16[8,64,512]{2,1,0:T(8,128)(2,1)}), bf16[8,64,512]{2,1,0:T(8,128)(2,1)S(1)}, u32[]{:S(2)}, u32[]{:S(2)}) async-start(bf16[8,64,512]{2,1,0:T(8,128)(2,1)} %bitcast.28), calls=%async_computation.2 | async-start | bytes 1048576 | tf_op jit(solution)/shard_map/all_to_all | solution.py:36
  100.9 0.7 copy-start
  101.6 1.0 copy-start.1
  121.9 34.1 %copy-start.2 = (bf16[256,128]{1,0:T(8,128)(2,1)S(1)}, bf16[256,128]{1,0:T(8,128)(2,1)}, u32[]{:S(2)}) copy-start(bf16[256,128]{1,0:T(8,128)(2,1)} %get-tuple-element.21.hot_here_ref) | copy-start | bytes 196612
  122.0 34.1 %copy-start.3 = (bf16[256,128]{1,0:T(8,128)(2,1)S(1)}, bf16[256,128]{1,0:T(8,128)(2,1)}, u32[]{:S(2)}) copy-start(bf16[256,128]{1,0:T(8,128)(2,1)} %get-tuple-element.23.hot_there_ref) | copy-start | bytes 196612
  156.5 3.7 %collective-permute-start.1 = (bf16[256,896]{1,0:T(8,128)(2,1)S(1)}, bf16[256,896]{1,0:T(8,128)(2,1)S(1)}, u32[]{:S(2)}, u32[]{:S(2)}) collective-permute-start(bf16[256,896]{1,0:T(8,128)(2,1)S(1)} %get-tuple-element.34), channel_id=1, source_target_pairs={{0,32},{32,0},{64,96},{96,64},{128,160},{160,128},{192,224},{224,1... | collective-permute-start | bytes 1376264 | tf_op jit(solution)/shard_map/ppermute | solution.py:370

commit v8 on v7

--- a/solution.py
+++ b/solution.py
@@ -9,7 +9,7 @@
 
 SPLIT = 8
 C_DEV = 2
-ROWS_AT_ONCE = 128
+BLOCK = 128
 META = 128
 VMEM = 48 * 1024 * 1024
 f32, bf16 = jnp.float32, jnp.bfloat16
@@ -115,18 +115,20 @@
     )(*hbm(gate, up, down))
 
 
-def forward_body(run_ref, x_ref, gate_ref, up_ref, *refs):
-    done_ref = refs[0] if len(refs) == 6 else None
-    out_ref, held_x, held_w, sem_x, sem_w = refs[-5:]
+def coefficients(pre_gate, pre_up):
+    squash = jax.nn.sigmoid(pre_gate)
+    return pre_up * squash * (1.0 + pre_gate * (1.0 - squash)), pre_gate * squash
+
+
+def early_body(run_ref, x_ref, gate_ref, up_ref, out_ref, held_x, held_w, sem_x, sem_w):
     n = gate_ref.shape[0]
     n_slot = x_ref.shape[0]
     rows = n_slot // sem_x.shape[0]
-    block = ROWS_AT_ONCE
 
     @pl.when(run_ref[0] != 0)
     def _():
         weights = [
-            pltpu.make_async_copy(ref, held_w.at[pl.ds(j * n, n)], sem_w.at[j])
+            pltpu.make_async_copy(ref, held_w.at[j], sem_w.at[j])
             for j, ref in enumerate((gate_ref, up_ref))
         ]
         inputs = [
@@ -141,45 +143,82 @@
             copy.start()
         for copy in weights:
             copy.wait()
-        for start in range(0, n_slot, block):
-            for i in range(start // rows, (start + block) // rows):
+        for start in range(0, n_slot, BLOCK):
+            for i in range(start // rows, (start + BLOCK) // rows):
                 inputs[i].wait()
-            pre = lax.dot_general(
-                held_w[...],
-                held_x[start : start + block],
-                (((1,), (1,)), ((), ())),
-                preferred_element_type=f32,
+            pre_gate, pre_up = (
+                lax.dot_general(
+                    held_w[j],
+                    held_x[start : start + BLOCK],
+                    (((1,), (1,)), ((), ())),
+                    preferred_element_type=f32,
+                )
+                for j in range(2)
             )
-            pre_gate, pre_up = pre[:n], pre[n:]
-            squash = jax.nn.sigmoid(pre_gate)
-            out_ref[:n, start : start + block] = (
-                pre_up * squash * (1.0 + pre_gate * (1.0 - squash))
-            )
-            out_ref[n:, start : start + block] = pre_gate * squash
+            for j, value in enumerate(coefficients(pre_gate, pre_up)):
+                out_ref[j * n : (j + 1) * n, start : start + BLOCK] = value
 
     @pl.when(run_ref[0] == 0)
     def _():
-        out_ref[...] = jnp.zeros_like(out_ref) if done_ref is None else done_ref[...]
-
-
-def forward(run, x, gate, up, *done):
+        out_ref[...] = jnp.zeros_like(out_ref)
+
+
+def early_forward(run, x, gate, up):
     n_slot, width = x.shape
     n_hid = gate.shape[0]
     return call(
-        forward_body,
+        early_body,
         jax.ShapeDtypeStruct((2 * n_hid, n_slot), f32),
         (4 * n_hid * n_slot * width, 2 * (n_slot + 2 * n_hid) * width),
         in_specs=[pl.BlockSpec(memory_space=pltpu.SMEM)]
-        + [pl.BlockSpec(memory_space=pl.ANY)] * 3
-        + [pl.BlockSpec(memory_space=pltpu.VMEM)] * len(done),
+        + [pl.BlockSpec(memory_space=pl.ANY)] * 3,
         out_specs=pl.BlockSpec(memory_space=pltpu.VMEM),
         scratch_shapes=[
             pltpu.VMEM((n_slot, width), bf16),
-            pltpu.VMEM((2 * n_hid, width), bf16),
+            pltpu.VMEM((2, n_hid, width), bf16),
             pltpu.SemaphoreType.DMA((16,)),
             pltpu.SemaphoreType.DMA((2,)),
         ],
-    )(run, *hbm(x, gate, up), *done)
+    )(run, *hbm(x, gate, up))
+
+
+def late_body(run_ref, x_ref, gate_ref, up_ref, done_ref, out_ref):
+    n = gate_ref.shape[0]
+
+    @pl.when(run_ref[0] != 0)
+    def _():
+        both = jnp.concatenate([gate_ref[...], up_ref[...]], axis=0)
+        pre = lax.dot_general(
+            x_ref[...], both, (((1,), (1,)), ((), ())), preferred_element_type=f32
+        ).T
+        for j, value in enumerate(coefficients(pre[:n], pre[n:])):
+            out_ref[j * n : (j + 1) * n] = value
+
+    @pl.when(run_ref[0] == 0)
+    def _():
+        out_ref[...] = done_ref[...]
+
+
+def late_forward(run, x, gate, up, done):
+    n_slot, width = x.shape
+    n_hid = gate.shape[0]
+    half = n_slot // 2
+    spec = pl.BlockSpec((n_hid, width), lambda i: (0, 0))
+    out = pl.BlockSpec((2 * n_hid, half), lambda i: (0, i))
+    return call(
+        late_body,
+        pltpu.HBM((2 * n_hid, n_slot), f32),
+        (4 * n_hid * n_slot * width, 2 * (n_slot + 2 * n_hid) * width),
+        grid=(2,),
+        in_specs=[
+            pl.BlockSpec(memory_space=pltpu.SMEM),
+            pl.BlockSpec((half, width), lambda i: (i, 0)),
+            spec,
+            spec,
+            out,
+        ],
+        out_specs=out,
+    )(run, *hbm(x, gate, up), done)
 
 
 def select_body(n_tok, per_node, n_pick, expert_ref, tok_ref, *refs):
@@ -265,7 +304,7 @@
         grads_body,
         jax.ShapeDtypeStruct((n, n_slot, 2 * h), bf16),
         (2 * n * h * n_slot, 6 * n * h * n_slot),
-    )(parts, coef)
+    )(parts, *hbm(coef))
 
 
 def slot_body(grads_ref, w_ref, out_ref):
@@ -355,14 +394,14 @@
     rows, hot_there = select(expert, there, (rows,), n_rest, n_tok, per_node, n_pick)
     late = (my_expert % C_DEV).astype(jnp.int32).reshape(1)
     gate, rows = lax.optimization_barrier((gate, rows))
-    coef = forward(late, saved_x[0], gate, up)
+    coef = early_forward(late, saved_x[0], gate, up)
     rows, weights, coef = lax.optimization_barrier((rows, weights, coef))
     rows = lax.all_to_all(rows, "node", 0, 0, tiled=True)
 
     gate, rows = lax.optimization_barrier((gate, rows))
     hidden = swap(hidden_part(weights, rows), "node", block)
     hidden = hidden.reshape(SPLIT, n_hid, n_slot)
-    coef = forward(1 - late, saved_x[0], gate, up, coef)
+    coef = late_forward(1 - late, saved_x[0], gate, up, coef)
     grads = swap(grads_of(hidden, coef), "node", block)
     parts = lax.all_to_all(slot_part(grads, weights), "node", 0, 0, tiled=True)
 

time: 194 us -> 185 us (0.954)
  blocking collectives: 142 us -> 133 us
  starting transfers between devices: 27.3 us -> 30.7 us
    all_to_all x2, blocking collectives: 51.3 us -> 46 us  [swap(): return lax.all_to_all(a, axis, 0, 0, axis_index_groups=members, tiled=True)]
    ppermute x1, starting transfers between devices: 1.92 us -> 5.01 us  [local(): back = total([here, lax.ppermute(there, 'grp', other)])]
    all_to_all x1, blocking collectives: 32.4 us -> 29.5 us  [local(): parts = lax.all_to_all(slot_part(grads, weights), 'node', 0, 0, tiled=True)]
    pallas_call x2, Pallas kernels: 8.24 us -> 5.79 us  [the longest x1 5.61 us: late_forward(): call(late_body, pltpu.HBM((2 * n_hid, n_slot), f32), (4 * n_hid * n_slot...]
  transfers between devices with their start and end apart: 4 -> 4, of which waited for: 2 -> 3; matrix products, arithmetic and copies ran while one was open for 0% -> 0% of each run, Pallas kernels for 6% -> 5%
where the time goes in v8:
time: 185 us
  blocking collectives  133 us (72%)
  starting transfers between devices  30.7 us (17%)
  Pallas kernels  17.8 us (10%)
  waiting for transfers between devices  3.09 us (2%)
    all_to_all x2, blocking collectives, swap(): return lax.all_to_all(a, axis, 0, 0, axis_index_groups=members, tiled=True)  46 us
    all_gather x1, blocking collectives, local(): lax.all_gather(payload, 'grp', axis=0, axis_index_groups=along_z, tiled=T...  30.2 us
    all_to_all x1, blocking collectives, local(): parts = lax.all_to_all(slot_part(grads, weights), 'node', 0, 0, tiled=True)  29.5 us
    all_to_all x1, blocking collectives, local(): rows = lax.all_to_all(rows, 'node', 0, 0, tiled=True)  27.3 us
    all_to_all x2, starting transfers between devices, swap(): return lax.all_to_all(a, axis, 0, 0, axis_index_groups=members, tiled=True)  22.8 us
    pallas_call x1, Pallas kernels, late_forward(): call(late_body, pltpu.HBM((2 * n_hid, n_slot), f32), (4 * n_hid * n_slot...  5.61 us
    ppermute x1, starting transfers between devices, local(): back = total([here, lax.ppermute(there, 'grp', other)])  5.01 us
  transfers between devices with their start and end apart: 4, of which 3 were waited for; matrix products, arithmetic and copies ran while one was open for 0% of the time, Pallas kernels for 5%

profile of v8, /device:TPU:2, one launch (start us, length us, event | category | flops | bytes accessed | tf_op | source)
XLA Modules:
  0.0 184.8 jit_solution(13551046887934310443)
XLA Ops:
  0.0 0.0 copy-start.2
  0.0 0.0 copy-start.3
  0.0 0.0 copy-start.4
  0.0 0.0 copy-start.5
  0.0 2.9 %shard_map.83 = bf16[8,192,896]{2,1,0:T(8,128)(2,1)} custom-call(bf16[64,7168]{1,0:T(8,128)(2,1)} %bitcast.22, bf16[64,7168]{1,0:T(8,128)(2,1)} %bitcast.25, bf16[64,7168]{1,0:T(8,128)(2,1)} %bitcast.31), custom_call_target="tpu_custom_call" | custom-call | bytes 5505024 | tf_op jit(solution)/shard_map/pallas_call | solution.py:104
  3.0 0.0 copy-done.2
  3.0 0.0 copy-done.3
  3.0 0.0 copy-done.4
  3.0 0.0 copy-done.5
  3.0 0.1 shard_map.82
  3.1 16.7 %all-to-all-start = ((bf16[8,192,896]{2,1,0:T(8,128)(2,1)}), bf16[8,192,896]{2,1,0:T(8,128)(2,1)S(1)}, u32[]{:S(2)}, u32[]{:S(2)}) async-start(bf16[8,192,896]{2,1,0:T(8,128)(2,1)} %shard_map.83), calls=%async_computation | async-start | bytes 5505024 | tf_op jit(solution)/shard_map/all_to_all | solution.py:36
  19.8 30.2 %all_gather.3.tok_ref = bf16[256,1024]{1,0:T(8,128)(2,1)S(1)} all-gather(bf16[16,1024]{1,0:T(8,128)(2,1)S(1)} %shard_map.82), channel_id=1, replica_groups={{0,64,160,224,256,320,416,480,512,576,672,736,768,832,928,992},{32,96,1..., dimensions={0}, use_global_device_ids=true | all-gather | bytes 557056 | tf_op jit(solution)/shard_map/all_gather | solution.py:390
  50.1 2.9 %collective-permute-start = (bf16[256,1024]{1,0:T(8,128)(2,1)S(1)}, bf16[256,1024]{1,0:T(8,128)(2,1)}, u32[]{:S(2)}, u32[]{:S(2)}) collective-permute-start(bf16[256,1024]{1,0:T(8,128)(2,1)S(1)} %all_gather.3.tok_ref), channel_id=1, source_target_pairs={{0,32},{32,0},{64,96},{96,64},{128,160},{160,128},{192,224},{224,1... | collective-permute-start | bytes 1572872 | tf_op jit(solution)/shard_map/ppermute | solution.py:391
  53.0 1.0 shard_map.84
  53.9 0.7 collective-permute-done.tok_ref
  54.6 2.4 %shard_map.85 = (bf16[512,896]{1,0:T(8,128)(2,1)}, bf16[256,128]{1,0:T(8,128)(2,1)}) custom-call(s32[1]{0:T(128)} %bitcast.expert_ref, bf16[256,1024]{1,0:T(8,128)(2,1)} %collective-permute-done.tok_ref, bf16[128,896]{1,0:T(8,128)(2,1)S(1)} %get-tuple-element.22.refs_0_), custom_call_target="tpu_custom_call" | custom-call | flops 58720256 | bytes 524288 | tf_op jit(solution)/shard_map/pallas_call | solution.py:251
  57.0 0.2 shard_map.86.done_ref
  57.2 0.0 all-to-all-done.w_ref
  57.2 27.3 %all_to_all.49 = bf16[32,16,896]{2,1,0:T(8,128)(2,1)S(1)} all-to-all(bf16[32,16,896]{2,1,0:T(8,128)(2,1)} %bitcast.30), channel_id=1, replica_groups=mesh['grp'=32,'node'=32] {'node'}, dimensions={0} | all-to-all | bytes 1835008 | tf_op jit(solution)/shard_map/all_to_all | solution.py:399
  84.5 1.5 shard_map.87
  86.1 6.1 %all-to-all-start.2 = ((bf16[8,64,512]{2,1,0:T(8,128)(2,1)}), bf16[8,64,512]{2,1,0:T(8,128)(2,1)S(1)}, u32[]{:S(2)}, u32[]{:S(2)}) async-start(bf16[8,64,512]{2,1,0:T(8,128)(2,1)} %bitcast.28), calls=%async_computation.2 | async-start | bytes 1048576 | tf_op jit(solution)/shard_map/all_to_all | solution.py:36
  92.1 5.6 %shard_map.88.coef_ref = f32[128,512]{1,0:T(8,128)} custom-call(s32[1]{0:T(128)S(6)} %sub.3.run_ref, bf16[512,7168]{1,0:T(8,128)(2,1)} %bitcast.21, bf16[64,7168]{1,0:T(8,128)(2,1)} %bitcast.24, bf16[64,7168]{1,0:T(8,128)(2,1)} %bitcast.27, f32[128,512]{1,0:T(8,128)S(1)} %shard_map.86.done_ref), custom_call_target="tpu_custom_call" | custom-call | flops 939524096 | bytes 9175040 | tf_op jit(solution)/shard_map/pallas_call | solution.py:208
  97.8 1.0 all-to-all-done.2.parts_ref
  98.8 1.2 shard_map.89
  100.0 14.5 %all_to_all.50.grads_ref = bf16[8,512,128]{2,1,0:T(8,128)(2,1)S(1)} all-to-all(bf16[8,512,128]{2,1,0:T(8,128)(2,1)S(1)} %shard_map.89), channel_id=1, replica_groups={{0,1,2,3,4,5,6,7},{8,9,10,11,12,13,14,15},{16,17,18,19,20,21,22,23},{24..., dimensions={0} | all-to-all | bytes 2097152 | tf_op jit(solution)/shard_map/all_to_all | solution.py:36
  114.4 0.0 copy-start
  114.4 0.0 copy-start.1
  114.4 1.7 shard_map.90
  116.1 29.5 %all_to_all.51 = bf16[32,16,896]{2,1,0:T(8,128)(2,1)S(1)} all-to-all(bf16[32,16,896]{2,1,0:T(8,128)(2,1)S(1)} %bitcast.17), channel_id=1, replica_groups=mesh['grp'=32,'node'=32] {'node'}, dimensions={0} | all-to-all | bytes 1835008 | tf_op jit(solution)/shard_map/all_to_all | solution.py:406
  145.6 0.0 copy-done
  145.6 0.0 copy-done.1
  145.6 0.4 shard_map.91
  146.0 5.0 %collective-permute-start.1 = (bf16[256,896]{1,0:T(8,128)(2,1)S(1)}, bf16[256,896]{1,0:T(8,128)(2,1)S(1)}, u32[]{:S(2)}, u32[]{:S(2)}) collective-permute-start(bf16[256,896]{1,0:T(8,128)(2,1)S(1)} %get-tuple-element.34), channel_id=1, source_target_pairs={{0,32},{32,0},{64,96},{96,64},{128,160},{160,128},{192,224},{224,1... | collective-permute-start | bytes 1376264 | tf_op jit(solution)/shard_map/ppermute | solution.py:409
  151.1 1.4 collective-permute-done.1
  152.5 0.1 add_convert_fusion
  152.6 31.5 %all_to_all.52.parts_ref = bf16[16,16,896]{2,1,0:T(8,128)(2,1)S(1)} all-to-all(bf16[16,16,896]{2,1,0:T(8,128)(2,1)S(1)} %bitcast.29), channel_id=1, replica_groups={{0,64,160,224,256,320,416,480,512,576,672,736,768,832,928,992},{32,96,1..., dimensions={0} | all-to-all | bytes 917504 | tf_op jit(solution)/shard_map/all_to_all | solution.py:36
  184.1 0.7 shard_map.92
Async XLA Ops:
  0.0 3.0 %copy-start.2 = (bf16[2,7168]{1,0:T(2,128)(2,1)S(1)}, bf16[2,7168]{1,0:T(2,128)(2,1)}, u32[]{:S(2)}) copy-start(bf16[2,7168]{1,0:T(2,128)(2,1)} %grad_ref.1) | copy-start | bytes 86020
  0.0 3.0 %copy-start.3 = (s32[2,8]{1,0:T(2,128)S(1)}, s32[2,8]{1,0:T(2,128)}, u32[]{:S(2)}) copy-start(s32[2,8]{1,0:T(2,128)} %ids_ref.1) | copy-start | bytes 196
  0.0 3.0 %copy-start.4 = (s32[2,8]{1,0:T(2,128)S(1)}, s32[2,8]{1,0:T(2,128)}, u32[]{:S(2)}) copy-start(s32[2,8]{1,0:T(2,128)} %slots_ref.1) | copy-start | bytes 196
  0.0 3.0 %copy-start.5 = (s32[2,8]{1,0:T(2,128)S(1)}, s32[2,8]{1,0:T(2,128)}, u32[]{:S(2)}) copy-start(s32[2,8]{1,0:T(2,128)} %gates_ref.1) | copy-start | bytes 196
  3.1 54.1 %all-to-all-start = ((bf16[8,192,896]{2,1,0:T(8,128)(2,1)}), bf16[8,192,896]{2,1,0:T(8,128)(2,1)S(1)}, u32[]{:S(2)}, u32[]{:S(2)}) async-start(bf16[8,192,896]{2,1,0:T(8,128)(2,1)} %shard_map.83), calls=%async_computation | async-start | bytes 5505024 | tf_op jit(solution)/shard_map/all_to_all | solution.py:36
  50.1 4.5 %collective-permute-start = (bf16[256,1024]{1,0:T(8,128)(2,1)S(1)}, bf16[256,1024]{1,0:T(8,128)(2,1)}, u32[]{:S(2)}, u32[]{:S(2)}) collective-permute-start(bf16[256,1024]{1,0:T(8,128)(2,1)S(1)} %all_gather.3.tok_ref), channel_id=1, source_target_pairs={{0,32},{32,0},{64,96},{96,64},{128,160},{160,128},{192,224},{224,1... | collective-permute-start | bytes 1572872 | tf_op jit(solution)/shard_map/ppermute | solution.py:391
  86.1 12.7 %all-to-all-start.2 = ((bf16[8,64,512]{2,1,0:T(8,128)(2,1)}), bf16[8,64,512]{2,1,0:T(8,128)(2,1)S(1)}, u32[]{:S(2)}, u32[]{:S(2)}) async-start(bf16[8,64,512]{2,1,0:T(8,128)(2,1)} %bitcast.28), calls=%async_computation.2 | async-start | bytes 1048576 | tf_op jit(solution)/shard_map/all_to_all | solution.py:36
  114.4 31.1 %copy-start = (bf16[256,128]{1,0:T(8,128)(2,1)S(1)}, bf16[256,128]{1,0:T(8,128)(2,1)}, u32[]{:S(2)}) copy-start(bf16[256,128]{1,0:T(8,128)(2,1)} %get-tuple-element.21.hot_here_ref) | copy-start | bytes 196612
  114.4 31.2 %copy-start.1 = (bf16[256,128]{1,0:T(8,128)(2,1)S(1)}, bf16[256,128]{1,0:T(8,128)(2,1)}, u32[]{:S(2)}) copy-start(bf16[256,128]{1,0:T(8,128)(2,1)} %get-tuple-element.23.hot_there_ref) | copy-start | bytes 196612
  146.0 6.4 %collective-permute-start.1 = (bf16[256,896]{1,0:T(8,128)(2,1)S(1)}, bf16[256,896]{1,0:T(8,128)(2,1)S(1)}, u32[]{:S(2)}, u32[]{:S(2)}) collective-permute-start(bf16[256,896]{1,0:T(8,128)(2,1)S(1)} %get-tuple-element.34), channel_id=1, source_target_pairs={{0,32},{32,0},{64,96},{96,64},{128,160},{160,128},{192,224},{224,1... | collective-permute-start | bytes 1376264 | tf_op jit(solution)/shard_map/ppermute | solution.py:409

commit v9 on v8

--- a/solution.py
+++ b/solution.py
@@ -9,6 +9,7 @@
 
 SPLIT = 8
 C_DEV = 2
+Z_STEP = 4
 BLOCK = 128
 META = 128
 VMEM = 48 * 1024 * 1024
@@ -141,11 +142,9 @@
         ]
         for copy in weights + inputs:
             copy.start()
-        for copy in weights:
+        for copy in weights + inputs:
             copy.wait()
         for start in range(0, n_slot, BLOCK):
-            for i in range(start // rows, (start + BLOCK) // rows):
-                inputs[i].wait()
             pre_gate, pre_up = (
                 lax.dot_general(
                     held_w[j],
@@ -289,10 +288,13 @@
     )(weights, rows)
 
 
-def grads_body(parts_ref, coef_ref, out_ref):
+def grads_body(parts_ref, coef_ref, out_ref, held, sem):
     n, h, _ = parts_ref.shape
+    copy = pltpu.make_async_copy(coef_ref, held, sem)
+    copy.start()
     total = jnp.sum(parts_ref[...].astype(f32), axis=0)
-    grads = jnp.concatenate([total * coef_ref[:h], total * coef_ref[h:]], axis=0)
+    copy.wait()
+    grads = jnp.concatenate([total * held[:h], total * held[h:]], axis=0)
     grads = grads.T.astype(bf16)
     for i in range(n):
         out_ref[i] = grads
@@ -304,6 +306,12 @@
         grads_body,
         jax.ShapeDtypeStruct((n, n_slot, 2 * h), bf16),
         (2 * n * h * n_slot, 6 * n * h * n_slot),
+        in_specs=[
+            pl.BlockSpec(memory_space=pltpu.VMEM),
+            pl.BlockSpec(memory_space=pl.ANY),
+        ],
+        out_specs=pl.BlockSpec(memory_space=pltpu.VMEM),
+        scratch_shapes=[pltpu.VMEM((2 * h, n_slot), f32), pltpu.SemaphoreType.DMA],
     )(parts, *hbm(coef))
 
 
@@ -331,18 +339,20 @@
     )(grads, weights)
 
 
-def back_body(hot_here_ref, hot_there_ref, parts_ref, here_ref, there_ref):
+def back_body(order, hot_here_ref, hot_there_ref, parts_ref, here_ref, there_ref):
     own = jnp.sum(parts_ref[...].astype(f32), axis=0).astype(bf16)
+    rows = here_ref.shape[0] // len(order)
     for hot_ref, out_ref in ((hot_there_ref, there_ref), (hot_here_ref, here_ref)):
-        got = jnp.dot(hot_ref[...], own, preferred_element_type=f32)
-        out_ref[...] = got.astype(bf16)
-
-
-def back_rows(hot_here, hot_there, parts):
+        got = jnp.dot(hot_ref[...], own, preferred_element_type=f32).astype(bf16)
+        for i, z in enumerate(order):
+            out_ref[i * rows : (i + 1) * rows] = got[z * rows : (z + 1) * rows]
+
+
+def back_rows(order, hot_here, hot_there, parts):
     half, n_own = hot_here.shape
     part = parts.shape[2]
     return call(
-        back_body,
+        functools.partial(back_body, order),
         (jax.ShapeDtypeStruct((half, part), bf16),) * 2,
         (4 * half * n_own * part, 4 * half * part + 2 * parts.size),
     )(hot_here, hot_there, parts)
@@ -371,6 +381,7 @@
     along_z = [
         [z * C_DEV + (c + z // 2) % C_DEV for z in range(n_z)] for c in range(C_DEV)
     ]
+    order = [z for first in range(Z_STEP) for z in range(first, n_z, Z_STEP)]
     other = [(z * C_DEV + c, z * C_DEV + 1 - c) for z in range(n_z) for c in range(C_DEV)]
     n_tok, width = out_grad.shape
     part = width // SPLIT
@@ -405,9 +416,9 @@
     grads = swap(grads_of(hidden, coef), "node", block)
     parts = lax.all_to_all(slot_part(grads, weights), "node", 0, 0, tiled=True)
 
-    here, there = back_rows(hot_here, hot_there, parts.reshape(n_rest, n_own, part))
+    here, there = back_rows(order, hot_here, hot_there, parts.reshape(n_rest, n_own, part))
     back = total([here, lax.ppermute(there, "grp", other)])
-    back = swap(back, "grp", along_z).reshape(n_z, SPLIT * n_tok, part)
+    back = swap(back, "grp", [[ring[z] for z in order] for ring in along_z]).reshape(n_z, SPLIT * n_tok, part)
     return unpack(back, n_tok)
 
 

time: 185 us -> 187 us (1.011)
  the two profiles are of different devices: /device:TPU:2 before, /device:TPU:131 now
where the time goes in v9:
time: 187 us
  blocking collectives  144 us (77%)
  Pallas kernels  25.2 us (13%)
  starting transfers between devices  13.6 us (7%)
  waiting for transfers between devices  3.91 us (2%)
    all_to_all x2, blocking collectives, swap(): return lax.all_to_all(a, axis, 0, 0, axis_index_groups=members, tiled=True)  50 us
    all_gather x1, blocking collectives, local(): lax.all_gather(payload, 'grp', axis=0, axis_index_groups=along_z, tiled=T...  38.5 us
    all_to_all x1, blocking collectives, local(): parts = lax.all_to_all(slot_part(grads, weights), 'node', 0, 0, tiled=True)  27.8 us
    all_to_all x1, blocking collectives, local(): rows = lax.all_to_all(rows, 'node', 0, 0, tiled=True)  27.4 us
    all_to_all x2, starting transfers between devices, swap(): return lax.all_to_all(a, axis, 0, 0, axis_index_groups=members, tiled=True)  9.56 us
    pallas_call x1, Pallas kernels, early_forward(): call(early_body, jax.ShapeDtypeStruct((2 * n_hid, n_slot), f32), (4 * n_h...  8.81 us
    pallas_call x1, Pallas kernels, late_forward(): call(late_body, pltpu.HBM((2 * n_hid, n_slot), f32), (4 * n_hid * n_slot...  4.43 us
  transfers between devices with their start and end apart: 4, of which 3 were waited for; matrix products, arithmetic and copies ran while one was open for 0% of the time, Pallas kernels for 9%

profile of v9, /device:TPU:131, one launch (start us, length us, event | category | flops | bytes accessed | tf_op | source)
XLA Modules:
  0.0 186.6 jit_solution(18059136892939305573)
XLA Ops:
  0.0 0.0 copy-start.2
  0.0 0.0 copy-start.3
  0.0 0.0 copy-start.4
  0.0 0.0 copy-start.5
  0.0 2.9 %shard_map.83 = bf16[8,192,896]{2,1,0:T(8,128)(2,1)} custom-call(bf16[64,7168]{1,0:T(8,128)(2,1)} %bitcast.22, bf16[64,7168]{1,0:T(8,128)(2,1)} %bitcast.25, bf16[64,7168]{1,0:T(8,128)(2,1)} %bitcast.31), custom_call_target="tpu_custom_call" | custom-call | bytes 5505024 | tf_op jit(solution)/shard_map/pallas_call | solution.py:105
  3.0 0.0 copy-done.2
  3.0 0.0 copy-done.3
  3.0 0.0 copy-done.4
  3.0 0.0 copy-done.5
  3.0 0.1 shard_map.82
  3.1 5.3 %all-to-all-start = ((bf16[8,192,896]{2,1,0:T(8,128)(2,1)}), bf16[8,192,896]{2,1,0:T(8,128)(2,1)S(1)}, u32[]{:S(2)}, u32[]{:S(2)}) async-start(bf16[8,192,896]{2,1,0:T(8,128)(2,1)} %shard_map.83), calls=%async_computation | async-start | bytes 5505024 | tf_op jit(solution)/shard_map/all_to_all | solution.py:37
  8.4 38.5 %all_gather.3.tok_ref = bf16[256,1024]{1,0:T(8,128)(2,1)S(1)} all-gather(bf16[16,1024]{1,0:T(8,128)(2,1)S(1)} %shard_map.82), channel_id=1, replica_groups={{0,64,160,224,256,320,416,480,512,576,672,736,768,832,928,992},{32,96,1..., dimensions={0}, use_global_device_ids=true | all-gather | bytes 557056 | tf_op jit(solution)/shard_map/all_gather | solution.py:401
  46.9 2.1 %collective-permute-start = (bf16[256,1024]{1,0:T(8,128)(2,1)S(1)}, bf16[256,1024]{1,0:T(8,128)(2,1)}, u32[]{:S(2)}, u32[]{:S(2)}) collective-permute-start(bf16[256,1024]{1,0:T(8,128)(2,1)S(1)} %all_gather.3.tok_ref), channel_id=1, source_target_pairs={{0,32},{32,0},{64,96},{96,64},{128,160},{160,128},{192,224},{224,1... | collective-permute-start | bytes 1572872 | tf_op jit(solution)/shard_map/ppermute | solution.py:402
  49.0 1.0 shard_map.84
  50.0 0.8 collective-permute-done.tok_ref
  50.8 2.4 %shard_map.85 = (bf16[512,896]{1,0:T(8,128)(2,1)}, bf16[256,128]{1,0:T(8,128)(2,1)}) custom-call(s32[1]{0:T(128)} %bitcast.expert_ref, bf16[256,1024]{1,0:T(8,128)(2,1)} %collective-permute-done.tok_ref, bf16[128,896]{1,0:T(8,128)(2,1)S(1)} %get-tuple-element.22.refs_0_), custom_call_target="tpu_custom_call" | custom-call | flops 58720256 | bytes 524288 | tf_op jit(solution)/shard_map/pallas_call | solution.py:250
  53.2 8.8 %shard_map.86.done_ref = f32[128,512]{1,0:T(8,128)S(1)} custom-call(s32[1]{0:T(128)} %bitcast.8.run_ref, bf16[512,7168]{1,0:T(8,128)(2,1)} %bitcast.20, bf16[64,7168]{1,0:T(8,128)(2,1)} %bitcast.23, bf16[64,7168]{1,0:T(8,128)(2,1)} %bitcast.26), custom_call_target="tpu_custom_call" | custom-call | flops 939524096 | bytes 9175040 | tf_op jit(solution)/shard_map/pallas_call | solution.py:168
  62.0 0.0 all-to-all-done.w_ref
  62.1 27.4 %all_to_all.49 = bf16[32,16,896]{2,1,0:T(8,128)(2,1)S(1)} all-to-all(bf16[32,16,896]{2,1,0:T(8,128)(2,1)} %bitcast.30), channel_id=1, replica_groups=mesh['grp'=32,'node'=32] {'node'}, dimensions={0} | all-to-all | bytes 1835008 | tf_op jit(solution)/shard_map/all_to_all | solution.py:410
  89.4 1.5 shard_map.87
  91.0 4.3 %all-to-all-start.2 = ((bf16[8,64,512]{2,1,0:T(8,128)(2,1)}), bf16[8,64,512]{2,1,0:T(8,128)(2,1)S(1)}, u32[]{:S(2)}, u32[]{:S(2)}) async-start(bf16[8,64,512]{2,1,0:T(8,128)(2,1)} %bitcast.28), calls=%async_computation.2 | async-start | bytes 1048576 | tf_op jit(solution)/shard_map/all_to_all | solution.py:37
  95.3 4.4 %shard_map.88.coef_ref = f32[128,512]{1,0:T(8,128)} custom-call(s32[1]{0:T(128)S(6)} %sub.3.run_ref, bf16[512,7168]{1,0:T(8,128)(2,1)} %bitcast.21, bf16[64,7168]{1,0:T(8,128)(2,1)} %bitcast.24, bf16[64,7168]{1,0:T(8,128)(2,1)} %bitcast.27, f32[128,512]{1,0:T(8,128)S(1)} %shard_map.86.done_ref), custom_call_target="tpu_custom_call" | custom-call | flops 939524096 | bytes 9175040 | tf_op jit(solution)/shard_map/pallas_call | solution.py:207
  99.7 1.3 all-to-all-done.2.parts_ref
  101.0 1.1 shard_map.89
  102.2 13.5 %all_to_all.50.grads_ref = bf16[8,512,128]{2,1,0:T(8,128)(2,1)S(1)} all-to-all(bf16[8,512,128]{2,1,0:T(8,128)(2,1)S(1)} %shard_map.89), channel_id=1, replica_groups={{0,1,2,3,4,5,6,7},{8,9,10,11,12,13,14,15},{16,17,18,19,20,21,22,23},{24..., dimensions={0} | all-to-all | bytes 2097152 | tf_op jit(solution)/shard_map/all_to_all | solution.py:37
  115.7 0.0 copy-start
  115.7 0.0 copy-start.1
  115.7 1.7 shard_map.90
  117.4 27.8 %all_to_all.51 = bf16[32,16,896]{2,1,0:T(8,128)(2,1)S(1)} all-to-all(bf16[32,16,896]{2,1,0:T(8,128)(2,1)S(1)} %bitcast.17), channel_id=1, replica_groups=mesh['grp'=32,'node'=32] {'node'}, dimensions={0} | all-to-all | bytes 1835008 | tf_op jit(solution)/shard_map/all_to_all | solution.py:417
  145.1 0.0 copy-done
  145.1 0.0 copy-done.1
  145.1 0.4 shard_map.91
  145.6 1.9 %collective-permute-start.1 = (bf16[256,896]{1,0:T(8,128)(2,1)S(1)}, bf16[256,896]{1,0:T(8,128)(2,1)S(1)}, u32[]{:S(2)}, u32[]{:S(2)}) collective-permute-start(bf16[256,896]{1,0:T(8,128)(2,1)S(1)} %get-tuple-element.34), channel_id=1, source_target_pairs={{0,32},{32,0},{64,96},{96,64},{128,160},{160,128},{192,224},{224,1... | collective-permute-start | bytes 1376264 | tf_op jit(solution)/shard_map/ppermute | solution.py:420
  147.5 1.8 collective-permute-done.1
  149.3 0.1 add_convert_fusion
  149.4 36.5 %all_to_all.52.parts_ref = bf16[16,16,896]{2,1,0:T(8,128)(2,1)S(1)} all-to-all(bf16[16,16,896]{2,1,0:T(8,128)(2,1)S(1)} %bitcast.29), channel_id=1, replica_groups={{0,256,512,768,64,320,576,832,160,416,672,928,224,480,736,992},{32,288,..., dimensions={0} | all-to-all | bytes 917504 | tf_op jit(solution)/shard_map/all_to_all | solution.py:37
  185.9 0.7 shard_map.92
Async XLA Ops:
  0.0 3.0 %copy-start.2 = (bf16[2,7168]{1,0:T(2,128)(2,1)S(1)}, bf16[2,7168]{1,0:T(2,128)(2,1)}, u32[]{:S(2)}) copy-start(bf16[2,7168]{1,0:T(2,128)(2,1)} %grad_ref.1) | copy-start | bytes 86020
  0.0 3.0 %copy-start.3 = (s32[2,8]{1,0:T(2,128)S(1)}, s32[2,8]{1,0:T(2,128)}, u32[]{:S(2)}) copy-start(s32[2,8]{1,0:T(2,128)} %ids_ref.1) | copy-start | bytes 196
  0.0 3.0 %copy-start.4 = (s32[2,8]{1,0:T(2,128)S(1)}, s32[2,8]{1,0:T(2,128)}, u32[]{:S(2)}) copy-start(s32[2,8]{1,0:T(2,128)} %slots_ref.1) | copy-start | bytes 196
  0.0 3.0 %copy-start.5 = (s32[2,8]{1,0:T(2,128)S(1)}, s32[2,8]{1,0:T(2,128)}, u32[]{:S(2)}) copy-start(s32[2,8]{1,0:T(2,128)} %gates_ref.1) | copy-start | bytes 196
  3.1 58.9 %all-to-all-start = ((bf16[8,192,896]{2,1,0:T(8,128)(2,1)}), bf16[8,192,896]{2,1,0:T(8,128)(2,1)S(1)}, u32[]{:S(2)}, u32[]{:S(2)}) async-start(bf16[8,192,896]{2,1,0:T(8,128)(2,1)} %shard_map.83), calls=%async_computation | async-start | bytes 5505024 | tf_op jit(solution)/shard_map/all_to_all | solution.py:37
  46.9 3.9 %collective-permute-start = (bf16[256,1024]{1,0:T(8,128)(2,1)S(1)}, bf16[256,1024]{1,0:T(8,128)(2,1)}, u32[]{:S(2)}, u32[]{:S(2)}) collective-permute-start(bf16[256,1024]{1,0:T(8,128)(2,1)S(1)} %all_gather.3.tok_ref), channel_id=1, source_target_pairs={{0,32},{32,0},{64,96},{96,64},{128,160},{160,128},{192,224},{224,1... | collective-permute-start | bytes 1572872 | tf_op jit(solution)/shard_map/ppermute | solution.py:402
  91.0 10.0 %all-to-all-start.2 = ((bf16[8,64,512]{2,1,0:T(8,128)(2,1)}), bf16[8,64,512]{2,1,0:T(8,128)(2,1)S(1)}, u32[]{:S(2)}, u32[]{:S(2)}) async-start(bf16[8,64,512]{2,1,0:T(8,128)(2,1)} %bitcast.28), calls=%async_computation.2 | async-start | bytes 1048576 | tf_op jit(solution)/shard_map/all_to_all | solution.py:37
  115.7 29.5 %copy-start = (bf16[256,128]{1,0:T(8,128)(2,1)S(1)}, bf16[256,128]{1,0:T(8,128)(2,1)}, u32[]{:S(2)}) copy-start(bf16[256,128]{1,0:T(8,128)(2,1)} %get-tuple-element.21.hot_here_ref) | copy-start | bytes 196612
  115.7 29.5 %copy-start.1 = (bf16[256,128]{1,0:T(8,128)(2,1)S(1)}, bf16[256,128]{1,0:T(8,128)(2,1)}, u32[]{:S(2)}) copy-start(bf16[256,128]{1,0:T(8,128)(2,1)} %get-tuple-element.23.hot_there_ref) | copy-start | bytes 196612
  145.6 3.7 %collective-permute-start.1 = (bf16[256,896]{1,0:T(8,128)(2,1)S(1)}, bf16[256,896]{1,0:T(8,128)(2,1)S(1)}, u32[]{:S(2)}, u32[]{:S(2)}) collective-permute-start(bf16[256,896]{1,0:T(8,128)(2,1)S(1)} %get-tuple-element.34), channel_id=1, source_target_pairs={{0,32},{32,0},{64,96},{96,64},{128,160},{160,128},{192,224},{224,1... | collective-permute-start | bytes 1376264 | tf_op jit(solution)/shard_map/ppermute | solution.py:420

commit v10 on v8

--- a/solution.py
+++ b/solution.py
@@ -9,6 +9,7 @@
 
 SPLIT = 8
 C_DEV = 2
+RING = 2
 BLOCK = 128
 META = 128
 VMEM = 48 * 1024 * 1024
@@ -331,21 +332,32 @@
     )(grads, weights)
 
 
-def back_body(hot_here_ref, hot_there_ref, parts_ref, here_ref, there_ref):
+def back_body(order, flip_ref, hot_here_ref, hot_there_ref, parts_ref, here_ref, there_ref):
     own = jnp.sum(parts_ref[...].astype(f32), axis=0).astype(bf16)
-    for hot_ref, out_ref in ((hot_there_ref, there_ref), (hot_here_ref, here_ref)):
-        got = jnp.dot(hot_ref[...], own, preferred_element_type=f32)
-        out_ref[...] = got.astype(bf16)
-
-
-def back_rows(hot_here, hot_there, parts):
+    rows = here_ref.shape[0] // len(order)
+    z = lax.broadcasted_iota(jnp.int32, hot_here_ref.shape, 0) // rows
+    same = (z // RING) % C_DEV == flip_ref[0]
+    here, there = hot_here_ref[...].astype(f32), hot_there_ref[...].astype(f32)
+    for hot, out_ref in (
+        (jnp.where(same, there, here), there_ref),
+        (jnp.where(same, here, there), here_ref),
+    ):
+        got = jnp.dot(hot.astype(bf16), own, preferred_element_type=f32).astype(bf16)
+        for i, z in enumerate(order):
+            out_ref[i * rows : (i + 1) * rows] = got[z * rows : (z + 1) * rows]
+
+
+def back_rows(order, flip, hot_here, hot_there, parts):
     half, n_own = hot_here.shape
     part = parts.shape[2]
     return call(
-        back_body,
+        functools.partial(back_body, order),
         (jax.ShapeDtypeStruct((half, part), bf16),) * 2,
         (4 * half * n_own * part, 4 * half * part + 2 * parts.size),
-    )(hot_here, hot_there, parts)
+        in_specs=[pl.BlockSpec(memory_space=pltpu.SMEM)]
+        + [pl.BlockSpec(memory_space=pltpu.VMEM)] * 3,
+        out_specs=[pl.BlockSpec(memory_space=pltpu.VMEM)] * 2,
+    )(flip, hot_here, hot_there, parts)
 
 
 def unpack_body(parts_ref, out_ref):
@@ -369,8 +381,9 @@
     n_rest, n_z = n_node // SPLIT, n_grp // C_DEV
     block = [[h * SPLIT + d for d in range(SPLIT)] for h in range(n_rest)]
     along_z = [
-        [z * C_DEV + (c + z // 2) % C_DEV for z in range(n_z)] for c in range(C_DEV)
+        [z * C_DEV + (c + z // RING) % C_DEV for z in range(n_z)] for c in range(C_DEV)
     ]
+    order = list(range(0, n_z, 2)) + list(range(1, n_z, 2))
     other = [(z * C_DEV + c, z * C_DEV + 1 - c) for z in range(n_z) for c in range(C_DEV)]
     n_tok, width = out_grad.shape
     part = width // SPLIT
@@ -405,9 +418,10 @@
     grads = swap(grads_of(hidden, coef), "node", block)
     parts = lax.all_to_all(slot_part(grads, weights), "node", 0, 0, tiled=True)
 
-    here, there = back_rows(hot_here, hot_there, parts.reshape(n_rest, n_own, part))
+    flip = (my_expert // C_DEV // RING % C_DEV).astype(jnp.int32).reshape(1)
+    here, there = back_rows(order, flip, hot_here, hot_there, parts.reshape(n_rest, n_own, part))
     back = total([here, lax.ppermute(there, "grp", other)])
-    back = swap(back, "grp", along_z).reshape(n_z, SPLIT * n_tok, part)
+    back = swap(back, "grp", [[z * C_DEV + c for z in order] for c in range(C_DEV)]).reshape(n_z, SPLIT * n_tok, part)
     return unpack(back, n_tok)
 
 

time: 185 us -> 187 us (1.011)
  the two profiles are of different devices: /device:TPU:2 before, /device:TPU:128 now
where the time goes in v10:
time: 187 us; the launch traced here: 186 us
  blocking collectives  114 us (61%)
  waiting for transfers between devices  27.3 us (15%)
  starting transfers between devices  25.1 us (13%)
  Pallas kernels  17.9 us (10%)
    all_to_all x2, blocking collectives, swap(): return lax.all_to_all(a, axis, 0, 0, axis_index_groups=members, tiled=True)  49.5 us
    all_gather x1, blocking collectives, local(): lax.all_gather(payload, 'grp', axis=0, axis_index_groups=along_z, tiled=T...  38.5 us
    all_to_all x1, blocking collectives, local(): rows = lax.all_to_all(rows, 'node', 0, 0, tiled=True)  26.4 us
    all_to_all x1, waiting for transfers between devices, local(): parts = lax.all_to_all(slot_part(grads, weights), 'node', 0, 0, tiled=True)  22.5 us
    all_to_all x2, starting transfers between devices, swap(): return lax.all_to_all(a, axis, 0, 0, axis_index_groups=members, tiled=True)  11.6 us
    ppermute x1, starting transfers between devices, local(): back = total([here, lax.ppermute(there, 'grp', other)])  6.58 us
    pallas_call x1, Pallas kernels, late_forward(): call(late_body, pltpu.HBM((2 * n_hid, n_slot), f32), (4 * n_hid * n_slot...  5.61 us
    all_to_all x1, starting transfers between devices, local(): parts = lax.all_to_all(slot_part(grads, weights), 'node', 0, 0, tiled=True)  4.65 us
  transfers between devices with their start and end apart: 5, of which 4 were waited for; matrix products, arithmetic and copies ran while one was open for 0% of the time, Pallas kernels for 5%

profile of v10, /device:TPU:128, one launch (start us, length us, event | category | flops | bytes accessed | tf_op | source)
XLA Modules:
  0.0 185.9 jit_solution(1442162963069390594)
XLA Ops:
  0.0 0.0 copy-start.3
  0.0 0.0 copy-start.4
  0.0 0.0 copy-start.5
  0.0 0.0 copy-start.6
  0.0 2.9 %shard_map.83 = bf16[8,192,896]{2,1,0:T(8,128)(2,1)} custom-call(bf16[64,7168]{1,0:T(8,128)(2,1)} %bitcast.23, bf16[64,7168]{1,0:T(8,128)(2,1)} %bitcast.26, bf16[64,7168]{1,0:T(8,128)(2,1)} %bitcast.32), custom_call_target="tpu_custom_call" | custom-call | bytes 5505024 | tf_op jit(solution)/shard_map/pallas_call | solution.py:105
  3.0 0.0 copy-done.3
  3.0 0.0 copy-done.4
  3.0 0.0 copy-done.5
  3.0 0.0 copy-done.6
  3.0 0.1 shard_map.82
  3.1 5.3 %all-to-all-start = ((bf16[8,192,896]{2,1,0:T(8,128)(2,1)}), bf16[8,192,896]{2,1,0:T(8,128)(2,1)S(1)}, u32[]{:S(2)}, u32[]{:S(2)}) async-start(bf16[8,192,896]{2,1,0:T(8,128)(2,1)} %shard_map.83), calls=%async_computation | async-start | bytes 5505024 | tf_op jit(solution)/shard_map/all_to_all | solution.py:37
  8.4 38.5 %all_gather.3.tok_ref = bf16[256,1024]{1,0:T(8,128)(2,1)S(1)} all-gather(bf16[16,1024]{1,0:T(8,128)(2,1)S(1)} %shard_map.82), channel_id=1, replica_groups={{0,64,160,224,256,320,416,480,512,576,672,736,768,832,928,992},{32,96,1..., dimensions={0}, use_global_device_ids=true | all-gather | bytes 557056 | tf_op jit(solution)/shard_map/all_gather | solution.py:403
  46.9 2.3 %collective-permute-start = (bf16[256,1024]{1,0:T(8,128)(2,1)S(1)}, bf16[256,1024]{1,0:T(8,128)(2,1)}, u32[]{:S(2)}, u32[]{:S(2)}) collective-permute-start(bf16[256,1024]{1,0:T(8,128)(2,1)S(1)} %all_gather.3.tok_ref), channel_id=1, source_target_pairs={{0,32},{32,0},{64,96},{96,64},{128,160},{160,128},{192,224},{224,1... | collective-permute-start | bytes 1572872 | tf_op jit(solution)/shard_map/ppermute | solution.py:404
  49.2 1.0 shard_map.84
  50.2 0.7 collective-permute-done.tok_ref
  50.9 2.4 %shard_map.85 = (bf16[512,896]{1,0:T(8,128)(2,1)}, bf16[256,128]{1,0:T(8,128)(2,1)}) custom-call(s32[1]{0:T(128)} %bitcast.1.expert_ref, bf16[256,1024]{1,0:T(8,128)(2,1)} %collective-permute-done.tok_ref, bf16[128,896]{1,0:T(8,128)(2,1)S(1)} %get-tuple-element.22.refs_0_), custom_call_target="tpu_custom_call" | custom-call | flops 58720256 | bytes 524288 | tf_op jit(solution)/shard_map/pallas_call | solution.py:252
  53.3 0.2 shard_map.86.done_ref
  53.5 0.0 all-to-all-done.w_ref
  53.5 26.4 %all_to_all.49 = bf16[32,16,896]{2,1,0:T(8,128)(2,1)S(1)} all-to-all(bf16[32,16,896]{2,1,0:T(8,128)(2,1)} %bitcast.31), channel_id=1, replica_groups=mesh['grp'=32,'node'=32] {'node'}, dimensions={0} | all-to-all | bytes 1835008 | tf_op jit(solution)/shard_map/all_to_all | solution.py:412
  79.9 1.5 shard_map.87
  81.5 6.2 %all-to-all-start.2 = ((bf16[8,64,512]{2,1,0:T(8,128)(2,1)}), bf16[8,64,512]{2,1,0:T(8,128)(2,1)S(1)}, u32[]{:S(2)}, u32[]{:S(2)}) async-start(bf16[8,64,512]{2,1,0:T(8,128)(2,1)} %bitcast.29), calls=%async_computation.2 | async-start | bytes 1048576 | tf_op jit(solution)/shard_map/all_to_all | solution.py:37
  87.7 5.6 %shard_map.88.coef_ref = f32[128,512]{1,0:T(8,128)} custom-call(s32[1]{0:T(128)S(6)} %sub.12.run_ref, bf16[512,7168]{1,0:T(8,128)(2,1)} %bitcast.22, bf16[64,7168]{1,0:T(8,128)(2,1)} %bitcast.25, bf16[64,7168]{1,0:T(8,128)(2,1)} %bitcast.28, f32[128,512]{1,0:T(8,128)S(1)} %shard_map.86.done_ref), custom_call_target="tpu_custom_call" | custom-call | flops 939524096 | bytes 9175040 | tf_op jit(solution)/shard_map/pallas_call | solution.py:209
  93.3 2.7 %all-to-all-done.2.parts_ref = bf16[8,64,512]{2,1,0:T(8,128)(2,1)S(1)} async-done(((bf16[8,64,512]{2,1,0:T(8,128)(2,1)}), bf16[8,64,512]{2,1,0:T(8,128)(2,1)S(1)}, u32[]{:S(2)}, u32[]{:S(2)}) %all-to-all-start.2) | async-done | bytes 524320 | tf_op jit(solution)/shard_map/all_to_all | solution.py:37
  96.0 1.2 shard_map.89
  97.2 14.7 %all_to_all.50.grads_ref = bf16[8,512,128]{2,1,0:T(8,128)(2,1)S(1)} all-to-all(bf16[8,512,128]{2,1,0:T(8,128)(2,1)S(1)} %shard_map.89), channel_id=1, replica_groups={{0,1,2,3,4,5,6,7},{8,9,10,11,12,13,14,15},{16,17,18,19,20,21,22,23},{24..., dimensions={0} | all-to-all | bytes 2097152 | tf_op jit(solution)/shard_map/all_to_all | solution.py:37
  111.9 0.0 copy-start.1
  111.9 0.0 copy-start.2
  111.9 1.7 shard_map.90
  113.6 0.0 copy-start
  113.6 0.9 copy-done
  114.5 4.6 %all-to-all-start.4 = ((bf16[32,16,896]{2,1,0:T(8,128)(2,1)}), bf16[32,16,896]{2,1,0:T(8,128)(2,1)S(1)}, u32[]{:S(2)}, u32[]{:S(2)}) async-start(bf16[32,16,896]{2,1,0:T(8,128)(2,1)} %bitcast.18), calls=%async_computation.4 | async-start | bytes 1835008 | tf_op jit(solution)/shard_map/all_to_all | solution.py:419
  119.2 22.5 %all-to-all-done.4 = bf16[32,16,896]{2,1,0:T(8,128)(2,1)S(1)} async-done(((bf16[32,16,896]{2,1,0:T(8,128)(2,1)}), bf16[32,16,896]{2,1,0:T(8,128)(2,1)S(1)}, u32[]{:S(2)}, u32[]{:S(2)}) %all-to-all-start.4) | async-done | bytes 917536 | tf_op jit(solution)/shard_map/all_to_all | solution.py:419
  141.7 0.0 copy-done.1
  141.7 0.0 copy-done.2
  141.7 0.5 shard_map.91
  142.3 6.6 %collective-permute-start.1 = (bf16[256,896]{1,0:T(8,128)(2,1)S(1)}, bf16[256,896]{1,0:T(8,128)(2,1)S(1)}, u32[]{:S(2)}, u32[]{:S(2)}) collective-permute-start(bf16[256,896]{1,0:T(8,128)(2,1)S(1)} %get-tuple-element.34), channel_id=1, source_target_pairs={{0,32},{32,0},{64,96},{96,64},{128,160},{160,128},{192,224},{224,1... | collective-permute-start | bytes 1376264 | tf_op jit(solution)/shard_map/ppermute | solution.py:423
  148.9 1.4 collective-permute-done.1
  150.3 0.1 add_convert_fusion
  150.4 34.9 %all_to_all.51.parts_ref = bf16[16,16,896]{2,1,0:T(8,128)(2,1)S(1)} all-to-all(bf16[16,16,896]{2,1,0:T(8,128)(2,1)S(1)} %bitcast.30), channel_id=1, replica_groups={{0,128,256,384,512,640,768,896,64,192,320,448,576,704,832,960},{32,160,..., dimensions={0} | all-to-all | bytes 917504 | tf_op jit(solution)/shard_map/all_to_all | solution.py:37
  185.2 0.7 shard_map.92
Async XLA Ops:
  0.0 3.0 %copy-start.3 = (bf16[2,7168]{1,0:T(2,128)(2,1)S(1)}, bf16[2,7168]{1,0:T(2,128)(2,1)}, u32[]{:S(2)}) copy-start(bf16[2,7168]{1,0:T(2,128)(2,1)} %grad_ref.1) | copy-start | bytes 86020
  0.0 3.0 %copy-start.4 = (s32[2,8]{1,0:T(2,128)S(1)}, s32[2,8]{1,0:T(2,128)}, u32[]{:S(2)}) copy-start(s32[2,8]{1,0:T(2,128)} %ids_ref.1) | copy-start | bytes 196
  0.0 3.0 %copy-start.5 = (s32[2,8]{1,0:T(2,128)S(1)}, s32[2,8]{1,0:T(2,128)}, u32[]{:S(2)}) copy-start(s32[2,8]{1,0:T(2,128)} %slots_ref.1) | copy-start | bytes 196
  0.0 3.0 %copy-start.6 = (s32[2,8]{1,0:T(2,128)S(1)}, s32[2,8]{1,0:T(2,128)}, u32[]{:S(2)}) copy-start(s32[2,8]{1,0:T(2,128)} %gates_ref.1) | copy-start | bytes 196
  3.1 50.4 %all-to-all-start = ((bf16[8,192,896]{2,1,0:T(8,128)(2,1)}), bf16[8,192,896]{2,1,0:T(8,128)(2,1)S(1)}, u32[]{:S(2)}, u32[]{:S(2)}) async-start(bf16[8,192,896]{2,1,0:T(8,128)(2,1)} %shard_map.83), calls=%async_computation | async-start | bytes 5505024 | tf_op jit(solution)/shard_map/all_to_all | solution.py:37
  46.9 4.0 %collective-permute-start = (bf16[256,1024]{1,0:T(8,128)(2,1)S(1)}, bf16[256,1024]{1,0:T(8,128)(2,1)}, u32[]{:S(2)}, u32[]{:S(2)}) collective-permute-start(bf16[256,1024]{1,0:T(8,128)(2,1)S(1)} %all_gather.3.tok_ref), channel_id=1, source_target_pairs={{0,32},{32,0},{64,96},{96,64},{128,160},{160,128},{192,224},{224,1... | collective-permute-start | bytes 1572872 | tf_op jit(solution)/shard_map/ppermute | solution.py:404
  81.5 14.5 %all-to-all-start.2 = ((bf16[8,64,512]{2,1,0:T(8,128)(2,1)}), bf16[8,64,512]{2,1,0:T(8,128)(2,1)S(1)}, u32[]{:S(2)}, u32[]{:S(2)}) async-start(bf16[8,64,512]{2,1,0:T(8,128)(2,1)} %bitcast.29), calls=%async_computation.2 | async-start | bytes 1048576 | tf_op jit(solution)/shard_map/all_to_all | solution.py:37
  111.9 29.9 %copy-start.1 = (bf16[256,128]{1,0:T(8,128)(2,1)S(1)}, bf16[256,128]{1,0:T(8,128)(2,1)}, u32[]{:S(2)}) copy-start(bf16[256,128]{1,0:T(8,128)(2,1)} %get-tuple-element.21.hot_here_ref) | copy-start | bytes 196612
  111.9 29.9 %copy-start.2 = (bf16[256,128]{1,0:T(8,128)(2,1)S(1)}, bf16[256,128]{1,0:T(8,128)(2,1)}, u32[]{:S(2)}) copy-start(bf16[256,128]{1,0:T(8,128)(2,1)} %get-tuple-element.23.hot_there_ref) | copy-start | bytes 196612
  113.6 0.9 copy-start
  114.5 27.2 %all-to-all-start.4 = ((bf16[32,16,896]{2,1,0:T(8,128)(2,1)}), bf16[32,16,896]{2,1,0:T(8,128)(2,1)S(1)}, u32[]{:S(2)}, u32[]{:S(2)}) async-start(bf16[32,16,896]{2,1,0:T(8,128)(2,1)} %bitcast.18), calls=%async_computation.4 | async-start | bytes 1835008 | tf_op jit(solution)/shard_map/all_to_all | solution.py:419
  142.3 8.0 %collective-permute-start.1 = (bf16[256,896]{1,0:T(8,128)(2,1)S(1)}, bf16[256,896]{1,0:T(8,128)(2,1)S(1)}, u32[]{:S(2)}, u32[]{:S(2)}) collective-permute-start(bf16[256,896]{1,0:T(8,128)(2,1)S(1)} %get-tuple-element.34), channel_id=1, source_target_pairs={{0,32},{32,0},{64,96},{96,64},{128,160},{160,128},{192,224},{224,1... | collective-permute-start | bytes 1376264 | tf_op jit(solution)/shard_map/ppermute | solution.py:423

commit v11 on v8

--- a/solution.py
+++ b/solution.py
@@ -156,7 +156,7 @@
                 for j in range(2)
             )
             for j, value in enumerate(coefficients(pre_gate, pre_up)):
-                out_ref[j * n : (j + 1) * n, start : start + BLOCK] = value
+                out_ref[j * n : (j + 1) * n, start : start + BLOCK] = value.astype(bf16)
 
     @pl.when(run_ref[0] == 0)
     def _():
@@ -168,7 +168,7 @@
     n_hid = gate.shape[0]
     return call(
         early_body,
-        jax.ShapeDtypeStruct((2 * n_hid, n_slot), f32),
+        jax.ShapeDtypeStruct((2 * n_hid, n_slot), bf16),
         (4 * n_hid * n_slot * width, 2 * (n_slot + 2 * n_hid) * width),
         in_specs=[pl.BlockSpec(memory_space=pltpu.SMEM)]
         + [pl.BlockSpec(memory_space=pl.ANY)] * 3,
@@ -192,7 +192,7 @@
             x_ref[...], both, (((1,), (1,)), ((), ())), preferred_element_type=f32
         ).T
         for j, value in enumerate(coefficients(pre[:n], pre[n:])):
-            out_ref[j * n : (j + 1) * n] = value
+            out_ref[j * n : (j + 1) * n] = value.astype(bf16)
 
     @pl.when(run_ref[0] == 0)
     def _():
@@ -207,7 +207,7 @@
     out = pl.BlockSpec((2 * n_hid, half), lambda i: (0, i))
     return call(
         late_body,
-        pltpu.HBM((2 * n_hid, n_slot), f32),
+        pltpu.HBM((2 * n_hid, n_slot), bf16),
         (4 * n_hid * n_slot * width, 2 * (n_slot + 2 * n_hid) * width),
         grid=(2,),
         in_specs=[
@@ -292,7 +292,8 @@
 def grads_body(parts_ref, coef_ref, out_ref):
     n, h, _ = parts_ref.shape
     total = jnp.sum(parts_ref[...].astype(f32), axis=0)
-    grads = jnp.concatenate([total * coef_ref[:h], total * coef_ref[h:]], axis=0)
+    coef = coef_ref[...].astype(f32)
+    grads = jnp.concatenate([total * coef[:h], total * coef[h:]], axis=0)
     grads = grads.T.astype(bf16)
     for i in range(n):
         out_ref[i] = grads

time: 185 us -> 185 us (level)
  no operation moved by 1% of the time
where the time goes in v11:
time: 185 us
  blocking collectives  133 us (72%)
  starting transfers between devices  30.7 us (17%)
  Pallas kernels  17.7 us (10%)
  waiting for transfers between devices  3.12 us (2%)
    all_to_all x2, blocking collectives, swap(): return lax.all_to_all(a, axis, 0, 0, axis_index_groups=members, tiled=True)  46.1 us
    all_gather x1, blocking collectives, local(): lax.all_gather(payload, 'grp', axis=0, axis_index_groups=along_z, tiled=T...  30.2 us
    all_to_all x1, blocking collectives, local(): parts = lax.all_to_all(slot_part(grads, weights), 'node', 0, 0, tiled=True)  29.5 us
    all_to_all x1, blocking collectives, local(): rows = lax.all_to_all(rows, 'node', 0, 0, tiled=True)  27.3 us
    all_to_all x2, starting transfers between devices, swap(): return lax.all_to_all(a, axis, 0, 0, axis_index_groups=members, tiled=True)  22.8 us
    pallas_call x1, Pallas kernels, late_forward(): call(late_body, pltpu.HBM((2 * n_hid, n_slot), bf16), (4 * n_hid * n_slot...  5.58 us
    ppermute x1, starting transfers between devices, local(): back = total([here, lax.ppermute(there, 'grp', other)])  5 us
  transfers between devices with their start and end apart: 4, of which 3 were waited for; matrix products, arithmetic and copies ran while one was open for 0% of the time, Pallas kernels for 5%

profile of v11, /device:TPU:2, one launch (start us, length us, event | category | flops | bytes accessed | tf_op | source)
XLA Modules:
  0.0 184.8 jit_solution(9777375892045947353)
XLA Ops:
  0.0 0.0 copy-start.2
  0.0 0.0 copy-start.3
  0.0 0.0 copy-start.4
  0.0 0.0 copy-start.5
  0.0 2.9 %shard_map.83 = bf16[8,192,896]{2,1,0:T(8,128)(2,1)} custom-call(bf16[64,7168]{1,0:T(8,128)(2,1)} %bitcast.22, bf16[64,7168]{1,0:T(8,128)(2,1)} %bitcast.25, bf16[64,7168]{1,0:T(8,128)(2,1)} %bitcast.31), custom_call_target="tpu_custom_call" | custom-call | bytes 5505024 | tf_op jit(solution)/shard_map/pallas_call | solution.py:104
  3.0 0.0 copy-done.2
  3.0 0.0 copy-done.3
  3.0 0.0 copy-done.4
  3.0 0.0 copy-done.5
  3.0 0.1 shard_map.82
  3.1 16.7 %all-to-all-start = ((bf16[8,192,896]{2,1,0:T(8,128)(2,1)}), bf16[8,192,896]{2,1,0:T(8,128)(2,1)S(1)}, u32[]{:S(2)}, u32[]{:S(2)}) async-start(bf16[8,192,896]{2,1,0:T(8,128)(2,1)} %shard_map.83), calls=%async_computation | async-start | bytes 5505024 | tf_op jit(solution)/shard_map/all_to_all | solution.py:36
  19.8 30.2 %all_gather.3.tok_ref = bf16[256,1024]{1,0:T(8,128)(2,1)S(1)} all-gather(bf16[16,1024]{1,0:T(8,128)(2,1)S(1)} %shard_map.82), channel_id=1, replica_groups={{0,64,160,224,256,320,416,480,512,576,672,736,768,832,928,992},{32,96,1..., dimensions={0}, use_global_device_ids=true | all-gather | bytes 557056 | tf_op jit(solution)/shard_map/all_gather | solution.py:391
  50.1 2.9 %collective-permute-start = (bf16[256,1024]{1,0:T(8,128)(2,1)S(1)}, bf16[256,1024]{1,0:T(8,128)(2,1)}, u32[]{:S(2)}, u32[]{:S(2)}) collective-permute-start(bf16[256,1024]{1,0:T(8,128)(2,1)S(1)} %all_gather.3.tok_ref), channel_id=1, source_target_pairs={{0,32},{32,0},{64,96},{96,64},{128,160},{160,128},{192,224},{224,1... | collective-permute-start | bytes 1572872 | tf_op jit(solution)/shard_map/ppermute | solution.py:392
  53.0 1.0 shard_map.84
  53.9 0.7 collective-permute-done.tok_ref
  54.6 2.4 %shard_map.85 = (bf16[512,896]{1,0:T(8,128)(2,1)}, bf16[256,128]{1,0:T(8,128)(2,1)}) custom-call(s32[1]{0:T(128)} %bitcast.expert_ref, bf16[256,1024]{1,0:T(8,128)(2,1)} %collective-permute-done.tok_ref, bf16[128,896]{1,0:T(8,128)(2,1)S(1)} %get-tuple-element.22.refs_0_), custom_call_target="tpu_custom_call" | custom-call | flops 58720256 | bytes 524288 | tf_op jit(solution)/shard_map/pallas_call | solution.py:251
  57.0 0.2 shard_map.86.done_ref
  57.2 0.0 all-to-all-done.w_ref
  57.2 27.3 %all_to_all.49 = bf16[32,16,896]{2,1,0:T(8,128)(2,1)S(1)} all-to-all(bf16[32,16,896]{2,1,0:T(8,128)(2,1)} %bitcast.30), channel_id=1, replica_groups=mesh['grp'=32,'node'=32] {'node'}, dimensions={0} | all-to-all | bytes 1835008 | tf_op jit(solution)/shard_map/all_to_all | solution.py:400
  84.5 1.5 shard_map.87
  86.1 6.1 %all-to-all-start.2 = ((bf16[8,64,512]{2,1,0:T(8,128)(2,1)}), bf16[8,64,512]{2,1,0:T(8,128)(2,1)S(1)}, u32[]{:S(2)}, u32[]{:S(2)}) async-start(bf16[8,64,512]{2,1,0:T(8,128)(2,1)} %bitcast.28), calls=%async_computation.2 | async-start | bytes 1048576 | tf_op jit(solution)/shard_map/all_to_all | solution.py:36
  92.1 5.6 %shard_map.88.coef_ref = bf16[128,512]{1,0:T(8,128)(2,1)} custom-call(s32[1]{0:T(128)S(6)} %sub.3.run_ref, bf16[512,7168]{1,0:T(8,128)(2,1)} %bitcast.21, bf16[64,7168]{1,0:T(8,128)(2,1)} %bitcast.24, bf16[64,7168]{1,0:T(8,128)(2,1)} %bitcast.27, bf16[128,512]{1,0:T(8,128)(2,1)S(1)} %shard_map.86.done_ref), custom_call_target="tpu_custom_call" | custom-call | flops 939524096 | bytes 9175040 | tf_op jit(solution)/shard_map/pallas_call | solution.py:208
  97.7 1.0 all-to-all-done.2.parts_ref
  98.8 1.1 shard_map.89
  99.9 14.5 %all_to_all.50.grads_ref = bf16[8,512,128]{2,1,0:T(8,128)(2,1)S(1)} all-to-all(bf16[8,512,128]{2,1,0:T(8,128)(2,1)S(1)} %shard_map.89), channel_id=1, replica_groups={{0,1,2,3,4,5,6,7},{8,9,10,11,12,13,14,15},{16,17,18,19,20,21,22,23},{24..., dimensions={0} | all-to-all | bytes 2097152 | tf_op jit(solution)/shard_map/all_to_all | solution.py:36
  114.4 0.0 copy-start
  114.4 0.0 copy-start.1
  114.4 1.7 shard_map.90
  116.1 29.5 %all_to_all.51 = bf16[32,16,896]{2,1,0:T(8,128)(2,1)S(1)} all-to-all(bf16[32,16,896]{2,1,0:T(8,128)(2,1)S(1)} %bitcast.17), channel_id=1, replica_groups=mesh['grp'=32,'node'=32] {'node'}, dimensions={0} | all-to-all | bytes 1835008 | tf_op jit(solution)/shard_map/all_to_all | solution.py:407
  145.5 0.0 copy-done
  145.5 0.0 copy-done.1
  145.6 0.4 shard_map.91
  146.0 5.0 %collective-permute-start.1 = (bf16[256,896]{1,0:T(8,128)(2,1)S(1)}, bf16[256,896]{1,0:T(8,128)(2,1)S(1)}, u32[]{:S(2)}, u32[]{:S(2)}) collective-permute-start(bf16[256,896]{1,0:T(8,128)(2,1)S(1)} %get-tuple-element.34), channel_id=1, source_target_pairs={{0,32},{32,0},{64,96},{96,64},{128,160},{160,128},{192,224},{224,1... | collective-permute-start | bytes 1376264 | tf_op jit(solution)/shard_map/ppermute | solution.py:410
  151.0 1.4 collective-permute-done.1
  152.4 0.1 add_convert_fusion
  152.5 31.6 %all_to_all.52.parts_ref = bf16[16,16,896]{2,1,0:T(8,128)(2,1)S(1)} all-to-all(bf16[16,16,896]{2,1,0:T(8,128)(2,1)S(1)} %bitcast.29), channel_id=1, replica_groups={{0,64,160,224,256,320,416,480,512,576,672,736,768,832,928,992},{32,96,1..., dimensions={0} | all-to-all | bytes 917504 | tf_op jit(solution)/shard_map/all_to_all | solution.py:36
  184.1 0.7 shard_map.92
Async XLA Ops:
  0.0 3.0 %copy-start.2 = (bf16[2,7168]{1,0:T(2,128)(2,1)S(1)}, bf16[2,7168]{1,0:T(2,128)(2,1)}, u32[]{:S(2)}) copy-start(bf16[2,7168]{1,0:T(2,128)(2,1)} %grad_ref.1) | copy-start | bytes 86020
  0.0 3.0 %copy-start.3 = (s32[2,8]{1,0:T(2,128)S(1)}, s32[2,8]{1,0:T(2,128)}, u32[]{:S(2)}) copy-start(s32[2,8]{1,0:T(2,128)} %ids_ref.1) | copy-start | bytes 196
  0.0 3.0 %copy-start.4 = (s32[2,8]{1,0:T(2,128)S(1)}, s32[2,8]{1,0:T(2,128)}, u32[]{:S(2)}) copy-start(s32[2,8]{1,0:T(2,128)} %slots_ref.1) | copy-start | bytes 196
  0.0 3.0 %copy-start.5 = (s32[2,8]{1,0:T(2,128)S(1)}, s32[2,8]{1,0:T(2,128)}, u32[]{:S(2)}) copy-start(s32[2,8]{1,0:T(2,128)} %gates_ref.1) | copy-start | bytes 196
  3.1 54.1 %all-to-all-start = ((bf16[8,192,896]{2,1,0:T(8,128)(2,1)}), bf16[8,192,896]{2,1,0:T(8,128)(2,1)S(1)}, u32[]{:S(2)}, u32[]{:S(2)}) async-start(bf16[8,192,896]{2,1,0:T(8,128)(2,1)} %shard_map.83), calls=%async_computation | async-start | bytes 5505024 | tf_op jit(solution)/shard_map/all_to_all | solution.py:36
  50.1 4.5 %collective-permute-start = (bf16[256,1024]{1,0:T(8,128)(2,1)S(1)}, bf16[256,1024]{1,0:T(8,128)(2,1)}, u32[]{:S(2)}, u32[]{:S(2)}) collective-permute-start(bf16[256,1024]{1,0:T(8,128)(2,1)S(1)} %all_gather.3.tok_ref), channel_id=1, source_target_pairs={{0,32},{32,0},{64,96},{96,64},{128,160},{160,128},{192,224},{224,1... | collective-permute-start | bytes 1572872 | tf_op jit(solution)/shard_map/ppermute | solution.py:392
  86.1 12.7 %all-to-all-start.2 = ((bf16[8,64,512]{2,1,0:T(8,128)(2,1)}), bf16[8,64,512]{2,1,0:T(8,128)(2,1)S(1)}, u32[]{:S(2)}, u32[]{:S(2)}) async-start(bf16[8,64,512]{2,1,0:T(8,128)(2,1)} %bitcast.28), calls=%async_computation.2 | async-start | bytes 1048576 | tf_op jit(solution)/shard_map/all_to_all | solution.py:36
  114.4 31.1 %copy-start = (bf16[256,128]{1,0:T(8,128)(2,1)S(1)}, bf16[256,128]{1,0:T(8,128)(2,1)}, u32[]{:S(2)}) copy-start(bf16[256,128]{1,0:T(8,128)(2,1)} %get-tuple-element.21.hot_here_ref) | copy-start | bytes 196612
  114.4 31.1 %copy-start.1 = (bf16[256,128]{1,0:T(8,128)(2,1)S(1)}, bf16[256,128]{1,0:T(8,128)(2,1)}, u32[]{:S(2)}) copy-start(bf16[256,128]{1,0:T(8,128)(2,1)} %get-tuple-element.23.hot_there_ref) | copy-start | bytes 196612
  146.0 6.4 %collective-permute-start.1 = (bf16[256,896]{1,0:T(8,128)(2,1)S(1)}, bf16[256,896]{1,0:T(8,128)(2,1)S(1)}, u32[]{:S(2)}, u32[]{:S(2)}) collective-permute-start(bf16[256,896]{1,0:T(8,128)(2,1)S(1)} %get-tuple-element.34), channel_id=1, source_target_pairs={{0,32},{32,0},{64,96},{96,64},{128,160},{160,128},{192,224},{224,1... | collective-permute-start | bytes 1376264 | tf_op jit(solution)/shard_map/ppermute | solution.py:410
